TPU v7x, 32 devices: a whole 2x2x4 slice. The times are simulated.
32 devices in a mesh: shard: 2 (over y), ctx: 4 (over z), tensor: 4 (over x, core).
Axes of the slice: x: 2, y: 2, z: 4, core: 2. Of those that a mesh axis runs over, the one named last changes fastest.
Arguments:
- tokens: bfloat16 [4, 4096, 960], P('shard', 'ctx'), may hold values from -6 to 6
- gains: bfloat16 [2, 960], P(None, ('shard', 'ctx')), may hold values from 0.5 to 1.5
- qkv_weight: bfloat16 [960, 1600], P('tensor', ('shard', 'ctx')), may hold values from -0.1875 to 0.1875
- out_weight: bfloat16 [960, 960], P('tensor', ('shard', 'ctx')), may hold values from -6 to 6
- gate_weight: bfloat16 [960, 2560], P(('shard', 'ctx'), 'tensor'), may hold values from -0.1875 to 0.1875
- up_weight: bfloat16 [960, 2560], P(('shard', 'ctx'), 'tensor'), may hold values from -0.1875 to 0.1875
- down_weight: bfloat16 [2560, 960], P('tensor', ('shard', 'ctx')), may hold values from -0.125 to 0.125
- cotangent: float32 [4, 4096, 960], P('shard', 'ctx'), may hold values from -6 to 6
Outputs:
- block_out: bfloat16 [4, 4096, 960], P('shard', 'ctx')
- input_grad: float32 [4, 4096, 960], P('shard', 'ctx')
- gains_grad: float32 [2, 960], P(None, ('shard', 'ctx'))
- qkv_weight_grad: float32 [960, 1600], P('tensor', ('shard', 'ctx'))
- out_weight_grad: float32 [960, 960], P('tensor', ('shard', 'ctx'))
- gate_weight_grad: float32 [960, 2560], P(('shard', 'ctx'), 'tensor')
- up_weight_grad: float32 [960, 2560], P(('shard', 'ctx'), 'tensor')
- down_weight_grad: float32 [2560, 960], P('tensor', ('shard', 'ctx'))
All inputs are finite; a program needn't handle non-finite values.
Results may differ from a plain program's by a relative error of at most 0.03.
Values may be sent and summed in bfloat16 or wider, within the bound.
No kernel may reach another device: no remote copies, remote signals or barrier semaphores. Data moves between devices by JAX's collectives and lax.ppermute only.
A program may use at most 192 MiB of HBM per device.

v0:
```python
import jax
import jax.numpy as jnp
from jax import lax
from jax.sharding import PartitionSpec as P

HEADS = 15
KV_HEADS = 5
HEAD_DIM = 64
GROUP = 3


epsilon = 1e-05
rope_base = 100000.0
masked_score = -1e30


def rope_tables(positions):
    half_dim = HEAD_DIM // 2
    frequency = rope_base ** (-2.0 * jnp.arange(half_dim, dtype=jnp.float32) / HEAD_DIM)
    angles = positions.astype(jnp.float32)[:, None] * frequency[None, :]
    return (jnp.cos(angles)[:, None, :], jnp.sin(angles)[:, None, :])


def rotate(values, cosine_table, sine_table):
    half_dim = HEAD_DIM // 2
    first_half = values[..., :half_dim]
    second_half = values[..., half_dim:]
    return jnp.concatenate(
        [
            first_half * cosine_table - second_half * sine_table,
            second_half * cosine_table + first_half * sine_table,
        ],
        axis=-1,
    )


def norm_parts(values, gain_row):
    inv_rms = lax.rsqrt(jnp.mean(values * values, axis=-1, keepdims=True) + epsilon)
    unit_rows = values * inv_rms
    return (unit_rows, inv_rms, unit_rows * gain_row)


def norm_back(upstream, unit_rows, inv_rms, gain_row):
    shaped = upstream * gain_row
    inner_mean = jnp.mean(shaped * unit_rows, axis=-1, keepdims=True)
    return (inv_rms * (shaped - unit_rows * inner_mean), jnp.sum(upstream * unit_rows, axis=(0, 1)))


def shards(tokens, gains, qkv_weight, out_weight, gate_weight, up_weight, down_weight, cotangent):
    gain_all, qkv_all, out_all, gate_all, up_all, down_all = (
        lax.all_gather(gains, ("shard", "ctx"), axis=1, tiled=True),
        lax.all_gather(qkv_weight, ("shard", "ctx"), axis=1, tiled=True),
        lax.all_gather(out_weight, ("shard", "ctx"), axis=1, tiled=True),
        lax.all_gather(gate_weight, ("shard", "ctx"), axis=0, tiled=True),
        lax.all_gather(up_weight, ("shard", "ctx"), axis=0, tiled=True),
        lax.all_gather(down_weight, ("shard", "ctx"), axis=1, tiled=True),
    )
    seq_count, span_len, width = tokens.shape
    tensor_count = lax.axis_size("tensor")
    row_count = span_len // tensor_count
    quarter = width // tensor_count
    own_part = lax.axis_index("tensor")
    first_row = lax.axis_index(("ctx", "tensor")) * row_count
    seq_len = row_count * lax.axis_size(("ctx", "tensor"))
    kv_width = KV_HEADS * HEAD_DIM
    block_len = min(512, seq_len)
    scale_factor = HEAD_DIM ** (-0.5)
    gain_one = gain_all[0].astype(jnp.float32)
    gain_two = gain_all[1].astype(jnp.float32)
    inputs = tokens.astype(jnp.float32)
    unit_one, rms_one, normed_full = norm_parts(inputs, gain_one)
    normed = normed_full.astype(jnp.bfloat16)
    normed_part = lax.dynamic_slice_in_dim(normed, own_part * quarter, quarter, 2)
    projected = lax.psum_scatter(
        jnp.einsum("scd,de->sce", normed_part, qkv_all, preferred_element_type=jnp.float32).astype(
            jnp.bfloat16
        ),
        "tensor",
        scatter_dimension=1,
        tiled=True,
    ).astype(jnp.float32)
    query_pos = first_row + jnp.arange(row_count, dtype=jnp.int32)
    cosine_table, sine_table = rope_tables(query_pos)
    queries = rotate(
        projected[..., :width].reshape(seq_count, row_count, HEADS, HEAD_DIM),
        cosine_table,
        sine_table,
    )
    keys_own = rotate(
        projected[..., width : width + kv_width].reshape(seq_count, row_count, KV_HEADS, HEAD_DIM),
        cosine_table,
        sine_table,
    )
    query_low = queries.astype(jnp.bfloat16).reshape(
        seq_count, row_count, KV_HEADS, GROUP, HEAD_DIM
    )
    pair_own = jnp.concatenate(
        [keys_own.reshape(seq_count, row_count, kv_width), projected[..., width + kv_width :]],
        axis=-1,
    ).astype(jnp.bfloat16)
    pair_all = lax.all_gather(pair_own, ("ctx", "tensor"), axis=1, tiled=True)
    block_count = (first_row + row_count - 1) // block_len + 1

    def block_scores(pairs, block_index):
        pair_slice = lax.dynamic_slice_in_dim(pairs, block_index * block_len, block_len, 1)
        key_block = pair_slice[..., :kv_width].reshape(seq_count, block_len, KV_HEADS, HEAD_DIM)
        value_block = pair_slice[..., kv_width:].reshape(seq_count, block_len, KV_HEADS, HEAD_DIM)
        scores = (
            jnp.einsum(
                "sqhgd,skhd->shgqk", query_low, key_block, preferred_element_type=jnp.float32
            )
            * scale_factor
        )
        key_pos = block_index * block_len + jnp.arange(block_len, dtype=jnp.int32)
        scores = jnp.where(key_pos[None, :] <= query_pos[:, None], scores, masked_score)
        return (key_block, value_block, scores)

    def max_step(block_index, carry):
        row_max, row_sum = carry
        key_block, value_block, scores = block_scores(pair_all, block_index)
        new_max = jnp.maximum(row_max, jnp.max(scores, axis=-1))
        row_sum = row_sum * jnp.exp(row_max - new_max) + jnp.sum(
            jnp.exp(scores - new_max[..., None]), axis=-1
        )
        return (new_max, row_sum)

    stat_shape = (seq_count, KV_HEADS, GROUP, row_count)
    row_max, row_sum = lax.fori_loop(
        0,
        block_count,
        max_step,
        (jnp.full(stat_shape, masked_score, jnp.float32), jnp.zeros(stat_shape, jnp.float32)),
    )
    log_total = row_max + jnp.log(row_sum)

    def out_step(block_index, running):
        key_block, value_block, scores = block_scores(pair_all, block_index)
        weights_low = jnp.exp(scores - log_total[..., None]).astype(jnp.bfloat16)
        return running + jnp.einsum(
            "shgqk,skhd->sqhgd", weights_low, value_block, preferred_element_type=jnp.float32
        )

    head_shape = (seq_count, row_count, KV_HEADS, GROUP, HEAD_DIM)
    attn_sum = lax.fori_loop(0, block_count, out_step, jnp.zeros(head_shape, jnp.float32))
    attn_low = attn_sum.astype(jnp.bfloat16).reshape(seq_count, row_count, width)
    mixed_part = lax.all_to_all(attn_low, "tensor", split_axis=2, concat_axis=1, tiled=True)
    attn_term = jnp.einsum("scf,fe->sce", mixed_part, out_all, preferred_element_type=jnp.float32)
    attn_out = lax.psum(attn_term.astype(jnp.bfloat16), "tensor").astype(jnp.float32)
    hidden = inputs + attn_out
    unit_two, rms_two, normed_two_full = norm_parts(hidden, gain_two)
    normed_two = normed_two_full.astype(jnp.bfloat16)
    gate_value = jnp.einsum("scd,df->scf", normed_two, gate_all, preferred_element_type=jnp.float32)
    up_value = jnp.einsum("scd,df->scf", normed_two, up_all, preferred_element_type=jnp.float32)
    gate_sigmoid = jax.nn.sigmoid(gate_value)
    inner_act = (gate_value * gate_sigmoid * up_value).astype(jnp.bfloat16)
    feed_out = lax.psum(
        jnp.einsum("scf,fe->sce", inner_act, down_all, preferred_element_type=jnp.float32).astype(
            jnp.bfloat16
        ),
        "tensor",
    ).astype(jnp.float32)
    block_out = (hidden + feed_out).astype(jnp.bfloat16)
    cot_low = cotangent.astype(jnp.bfloat16)
    down_grad = jnp.einsum("scf,sce->fe", inner_act, cot_low, preferred_element_type=jnp.float32)
    inner_grad = jnp.einsum("sce,fe->scf", cot_low, down_all, preferred_element_type=jnp.float32)
    gate_grad = (
        inner_grad * up_value * gate_sigmoid * (1.0 + gate_value * (1.0 - gate_sigmoid))
    ).astype(jnp.bfloat16)
    up_grad = (inner_grad * gate_value * gate_sigmoid).astype(jnp.bfloat16)
    gate_weight_grad = jnp.einsum(
        "scd,scf->df", normed_two, gate_grad, preferred_element_type=jnp.float32
    )
    up_weight_grad = jnp.einsum(
        "scd,scf->df", normed_two, up_grad, preferred_element_type=jnp.float32
    )
    normed_two_grad = lax.psum(
        (
            jnp.einsum("scf,df->scd", gate_grad, gate_all, preferred_element_type=jnp.float32)
            + jnp.einsum("scf,df->scd", up_grad, up_all, preferred_element_type=jnp.float32)
        ).astype(jnp.bfloat16),
        "tensor",
    ).astype(jnp.float32)
    hidden_part_grad, gain_two_grad = norm_back(normed_two_grad, unit_two, rms_two, gain_two)
    hidden_grad = cotangent + hidden_part_grad
    hidden_low = hidden_grad.astype(jnp.bfloat16)
    out_weight_grad = jnp.einsum(
        "scf,sce->fe", mixed_part, hidden_low, preferred_element_type=jnp.float32
    )
    mixed_grad = lax.all_to_all(
        jnp.einsum("sce,fe->scf", hidden_low, out_all, preferred_element_type=jnp.float32).astype(
            jnp.bfloat16
        ),
        "tensor",
        split_axis=1,
        concat_axis=2,
        tiled=True,
    )
    attn_grad = mixed_grad.reshape(head_shape)
    row_delta = jnp.transpose(
        jnp.sum(attn_grad.astype(jnp.float32) * attn_sum, axis=-1), (0, 2, 3, 1)
    )

    def back_step(block_index, carry):
        query_grad, pair_grad = carry
        key_block, value_block, scores = block_scores(pair_all, block_index)
        weights_full = jnp.exp(scores - log_total[..., None])
        weights_low = weights_full.astype(jnp.bfloat16)
        prob_grad = jnp.einsum(
            "sqhgd,skhd->shgqk", attn_grad, value_block, preferred_element_type=jnp.float32
        )
        score_grad = (weights_full * (prob_grad - row_delta[..., None])).astype(jnp.bfloat16)
        query_grad = query_grad + jnp.einsum(
            "shgqk,skhd->sqhgd", score_grad, key_block, preferred_element_type=jnp.float32
        )
        key_grad = (
            jnp.einsum(
                "shgqk,sqhgd->skhd", score_grad, query_low, preferred_element_type=jnp.float32
            )
            * scale_factor
        )
        value_grad = jnp.einsum(
            "shgqk,sqhgd->skhd", weights_low, attn_grad, preferred_element_type=jnp.float32
        )
        block_grad = jnp.concatenate(
            [
                key_grad.reshape(seq_count, block_len, kv_width),
                value_grad.reshape(seq_count, block_len, kv_width),
            ],
            axis=-1,
        )
        pair_grad = lax.dynamic_update_slice_in_dim(
            pair_grad, block_grad, block_index * block_len, 1
        )
        return (query_grad, pair_grad)

    query_grad, pair_grad = lax.fori_loop(
        0,
        block_count,
        back_step,
        (
            jnp.zeros(head_shape, jnp.float32),
            jnp.zeros((seq_count, seq_len, 2 * kv_width), jnp.float32),
        ),
    )
    query_grad = query_grad * scale_factor
    pair_own_grad = lax.psum_scatter(
        pair_grad.astype(jnp.bfloat16), ("ctx", "tensor"), scatter_dimension=1, tiled=True
    ).astype(jnp.float32)
    query_back = rotate(
        query_grad.reshape(seq_count, row_count, HEADS, HEAD_DIM), cosine_table, -sine_table
    )
    key_back = rotate(
        pair_own_grad[..., :kv_width].reshape(seq_count, row_count, KV_HEADS, HEAD_DIM),
        cosine_table,
        -sine_table,
    )
    proj_grad = jnp.concatenate(
        [
            query_back.reshape(seq_count, row_count, width),
            key_back.reshape(seq_count, row_count, kv_width),
            pair_own_grad[..., kv_width:],
        ],
        axis=-1,
    ).astype(jnp.bfloat16)
    proj_grad_all = lax.all_gather(proj_grad, "tensor", axis=1, tiled=True)
    qkv_weight_grad = jnp.einsum(
        "scd,sce->de", normed_part, proj_grad_all, preferred_element_type=jnp.float32
    )
    normed_part_grad = jnp.einsum(
        "sce,de->scd", proj_grad_all, qkv_all, preferred_element_type=jnp.float32
    )
    normed_grad = lax.all_gather(
        normed_part_grad.astype(jnp.bfloat16), "tensor", axis=2, tiled=True
    ).astype(normed_part_grad.dtype)
    input_part_grad, gain_one_grad = norm_back(normed_grad, unit_one, rms_one, gain_one)
    input_grad = hidden_grad + input_part_grad
    gains_grad = jnp.stack([gain_one_grad, gain_two_grad])
    gains_out, qkv_out, out_out, gate_out, up_out, down_out = (
        lax.psum_scatter(gains_grad, ("shard", "ctx"), scatter_dimension=1, tiled=True),
        lax.psum_scatter(qkv_weight_grad, ("shard", "ctx"), scatter_dimension=1, tiled=True),
        lax.psum_scatter(out_weight_grad, ("shard", "ctx"), scatter_dimension=1, tiled=True),
        lax.psum_scatter(gate_weight_grad, ("shard", "ctx"), scatter_dimension=0, tiled=True),
        lax.psum_scatter(up_weight_grad, ("shard", "ctx"), scatter_dimension=0, tiled=True),
        lax.psum_scatter(down_grad, ("shard", "ctx"), scatter_dimension=1, tiled=True),
    )
    return (block_out, input_grad, gains_out, qkv_out, out_out, gate_out, up_out, down_out)


def solution(mesh):
    in_specs = (
        P("shard", "ctx", None),
        P(None, ("shard", "ctx")),
        P("tensor", ("shard", "ctx")),
        P("tensor", ("shard", "ctx")),
        P(("shard", "ctx"), "tensor"),
        P(("shard", "ctx"), "tensor"),
        P("tensor", ("shard", "ctx")),
        P("shard", "ctx", None),
    )
    out_specs = (
        P("shard", "ctx", None),
        P("shard", "ctx", None),
        P(None, ("shard", "ctx")),
        P("tensor", ("shard", "ctx")),
        P("tensor", ("shard", "ctx")),
        P(("shard", "ctx"), "tensor"),
        P(("shard", "ctx"), "tensor"),
        P("tensor", ("shard", "ctx")),
    )
    return jax.shard_map(shards, mesh=mesh, in_specs=in_specs, out_specs=out_specs, check_vma=False)
```

profile of v0, /device:TPU:0, one launch (start us, length us, event | category | flops | bytes accessed | tf_op | source)
XLA Modules:
  0.0 1582.0 jit_solution(2557040534260350899)
XLA Ops:
  8.0 22.3 %all-gather = bf16[8,120,2]{1,2,0:T(2,128)(2,1)S(1)} all-gather(bf16[1,120,2]{1,2,0:T(2,128)(2,1)} %bitcast.275), channel_id=1, replica_groups=mesh['shard'=2,'ctx'=4,'tensor'=4] {'shard','ctx'}, dimensions={0}, use_global_device_ids=true | all-gather | bytes 4320 | tf_op jit(solution)/shard_map/all_gather | solution.py:51
  33.8 34.0 %all_gather.28 = bf16[240,1600]{0,1:T(8,128)(2,1)S(1)} all-gather(bf16[240,200]{0,1:T(8,128)(2,1)} %param.16), channel_id=1, replica_groups=mesh['shard'=2,'ctx'=4,'tensor'=4] {'shard','ctx'}, dimensions={1}, use_global_device_ids=true | all-gather | bytes 864000 | tf_op jit(solution)/shard_map/all_gather | solution.py:52
  79.4 56.7 %reduce-scatter.17.cloned.1.call-done = bf16[2,256,1600]{1,2,0:T(8,128)(2,1)} async-done(((bf16[2,1024,1600]{1,2,0:T(8,128)(2,1)}), bf16[2,256,1600]{1,2,0:T(8,128)(2,1)}) %reduce-scatter.17.cloned.1.call-update) | async-done | bytes 1638416 | tf_op jit(solution)/shard_map/reduce_scatter | solution.py:74
  139.9 90.3 %all-gather.8.cloned.1.call-done = bf16[2,4096,640]{1,2,0:T(8,128)(2,1)} async-done(((bf16[2,256,640]{1,2,0:T(8,128)(2,1)}), bf16[2,4096,640]{1,2,0:T(8,128)(2,1)}) %all-gather.8.cloned.1.call-update) | async-done | bytes 10485776 | tf_op jit(solution)/shard_map/all_gather | solution.py:101
  230.3 17.0 %while.37 = (s32[]{:T(128)}, f32[2,5,3,256]{3,2,1,0:T(4,128)S(1)}, f32[2,5,3,256]{3,2,1,0:T(4,128)S(1)}, s32[]{:T(128)}, bf16[2,4096,640]{1,2,0:T(8,128)(2,1)}, ...) while((s32[]{:T(128)}, f32[2,5,3,256]{3,2,1,0:T(4,128)S(1)}, ...), condition=%wide.region_5.6_spmd.clone, body=%wide.region_2.5_spmd.clone.sunk | while | flops 530988800 | bytes 35205288 | solution.py:128
  238.4 8.8 exponential_reduce_fusion.2
  247.6 9.1 while.38
  258.8 28.3 %all-to-all-start = ((bf16[2,256,960]{1,0,2:T(2,128)(2,1)}), bf16[2,256,960]{1,0,2:T(2,128)(2,1)}, u32[]{:S(2)}, u32[]{:S(2)}) async-start(bf16[2,256,960]{1,0,2:T(2,128)(2,1)} %bitcast.256), calls=%async_computation.1 | async-start | bytes 1966080 | tf_op jit(solution)/shard_map/all_to_all | solution.py:146
  287.2 182.7 %all_gather.30 = bf16[240,960]{0,1:T(8,128)(2,1)S(1)} all-gather(bf16[240,120]{0,1:T(8,128)(2,1)S(1)} %copy.40), channel_id=1, replica_groups=mesh['shard'=2,'ctx'=4,'tensor'=4] {'shard','ctx'}, dimensions={1}, use_global_device_ids=true | all-gather | bytes 518400 | tf_op jit(solution)/shard_map/all_gather | solution.py:53
  477.5 82.2 %all-reduce.8.cloned.1.call-done = bf16[2,1024,960]{1,2,0:T(8,128)(2,1)} async-done(((bf16[2,1024,960]{1,2,0:T(8,128)(2,1)}), bf16[2,1024,960]{1,2,0:T(8,128)(2,1)}) %all-reduce.8.cloned.1.call-update) | async-done | bytes 3932176 | tf_op jit(solution)/shard_map/psum | solution.py:148
  569.6 8.3 fusion.65
  577.9 8.3 fusion.69
  586.2 21.5 %all-gather.14.cloned.1.call-done = bf16[640,960]{0,1:T(8,128)(2,1)} async-done(((bf16[640,120]{0,1:T(8,128)(2,1)}), bf16[640,960]{0,1:T(8,128)(2,1)}) %all-gather.14.cloned.1.call-update) | async-done | bytes 1228816 | tf_op jit(solution)/shard_map/all_gather | solution.py:56
  607.8 12.2 multiply_convert_fusion.1
  632.9 144.2 %all-reduce.10.cloned.1.call-done = (bf16[2,1024,960]{1,2,0:T(8,128)(2,1)}, bf16[2,1024,960]{1,2,0:T(8,128)(2,1)}) async-done(((bf16[2,1024,960]{1,2,0:T(8,128)(2,1)}, bf16[2,1024,960]{1,2,0:T(8,128)(2,1)}), (bf16[2,1024,960]{1,2,0:T(8,128)(2,1)}, bf16[2,1024,960]{1,2,0:T(8,128)(2,1)})) %all-reduce.10.cloned.1.call-update) | async-done | bytes 7864336 | tf_op jit(solution)/shard_map/psum | solution.py:156
  783.9 10.0 fusion.39
  807.1 14.5 all-to-all-done.1
  832.2 33.0 %while.39 = (s32[]{:T(128)}, f32[2,256,5,3,64]{1,4,3,2,0:T(8,128)S(1)}, bf16[2,4096,640]{1,2,0:T(8,128)(2,1)}, s32[]{:T(128)}, bf16[2,4096,640]{1,2,0:T(8,128)(2...) while((s32[]{:T(128)}, ...), condition=%wide.region_15.16_spmd.clone, body=%wide.region_14.15_spmd.clone.sunk | while | flops 2559804160 | bytes 90276096 | solution.py:236
  833.8 7.7 fusion.146
  841.5 10.2 fusion.148
  851.7 8.1 fusion.147
  866.4 348.2 %reduce-scatter.19.cloned.1.call-done = bf16[2,256,640]{1,2,0:T(8,128)(2,1)} async-done(((bf16[2,4096,640]{1,2,0:T(8,128)(2,1)}), bf16[2,256,640]{1,2,0:T(8,128)(2,1)}) %reduce-scatter.19.cloned.1.call-update) | async-done | bytes 655376 | tf_op jit(solution)/shard_map/reduce_scatter | solution.py:246
  1223.0 43.0 %all-gather.16.cloned.1.call-done = bf16[2,1024,1600]{1,2,0:T(8,128)(2,1)} async-done(((bf16[2,256,1600]{1,2,0:T(8,128)(2,1)}), bf16[2,1024,1600]{1,2,0:T(8,128)(2,1)}) %all-gather.16.cloned.1.call-update) | async-done | bytes 6553616 | tf_op jit(solution)/shard_map/all_gather | solution.py:265
  1271.9 7.9 convolution_bitcast_fusion.3
  1279.9 7.4 convolution_bitcast_fusion.2
  1287.4 8.7 fusion.53
  1311.1 22.2 %all-reduce = f32[2,960]{1,0:T(2,128)S(1)} all-reduce(f32[2,960]{1,0:T(2,128)S(1)} %pad_maximum_fusion.6), channel_id=4, replica_groups=mesh['shard'=2,'ctx'=4,'tensor'=4] {'shard','ctx'}, use_global_device_ids=true, to_apply=%region_20.21.clone | all-reduce | flops 1920 | bytes 15360
  1333.9 8.9 fusion.36
  1342.8 16.7 %reduce-scatter.25.cloned.1.call-done = f32[120,640]{1,0:T(8,128)} async-done(((f32[960,640]{1,0:T(8,128)}), f32[120,640]{1,0:T(8,128)}) %reduce-scatter.25.cloned.1.call-update) | async-done | bytes 307216
  1359.5 73.5 %reduce-scatter.27.cloned.1.call-done = f32[120,640]{1,0:T(8,128)} async-done(((f32[960,640]{1,0:T(8,128)}), f32[120,640]{1,0:T(8,128)}) %reduce-scatter.27.cloned.1.call-update) | async-done | bytes 307216
  1433.1 73.1 %reduce-scatter.29.cloned.1.call-done = f32[640,120]{0,1:T(8,128)} async-done(((f32[640,960]{0,1:T(8,128)}), f32[640,120]{0,1:T(8,128)}) %reduce-scatter.29.cloned.1.call-update) | async-done | bytes 307216
  1506.1 68.2 %reduce-scatter.21.cloned.1.call-done = f32[240,200]{0,1:T(8,128)} async-done(((f32[240,1600]{0,1:T(8,128)}), f32[240,200]{0,1:T(8,128)}) %reduce-scatter.21.cloned.1.call-update) | async-done | bytes 192016 | tf_op jit(solution)/shard_map/reduce_scatter | solution.py:280
  (178 shorter events, 135.8 us)
Async XLA Ops:
  8.0 128.1 %reduce-scatter.17.cloned.1.call-start = ((), (), s32[]{:S(2)}) async-start(), calls=%async_computation.9 | async-start | bytes 8192000 | tf_op jit(solution)/shard_map/reduce_scatter | solution.py:74
  30.5 37.3 %copy-start = (bf16[2,1024,960]{1,2,0:T(8,128)(2,1)S(1)}, bf16[2,1024,960]{1,2,0:T(8,128)(2,1)}, u32[]{:S(2)}) copy-start(bf16[2,1024,960]{1,2,0:T(8,128)(2,1)} %param.14) | copy-start | bytes 11796484
  30.5 41.6 %copy-start.18 = (f32[1,960]{1,0:T(1,128)}, f32[1,960]{1,0:T(1,128)S(1)}, u32[]{:S(2)}) copy-start(f32[1,960]{1,0:T(1,128)S(1)} %get-tuple-element.294) | copy-start | bytes 11524
  33.8 34.0 %copy-start.15 = (f32[2,1024]{1,0:T(2,128)}, f32[2,1024]{1,0:T(2,128)S(1)}, u32[]{:S(2)}) copy-start(f32[2,1024]{1,0:T(2,128)S(1)} %add_rsqrt_fusion.1) | copy-start | bytes 24580
  78.5 151.8 %all-gather.8.cloned.1.call-start = ((), (), s32[]{:S(2)}) async-start(), calls=%async_computation.10 | async-start | bytes 11141120 | tf_op jit(solution)/shard_map/all_gather | solution.py:101
  79.4 60.4 %copy-start.12 = (f32[256,32]{0,1:T(8,128)}, f32[256,32]{0,1:T(8,128)S(1)}, u32[]{:S(2)}) copy-start(f32[256,32]{0,1:T(8,128)S(1)} %get-tuple-element.297) | copy-start | bytes 98308
  256.7 30.4 %copy-start.17 = (bf16[240,120]{1,0:T(8,128)(2,1)S(1)}, bf16[240,120]{1,0:T(8,128)(2,1)}, u32[]{:S(2)}) copy-start(bf16[240,120]{1,0:T(8,128)(2,1)} %param.17) | copy-start | bytes 172804
  258.8 211.1 %all-to-all-start = ((bf16[2,256,960]{1,0,2:T(2,128)(2,1)}), bf16[2,256,960]{1,0,2:T(2,128)(2,1)}, u32[]{:S(2)}, u32[]{:S(2)}) async-start(bf16[2,256,960]{1,0,2:T(2,128)(2,1)} %bitcast.256), calls=%async_computation.1 | async-start | bytes 1966080 | tf_op jit(solution)/shard_map/all_to_all | solution.py:146
  287.1 272.5 %all-reduce.8.cloned.1.call-start = ((), (), s32[]{:S(2)}) async-start(), calls=%async_computation.11 | async-start | bytes 7864320 | tf_op jit(solution)/shard_map/psum | solution.py:148
  475.5 94.1 %all-gather.12.cloned.1.call-start = ((), (), s32[]{:S(2)}) async-start(), calls=%async_computation.13 | async-start | bytes 1382400 | tf_op jit(solution)/shard_map/all_gather | solution.py:55
  476.1 101.9 %all-gather.10.cloned.1.call-start = ((), (), s32[]{:S(2)}) async-start(), calls=%async_computation.12 | async-start | bytes 1382400 | tf_op jit(solution)/shard_map/all_gather | solution.py:54
  476.7 131.1 %all-gather.14.cloned.1.call-start = ((), (), s32[]{:S(2)}) async-start(), calls=%async_computation.14 | async-start | bytes 1382400 | tf_op jit(solution)/shard_map/all_gather | solution.py:56
  477.2 299.9 %all-reduce.10.cloned.1.call-start = ((), (), s32[]{:S(2)}) async-start(), calls=%async_computation.23 | async-start | bytes 15728640 | tf_op jit(solution)/shard_map/psum | solution.py:156
  607.8 12.2 copy-start.25
  620.0 8.1 copy-start.27
  802.8 18.8 %all-to-all-start.1 = ((bf16[2,1024,240]{2,0,1:T(2,128)(2,1)}), bf16[2,1024,240]{2,0,1:T(2,128)(2,1)}, u32[]{:S(2)}, u32[]{:S(2)}) async-start(bf16[2,1024,240]{2,0,1:T(2,128)(2,1)} %copy.42), calls=%async_computation.2 | async-start | bytes 2097152 | tf_op jit(solution)/shard_map/all_to_all | solution.py:189
  807.1 407.6 %reduce-scatter.19.cloned.1.call-start = ((), (), s32[]{:S(2)}) async-start(), calls=%async_computation.15 | async-start | bytes 11141120 | tf_op jit(solution)/shard_map/reduce_scatter | solution.py:246
  865.3 400.8 %all-gather.16.cloned.1.call-start = ((), (), s32[]{:S(2)}) async-start(), calls=%async_computation.16 | async-start | bytes 8192000 | tf_op jit(solution)/shard_map/all_gather | solution.py:265
  866.3 351.1 %copy-start.8 = (bf16[2,4,30,8,256]{4,3,1,2,0:T(8,128)(2,1)S(1)}, bf16[2,4,30,8,256]{4,3,1,2,0:T(8,128)(2,1)}, u32[]{:S(2)}) copy-start(bf16[2,4,30,8,256]{4,3,1,2,0:T(8,128)(2,1)} %copy-done.7) | copy-start | bytes 2949124
  1217.4 48.7 %copy-start.11 = (bf16[240,1600]{0,1:T(8,128)(2,1)S(1)}, bf16[240,1600]{0,1:T(8,128)(2,1)}, u32[]{:S(2)}) copy-start(bf16[240,1600]{0,1:T(8,128)(2,1)} %copy-done.10) | copy-start | bytes 2304004
  1217.4 87.0 %reduce-scatter.23.cloned.1.call-start = ((), (), s32[]{:S(2)}) async-start(), calls=%async_computation.19 | async-start | bytes 1105920
  1223.0 83.1 %all-gather.18.cloned.1.call-start = ((), (), s32[]{:S(2)}) async-start(), calls=%async_computation.17 | async-start | bytes 4915200 | tf_op jit(solution)/shard_map/all_gather | solution.py:272
  1271.9 8.1 copy-start.28
  1271.9 87.7 %reduce-scatter.25.cloned.1.call-start = ((), (), s32[]{:S(2)}) async-start(), calls=%async_computation.20 | async-start | bytes 2764800
  1279.9 153.2 %reduce-scatter.27.cloned.1.call-start = ((), (), s32[]{:S(2)}) async-start(), calls=%async_computation.21 | async-start | bytes 2764800
  1287.3 9.1 copy-start.22
  1287.3 218.8 %reduce-scatter.29.cloned.1.call-start = ((), (), s32[]{:S(2)}) async-start(), calls=%async_computation.22 | async-start | bytes 2764800
  1296.1 7.0 copy-start.26
  1296.1 9.9 copy-start.16
  1296.1 9.9 copy-start.19
  1296.2 278.2 %reduce-scatter.21.cloned.1.call-start = ((), (), s32[]{:S(2)}) async-start(), calls=%async_computation.18 | async-start | bytes 1843200 | tf_op jit(solution)/shard_map/reduce_scatter | solution.py:280
  1303.1 7.9 copy-start.20
  (16 other events, 63.3 us)
Sparse Core Ops, SparseCore 0:
  78.6 57.4 reduce-scatter.16
  139.5 90.7 all-gather.7
  475.6 83.9 all-reduce.7
  633.1 144.0 all-reduce.9
  865.4 349.2 reduce-scatter.18
  1217.5 48.4 all-gather.15
  1272.0 33.0 all-gather.17
Sparse Core Ops, SparseCore 1:
  478.3 44.2 all-gather.11
  524.8 40.2 all-gather.9
  567.3 40.4 all-gather.13
  1223.0 63.1 reduce-scatter.22
  1290.5 69.0 reduce-scatter.24
  1363.8 69.3 reduce-scatter.26
  1437.2 68.9 reduce-scatter.28
  1510.0 64.3 reduce-scatter.20
where the time goes:
time: 1590 us; the launch traced here: 1580 us
  waiting for transfers between devices  1030 us (65%)
  blocking collectives  261 us (16%)
  matrix products  138 us (9%)
  other arithmetic  64.5 us (4%)
  starting transfers between devices  33.5 us (2%)
  local copies, waits for them, and re-layouts  32.8 us (2%)
  between operations  17.1 us (1%)
    reduce_scatter x1, waiting for transfers between devices, shards(): lax.psum_scatter(pair_grad.astype(jnp.bfloat16), ('ctx', 'tensor'), scatt...  348 us
    all_gather x1, blocking collectives, shards(): lax.all_gather(out_weight, ('shard', 'ctx'), axis=1, tiled=True)  183 us
    unnamed x19, waiting for transfers between devices  165 us
    psum x1, waiting for transfers between devices, shards(): lax.psum(jnp.einsum('scf,fe->sce', inner_act, down_all, preferred_element...  144 us
    all_gather x1, waiting for transfers between devices, shards(): pair_all = lax.all_gather(pair_own, ('ctx', 'tensor'), axis=1, tiled=True)  90.3 us
    psum x1, waiting for transfers between devices, shards(): lax.psum(attn_term.astype(jnp.bfloat16), 'tensor').astype(jnp.float32)  82.2 us
    reduce_scatter x1, waiting for transfers between devices, shards(): lax.psum_scatter(qkv_weight_grad, ('shard', 'ctx'), scatter_dimension=1,...  68.2 us
    reduce_scatter x1, waiting for transfers between devices, shards(): lax.psum_scatter(jnp.einsum('scd,de->sce', normed_part, qkv_all, preferre...  56.7 us
  transfers between devices with their start and end apart: 17, of which 12 were waited for; matrix products, arithmetic and copies ran while one was open for 6% of the time, Pallas kernels for 0%

commit v1 on v0

v1 whole, which is shorter than its diff:
```python
import functools

import jax
import jax.numpy as jnp
from jax import lax
from jax.experimental import pallas as pl
from jax.experimental.pallas import tpu as pltpu
from jax.sharding import Mesh
from jax.sharding import PartitionSpec as P

HEADS = 15
KV_HEADS = 5
HEAD_DIM = 64
GROUP = 3
LANES = 128
HALF = HEAD_DIM


epsilon = 1e-05
rope_base = 100000.0
masked_score = -1e30


def pair_place(pair, ctx_count, sub):
    turn = pair // (2 * sub)
    spot = pair % (2 * sub)
    low = spot < sub
    return jnp.where(low, turn * sub + spot, (ctx_count - 1 - turn) * sub + 2 * sub - 1 - spot)


def dot_nt(a, b):
    return lax.dot_general(a, b, (((1,), (1,)), ((), ())), preferred_element_type=jnp.float32)


def dot_nn(a, b):
    return lax.dot_general(a, b, (((1,), (0,)), ((), ())), preferred_element_type=jnp.float32)


def dot_tn(a, b):
    return lax.dot_general(a, b, (((0,), (0,)), ((), ())), preferred_element_type=jnp.float32)


def causal(rows, cols, chunk, key_axis):
    shape = (rows, cols)
    query_axis = 1 - key_axis
    query = lax.broadcasted_iota(jnp.int32, shape, query_axis)
    key = lax.broadcasted_iota(jnp.int32, shape, key_axis)
    return key <= lax.rem(query, chunk)


def forward_kernel(ctx_count, sub, chunk, group, pair_ref, q_ref, kv_ref, out_ref, top, total):
    pairs = ctx_count * sub
    own = pair_ref[0]
    part = group * chunk
    lanes = lambda rows: lax.broadcasted_iota(jnp.int32, (rows, LANES), 1)

    def load(place, slot, count):
        return kv_ref[0, pl.ds(pl.multiple_of(place * 2 * chunk + slot * chunk, chunk), count * chunk), :]

    def weighted(powers, kv):
        ones = jnp.where(lanes(kv.shape[0]) < HALF, jnp.ones_like(kv), kv)
        return dot_nn(powers, ones)

    def update(start, rows, kv, first, mask):
        scores = dot_nt(q_ref[0, start : start + rows, :], kv)
        if mask is not None:
            scores = jnp.where(mask, scores, masked_score)
        best = jnp.max(scores, axis=1, keepdims=True)
        spot = slice(start, start + rows)
        if first:
            top[spot, :] = jnp.broadcast_to(best, (rows, LANES))
            powers = jnp.exp(scores - best).astype(jnp.bfloat16)
            total[spot, :] = weighted(powers, kv)
        else:
            old = top[spot, :]
            new = jnp.maximum(old, best)
            powers = jnp.exp(scores - new[:, :1]).astype(jnp.bfloat16)
            total[spot, :] = total[spot, :] * jnp.exp(old - new) + weighted(powers, kv)
            top[spot, :] = new

    place = pair_place(own, ctx_count, sub)
    near = load(place, 0, 1)
    both = load(place, 0, 2)
    near_mask = causal(chunk, chunk, chunk, 1)
    columns = lax.broadcasted_iota(jnp.int32, (chunk, 2 * chunk), 1)
    queries = lax.broadcasted_iota(jnp.int32, (chunk, 2 * chunk), 0)
    both_mask = columns <= queries + chunk
    for head in range(group):
        update(head * chunk, chunk, near, True, near_mask)
        update(part + head * chunk, chunk, both, True, both_mask)

    @pl.loop(0, own)
    def _(pair):
        kv = load(pair_place(pair, ctx_count, sub), 0, 1)
        for head in range(2 * group):
            update(head * chunk, chunk, kv, False, None)

    @pl.loop(own + 1, pairs)
    def _(pair):
        kv = load(pair_place(pair, ctx_count, sub), 0, 2)
        for head in range(group):
            update(part + head * chunk, chunk, kv, False, None)

    for head in range(2 * group):
        spot = slice(head * chunk, (head + 1) * chunk)
        sums = total[spot, :]
        count = sums[:, :1]
        out_ref[0, spot, :] = jnp.where(
            lanes(chunk) < HALF, top[spot, :] + jnp.log(count), sums / count
        )


def attention_forward(own_pair, queries, pairs_all, ctx_count, sub, chunk, group):
    heads, rows, _ = queries.shape
    length = pairs_all.shape[1]
    grid_spec = pltpu.PrefetchScalarGridSpec(
        num_scalar_prefetch=1,
        grid=(heads,),
        in_specs=[
            pl.BlockSpec((1, rows, LANES), lambda h, p: (h, 0, 0)),
            pl.BlockSpec((1, length, LANES), lambda h, p: (h, 0, 0)),
        ],
        out_specs=pl.BlockSpec((1, rows, LANES), lambda h, p: (h, 0, 0)),
        scratch_shapes=[
            pltpu.VMEM((rows, LANES), jnp.float32),
            pltpu.VMEM((rows, LANES), jnp.float32),
        ],
    )
    cost = heads * rows * length // 2
    return pl.pallas_call(
        functools.partial(forward_kernel, ctx_count, sub, chunk, group),
        out_shape=jax.ShapeDtypeStruct((heads, rows, LANES), jnp.float32),
        grid_spec=grid_spec,
        compiler_params=pltpu.CompilerParams(vmem_limit_bytes=48 * 2**20),
        cost_estimate=pl.CostEstimate(
            flops=cost * 4 * HALF, bytes_accessed=heads * LANES * (rows * 6 + length * 2), transcendentals=cost
        ),
        name="attention_forward",
    )(own_pair, queries, pairs_all)


def backward_kernel(
    ctx_count, sub, chunk, group, pair_ref, q_ref, cot_ref, extra_ref, kv_ref, dq_ref, dkv_ref
):
    pairs = ctx_count * sub
    own = pair_ref[0]
    part = group * chunk

    def minus(rows, low, high):
        lane = lax.broadcasted_iota(jnp.int32, (rows, LANES), 1)
        return jnp.where((lane >= low) & (lane < high), -1.0, 0.0).astype(jnp.bfloat16)

    def step(start, rows, place, slot, count, first, mask):
        keys = count * chunk
        base = pl.multiple_of(place * 2 * chunk + slot * chunk, chunk)
        kv = kv_ref[0, pl.ds(base, keys), :]
        key_side = jnp.concatenate([kv, minus(keys, 0, 3)], axis=1)
        value_side = jnp.concatenate([kv, minus(keys, 3, 6)], axis=1)
        pair_sum = None
        for at in range(start, start + rows, chunk):
            spot = slice(at, at + chunk)
            query = q_ref[0, spot, :]
            cot = cot_ref[0, spot, :]
            extra = extra_ref[0, spot, :]
            powers = jnp.exp(dot_nt(key_side, jnp.concatenate([query, extra], axis=1)))
            if mask is not None:
                powers = jnp.where(mask, powers, 0.0)
            slope = dot_nt(value_side, jnp.concatenate([cot, extra], axis=1))
            grads = (powers * slope).astype(jnp.bfloat16)
            powers = powers.astype(jnp.bfloat16)
            term = dot_nn(powers, cot) + dot_nn(grads, query)
            pair_sum = term if pair_sum is None else pair_sum + term
            moved = dot_tn(grads, kv)
            if first:
                dq_ref[0, spot, :] = moved
            else:
                dq_ref[0, spot, :] += moved
        return pair_sum

    def store(place, slot, count, value):
        base = pl.multiple_of(place * 2 * chunk + slot * chunk, chunk)
        dkv_ref[0, pl.ds(base, count * chunk), :] = value.astype(jnp.bfloat16)

    place = pair_place(own, ctx_count, sub)
    near_mask = causal(chunk, chunk, chunk, 0)
    keys = lax.broadcasted_iota(jnp.int32, (2 * chunk, chunk), 0)
    queries = lax.broadcasted_iota(jnp.int32, (2 * chunk, chunk), 1)
    far = step(part, part, place, 0, 2, True, keys <= queries + chunk)
    near = step(0, part, place, 0, 1, True, near_mask)
    store(place, 0, 1, far[:chunk] + near)
    store(place, 1, 1, far[chunk:])

    @pl.loop(0, own)
    def _(pair):
        at = pair_place(pair, ctx_count, sub)
        store(at, 0, 1, step(0, 2 * part, at, 0, 1, False, None))
        store(at, 1, 1, jnp.zeros((chunk, LANES), jnp.float32))

    @pl.loop(own + 1, pairs)
    def _(pair):
        at = pair_place(pair, ctx_count, sub)
        store(at, 0, 2, step(part, part, at, 0, 2, False, None))


def attention_backward(own_pair, queries, cots, extra, pairs_all, ctx_count, sub, chunk, group):
    heads, rows, _ = queries.shape
    length = pairs_all.shape[1]
    row_spec = pl.BlockSpec((1, rows, LANES), lambda h, p: (h, 0, 0))
    long_spec = pl.BlockSpec((1, length, LANES), lambda h, p: (h, 0, 0))
    cost = heads * rows * length // 2
    return pl.pallas_call(
        functools.partial(backward_kernel, ctx_count, sub, chunk, group),
        out_shape=(
            jax.ShapeDtypeStruct((heads, rows, LANES), jnp.float32),
            jax.ShapeDtypeStruct((heads, length, LANES), jnp.bfloat16),
        ),
        grid_spec=pltpu.PrefetchScalarGridSpec(
            num_scalar_prefetch=1,
            grid=(heads,),
            in_specs=[row_spec, row_spec, row_spec, long_spec],
            out_specs=(row_spec, long_spec),
        ),
        compiler_params=pltpu.CompilerParams(vmem_limit_bytes=48 * 2**20),
        cost_estimate=pl.CostEstimate(
            flops=cost * 10 * HALF, bytes_accessed=heads * LANES * (rows * 10 + length * 4), transcendentals=cost
        ),
        name="attention_backward",
    )(own_pair, queries, cots, extra, pairs_all)


def three_parts(values):
    high = values.astype(jnp.bfloat16)
    rest = values - high.astype(jnp.float32)
    middle = rest.astype(jnp.bfloat16)
    low = (rest - middle.astype(jnp.float32)).astype(jnp.bfloat16)
    return [high, middle, low]


def rope_tables(positions):
    half_dim = HEAD_DIM // 2
    frequency = rope_base ** (-2.0 * jnp.arange(half_dim, dtype=jnp.float32) / HEAD_DIM)
    angles = positions.astype(jnp.float32)[:, None] * frequency[None, :]
    return (jnp.cos(angles)[:, None, :], jnp.sin(angles)[:, None, :])


def rotate(values, cosine_table, sine_table):
    half_dim = HEAD_DIM // 2
    first_half = values[..., :half_dim]
    second_half = values[..., half_dim:]
    return jnp.concatenate(
        [
            first_half * cosine_table - second_half * sine_table,
            second_half * cosine_table + first_half * sine_table,
        ],
        axis=-1,
    )


def norm_parts(values, gain_row):
    inv_rms = lax.rsqrt(jnp.mean(values * values, axis=-1, keepdims=True) + epsilon)
    unit_rows = values * inv_rms
    return (unit_rows, inv_rms, unit_rows * gain_row)


def norm_back(upstream, unit_rows, inv_rms, gain_row):
    shaped = upstream * gain_row
    inner_mean = jnp.mean(shaped * unit_rows, axis=-1, keepdims=True)
    return (inv_rms * (shaped - unit_rows * inner_mean), jnp.sum(upstream * unit_rows, axis=0))


def matmul(spec, left, right):
    return jnp.einsum(spec, left, right, preferred_element_type=jnp.float32)


def swap_ends(values):
    count = lax.axis_size("ctx")
    return lax.ppermute(values, "ctx", [(i, count - 1 - i) for i in range(count)])


def spread(values):
    count = lax.axis_size("sub")
    parts = [values]
    for shift in range(1, count):
        parts.append(lax.ppermute(values, "sub", [(i, (i + shift) % count) for i in range(count)]))
    return jnp.concatenate(parts, axis=0)


def collect(values):
    count = lax.axis_size("sub")
    parts = jnp.split(values, count, axis=0)
    total = parts[0].astype(jnp.float32)
    for shift in range(1, count):
        total = total + lax.ppermute(
            parts[shift].astype(jnp.bfloat16), "sub", [((i + shift) % count, i) for i in range(count)]
        ).astype(jnp.float32)
    return total


def shards(tokens, gains, qkv_weight, out_weight, gate_weight, up_weight, down_weight, cotangent):
    seq_count, span_len, width = tokens.shape
    ctx_count, sub_count = lax.axis_size("ctx"), lax.axis_size("sub")
    pair_count = ctx_count * sub_count
    chunk = span_len // (2 * sub_count)
    row_count = 2 * chunk
    kv_width = KV_HEADS * HEAD_DIM
    owners = lax.axis_size(("shard", "ctx"))
    tensor_count = lax.axis_size(("seq", "sub"))
    everyone = ("seq", "sub", "shard", "ctx")
    own_seq, own_sub, own_ctx = lax.axis_index("seq"), lax.axis_index("sub"), lax.axis_index("ctx")
    is_low = own_ctx < ctx_count // 2
    own_pair = jnp.where(
        is_low,
        2 * sub_count * own_ctx + own_sub,
        2 * pair_count - 1 - 2 * sub_count * own_ctx - own_sub,
    ).astype(jnp.int32)
    scale_factor = HEAD_DIM ** (-0.5)

    def take_rows(values):
        span = lax.dynamic_index_in_dim(values, own_seq, 0, keepdims=False)
        kept = lax.dynamic_slice_in_dim(span, own_sub * chunk, chunk, 0)
        moved = lax.dynamic_slice_in_dim(span, (2 * sub_count - 1 - own_sub) * chunk, chunk, 0)
        return kept, moved

    def in_order(kept, moved):
        return jnp.where(is_low, jnp.concatenate([kept, moved]), jnp.concatenate([moved, kept]))

    def give_rows(values):
        low, high = values[:chunk], values[chunk:]
        kept = jnp.where(is_low, low, high)
        moved = swap_ends(jnp.where(is_low, high, low))
        both = lax.all_gather(jnp.stack([kept, moved]), ("seq", "sub"), axis=0, tiled=False)
        both = both.reshape(seq_count, sub_count, 2, chunk, width)
        return jnp.concatenate([both[:, :, 0], both[:, ::-1, 1]], axis=1).reshape(
            seq_count, span_len, width
        )

    tile_rows, tile_cols = qkv_weight.shape
    gain_part = gains.shape[1]
    first_tile = jnp.concatenate(
        [qkv_weight, jnp.pad(gains, ((0, 0), (0, tile_cols - gain_part)))], axis=0
    )
    first_all = lax.all_gather(first_tile, everyone, axis=0, tiled=False).reshape(
        tensor_count, owners, tile_rows + 2, tile_cols
    )
    qkv_all = jnp.transpose(first_all[:, :, :tile_rows], (0, 2, 1, 3)).reshape(
        tensor_count * tile_rows, owners * tile_cols
    )
    gain_all = (
        jnp.transpose(first_all[0, :, tile_rows:, :gain_part], (1, 0, 2))
        .reshape(2, width)
        .astype(jnp.float32)
    )
    gain_one, gain_two = gain_all[0], gain_all[1]
    out_rows, out_cols = out_weight.shape
    out_all = jnp.transpose(
        lax.all_gather(out_weight, everyone, axis=0, tiled=False).reshape(
            tensor_count, owners, out_rows, out_cols
        ),
        (0, 2, 1, 3),
    ).reshape(width, width)
    hidden_part = gate_weight.shape[1]
    ffn_tile = jnp.concatenate([gate_weight, up_weight, down_weight.T], axis=1)
    ffn_all = lax.all_gather(ffn_tile, ("seq", "shard", "ctx"), axis=0, tiled=True).reshape(
        seq_count, width, 3 * hidden_part
    )

    kept_tokens, moved_tokens = take_rows(tokens)
    kept_cot, moved_cot = take_rows(cotangent)
    rows_low = in_order(kept_tokens, swap_ends(moved_tokens))
    cot = in_order(kept_cot, swap_ends(moved_cot.astype(jnp.bfloat16)).astype(jnp.float32))
    inputs = rows_low.astype(jnp.float32)
    unit_one, rms_one, normed_full = norm_parts(inputs, gain_one)
    normed = normed_full.astype(jnp.bfloat16)
    projected = matmul("rd,de->re", normed, qkv_all)
    step = jnp.arange(chunk, dtype=jnp.int32)
    positions = jnp.concatenate([own_pair * chunk + step, (2 * pair_count - 1 - own_pair) * chunk + step])
    cosine_table, sine_table = rope_tables(positions)
    queries = rotate(
        projected[:, :width].reshape(row_count, HEADS, HEAD_DIM), cosine_table, sine_table
    )
    keys = rotate(
        projected[:, width : width + kv_width].reshape(row_count, KV_HEADS, HEAD_DIM),
        cosine_table,
        sine_table,
    )
    values = projected[:, width + kv_width :].reshape(row_count, KV_HEADS, HEAD_DIM)

    def by_head(rows, before, after):
        rows = rows.reshape(2, chunk, KV_HEADS, GROUP, HEAD_DIM)
        rows = jnp.transpose(rows, (2, 0, 3, 1, 4)).reshape(KV_HEADS, GROUP * row_count, HEAD_DIM)
        return jnp.pad(rows, ((0, 0), (0, 0), (before, after)))

    def by_row(rows):
        rows = rows.reshape(KV_HEADS, 2, GROUP, chunk, HEAD_DIM)
        return jnp.transpose(rows, (1, 3, 0, 2, 4)).reshape(row_count, HEADS, HEAD_DIM)

    query_heads = by_head(queries.astype(jnp.bfloat16) * jnp.bfloat16(scale_factor), 0, HEAD_DIM)
    pair_own = jnp.transpose(
        jnp.concatenate([keys, values], axis=-1).astype(jnp.bfloat16), (1, 0, 2)
    )
    pair_all = lax.all_gather(pair_own, ("ctx", "sub"), axis=1, tiled=True)
    place = own_pair[None]
    attended = attention_forward(place, query_heads, pair_all, ctx_count, sub_count, chunk, GROUP)
    attn_sum = attended[..., HEAD_DIM:]
    log_total = attended[..., 0]
    attn_low = by_row(attn_sum.astype(jnp.bfloat16)).reshape(row_count, width)
    hidden = inputs + matmul("rf,fe->re", attn_low, out_all)
    unit_two, rms_two, normed_two_full = norm_parts(hidden, gain_two)
    normed_two = spread(normed_two_full.astype(jnp.bfloat16))
    cot_low = spread(cot.astype(jnp.bfloat16))
    feed_sum, normed_sum, ffn_grads = 0.0, 0.0, []
    for part in range(seq_count):
        gate_up = ffn_all[part, :, : 2 * hidden_part]
        down = ffn_all[part, :, 2 * hidden_part :]
        both = matmul("rd,df->rf", normed_two, gate_up)
        gate_value, up_value = both[:, :hidden_part], both[:, hidden_part:]
        gate_sigmoid = jax.nn.sigmoid(gate_value)
        inner_act = (gate_value * gate_sigmoid * up_value).astype(jnp.bfloat16)
        feed_sum = feed_sum + matmul("rf,ef->re", inner_act, down)
        inner_grad = matmul("re,ef->rf", cot_low, down)
        gate_grad = (
            inner_grad * up_value * gate_sigmoid * (1.0 + gate_value * (1.0 - gate_sigmoid))
        ).astype(jnp.bfloat16)
        up_grad = (inner_grad * gate_value * gate_sigmoid).astype(jnp.bfloat16)
        both_grad = jnp.concatenate([gate_grad, up_grad], axis=1)
        normed_sum = normed_sum + matmul("rf,df->rd", both_grad, gate_up)
        ffn_grads.append(
            jnp.concatenate(
                [
                    matmul("rd,rf->df", normed_two, both_grad).astype(jnp.bfloat16),
                    matmul("re,rf->ef", cot_low, inner_act).astype(jnp.bfloat16),
                ],
                axis=1,
            )
        )
    normed_two_grad = collect(normed_sum)
    block_out = give_rows((hidden + collect(feed_sum)).astype(jnp.bfloat16))
    hidden_part_grad, gain_two_grad = norm_back(normed_two_grad, unit_two, rms_two, gain_two)
    hidden_grad = cot + hidden_part_grad
    hidden_low = hidden_grad.astype(jnp.bfloat16)
    attn_grad = matmul("re,fe->rf", hidden_low, out_all).astype(jnp.bfloat16)
    grad_heads = by_head(attn_grad, HEAD_DIM, 0)
    row_delta = jnp.sum(grad_heads[..., HEAD_DIM:].astype(jnp.float32) * attn_sum, axis=-1)
    extra = jnp.stack(three_parts(log_total) + three_parts(row_delta), axis=-1)
    extra = jnp.pad(extra, ((0, 0), (0, 0), (0, LANES - extra.shape[-1])))
    query_grad, pair_grad = attention_backward(
        place, query_heads, grad_heads, extra, pair_all, ctx_count, sub_count, chunk, GROUP
    )
    pair_own_grad = jnp.transpose(
        lax.psum_scatter(pair_grad, ("ctx", "sub"), scatter_dimension=1, tiled=True).astype(jnp.float32),
        (1, 0, 2),
    )
    query_back = rotate(by_row(query_grad[..., :HEAD_DIM] * scale_factor), cosine_table, -sine_table)
    key_back = rotate(pair_own_grad[..., :HEAD_DIM], cosine_table, -sine_table)
    proj_grad = jnp.concatenate(
        [
            query_back.reshape(row_count, width),
            key_back.reshape(row_count, kv_width),
            pair_own_grad[..., HEAD_DIM:].reshape(row_count, kv_width),
        ],
        axis=-1,
    ).astype(jnp.bfloat16)
    normed_grad = matmul("re,de->rd", proj_grad, qkv_all)
    input_part_grad, gain_one_grad = norm_back(normed_grad, unit_one, rms_one, gain_one)
    input_grad = give_rows((hidden_grad + input_part_grad).astype(jnp.bfloat16)).astype(jnp.float32)

    def tiles(grad, rows, cols):
        grad = grad.reshape(tensor_count, rows, owners, cols)
        return jnp.transpose(grad, (0, 2, 1, 3))

    qkv_grad = tiles(matmul("rd,re->de", normed, proj_grad).astype(jnp.bfloat16), tile_rows, tile_cols)
    gains_grad = jnp.transpose(
        jnp.stack([gain_one_grad, gain_two_grad]).reshape(2, owners, gain_part), (1, 0, 2)
    ).astype(jnp.bfloat16)
    gains_tile = jnp.pad(gains_grad, ((0, 0), (0, 0), (0, tile_cols - gain_part)))
    last = jnp.concatenate(
        [qkv_grad, jnp.broadcast_to(gains_tile, (tensor_count,) + gains_tile.shape)], axis=2
    ).reshape(tensor_count * owners, tile_rows + 2, tile_cols)
    last = lax.psum_scatter(last, everyone, scatter_dimension=0, tiled=False).astype(jnp.float32)
    out_grad = tiles(
        matmul("rf,re->fe", attn_low, hidden_low).astype(jnp.bfloat16), out_rows, out_cols
    ).reshape(tensor_count * owners, out_rows, out_cols)
    out_out = lax.psum_scatter(out_grad, everyone, scatter_dimension=0, tiled=False).astype(jnp.float32)
    ffn_out = lax.psum_scatter(
        jnp.concatenate(ffn_grads, axis=0), ("seq", "shard", "ctx"), scatter_dimension=0, tiled=True
    ).astype(jnp.float32)
    return (
        block_out,
        input_grad,
        last[tile_rows:, :gain_part],
        last[:tile_rows],
        out_out,
        ffn_out[:, :hidden_part],
        ffn_out[:, hidden_part : 2 * hidden_part],
        ffn_out[:, 2 * hidden_part :].T,
    )


def solution(mesh):
    shard_count, ctx_count, tensor_count = (mesh.shape[axis] for axis in ("shard", "ctx", "tensor"))

    def run(tokens, *rest):
        seq_count = tokens.shape[0] // shard_count
        split = Mesh(
            mesh.devices.reshape(shard_count, ctx_count, seq_count, tensor_count // seq_count),
            ("shard", "ctx", "seq", "sub"),
        )
        rows = P("shard", "ctx", None)
        pool = ("shard", "ctx")
        team = ("seq", "sub")
        weights = (P(None, pool), P(team, pool), P(team, pool), P(pool, team), P(pool, team), P(team, pool))
        return jax.shard_map(
            shards,
            mesh=split,
            in_specs=(rows,) + weights + (rows,),
            out_specs=(rows, rows) + weights,
            check_vma=False,
        )(tokens, *rest)

    return run
```

time: 1590 us -> 1050 us (0.66)
  waiting for transfers between devices: 1030 us -> 586 us
  blocking collectives: 261 us -> 0 us
  Pallas kernels: 0 us -> 133 us
  local copies, waits for them, and re-layouts: 32.8 us -> 135 us
  matrix products: 138 us -> 64.2 us
    reduce_scatter x3, waiting for transfers between devices: 473 us -> 178 us  [the longest x1 144 us: shards(): lax.psum_scatter(last, everyone, scatter_dimension=0, tiled=False)]
    all_gather x3 -> x0, blocking collectives: 239 us -> none  [the longest x1 183 us: shards(): lax.all_gather(out_weight, ('shard', 'ctx'), axis=1, tiled=True)]
    psum x2 -> x0, waiting for transfers between devices: 226 us -> none  [the longest x1 144 us: shards(): lax.psum(jnp.einsum('scf,fe->sce', inner_act, down_all, preferred_element...]
    pallas_call x0 -> x2, Pallas kernels: none -> 133 us  [the longest x1 69.4 us: attention_backward(): pl.pallas_call(functools.partial(backward_kernel, ctx_count, sub, chunk,...]
    dot_general x22 -> x18, matrix products: 138 us -> 64.2 us  [matmul(): return jnp.einsum(spec, left, right, preferred_element_type=jnp.float32)]
    all_gather x6, waiting for transfers between devices: 155 us -> 215 us  [the longest x2 61.2 us: give_rows(): lax.all_gather(jnp.stack([kept, moved]), ('seq', 'sub'), axis=0, tiled=Fa...]
    reshape x0 -> x13, local copies, waits for them, and re-layouts: none -> 49.7 us  [the longest x3 19.7 us: tiles(): grad = grad.reshape(tensor_count, rows, owners, cols)]
    ppermute x0 -> x8, waiting for transfers between devices: none -> 39.3 us  [the longest x4 39.3 us: swap_ends(): lax.ppermute(values, 'ctx', [(i, count - 1 - i) for i in range(count)])]
  transfers between devices with their start and end apart: 17 -> 18, of which waited for: 12 -> 12; matrix products, arithmetic and copies ran while one was open for 6% -> 19% of each run, Pallas kernels for 0% -> 6%
where the time goes in v1:
time: 1050 us; the launch traced here: 1040 us
  waiting for transfers between devices  586 us (56%)
  local copies, waits for them, and re-layouts  135 us (13%)
  Pallas kernels  133 us (13%)
  other arithmetic  80 us (8%)
  matrix products  64.2 us (6%)
  starting transfers between devices  22.7 us (2%)
  between operations  15.7 us (1%)
    unnamed x11, waiting for transfers between devices  153 us
    reduce_scatter x1, waiting for transfers between devices, shards(): lax.psum_scatter(last, everyone, scatter_dimension=0, tiled=False)  144 us
    pallas_call x1, Pallas kernels, attention_backward(): pl.pallas_call(functools.partial(backward_kernel, ctx_count, sub, chunk,...  69.4 us
    dot_general x18, matrix products, matmul(): return jnp.einsum(spec, left, right, preferred_element_type=jnp.float32)  64.2 us
    pallas_call x1, Pallas kernels, attention_forward(): pl.pallas_call(functools.partial(forward_kernel, ctx_count, sub, chunk, g...  63.6 us
    all_gather x2, waiting for transfers between devices, give_rows(): lax.all_gather(jnp.stack([kept, moved]), ('seq', 'sub'), axis=0, tiled=Fa...  61.2 us
    all_gather x1, waiting for transfers between devices, shards(): lax.all_gather(first_tile, everyone, axis=0, tiled=False)  48.4 us
    all_gather x1, waiting for transfers between devices, shards(): pair_all = lax.all_gather(pair_own, ('ctx', 'sub'), axis=1, tiled=True)  43.6 us
  transfers between devices with their start and end apart: 18, of which 12 were waited for; matrix products, arithmetic and copies ran while one was open for 19% of the time, Pallas kernels for 6%

profile of v1, /device:TPU:0, one launch (start us, length us, event | category | flops | bytes accessed | tf_op | source)
XLA Modules:
  0.0 1036.6 jit_solution(4580496619107448052)
XLA Ops:
  12.2 5.1 collective-permute-start
  19.2 10.2 collective-permute-done
  29.8 48.4 %all-gather.22.cloned.1.call-done = bf16[32,242,200]{1,2,0:T(8,128)(2,1)} async-done(((bf16[1,242,200]{1,2,0:T(8,128)(2,1)}), bf16[32,242,200]{1,2,0:T(8,128)(2,1)}) %all-gather.22.cloned.1.call-update) | async-done | bytes 3097616 | tf_op jit(solution)/shard_map/all_gather | solution.py:342
  80.0 4.5 copy.206
  89.8 4.5 fusion.30
  107.8 37.4 %all-gather.16.cloned.1.call-done = bf16[7680,120]{1,0:T(8,128)(2,1)} async-done(((bf16[240,120]{1,0:T(8,128)(2,1)}), bf16[7680,120]{1,0:T(8,128)(2,1)}) %all-gather.16.cloned.1.call-update) | async-done | bytes 1843216 | tf_op jit(solution)/shard_map/all_gather | solution.py:356
  158.6 43.6 %all-gather.12.cloned.1.call-done.kv_ref = bf16[5,4096,128]{2,1,0:T(8,128)(2,1)} async-done(((bf16[5,512,128]{2,1,0:T(8,128)(2,1)}), bf16[5,4096,128]{2,1,0:T(8,128)(2,1)}) %all-gather.12.cloned.1.call-update) | async-done | bytes 5242896 | tf_op jit(solution)/shard_map/all_gather | solution.py:401
  202.2 63.6 %attention_forward.1 = f32[5,1536,128]{2,1,0:T(8,128)S(1)} custom-call(s32[1]{0:T(128)} %bitcast.2.pair_ref, bf16[5,1536,128]{2,1,0:T(8,128)(2,1)S(1)} %pad.21.q_ref, bf16[5,4096,128]{2,1,0:T(8,128)(2,1)} %all-gather.12.cloned.1.call-done.kv_ref), custom_call_target="tpu_custom_call" | custom-call | flops 4026531840 | bytes 11141120 | tf_op jit(solution)/shard_map/attention_forward/pallas_call | solution.py:130
  283.1 24.5 %all-gather.14.cloned.1.call-done = bf16[1920,1920]{1,0:T(8,128)(2,1)} async-done(((bf16[120,1920]{1,0:T(8,128)(2,1)}), bf16[1920,1920]{1,0:T(8,128)(2,1)}) %all-gather.14.cloned.1.call-update) | async-done | bytes 7372816 | tf_op jit(solution)/shard_map/all_gather | solution.py:363
  307.7 5.4 fusion.6
  313.1 4.4 multiply_convert_fusion.3
  320.3 4.7 fusion.8
  353.2 4.9 multiply_reduce_fusion
  368.3 6.0 subtract_convert_fusion
  374.3 12.2 %stack.39 = bf16[5,1536,6]{2,1,0:T(8,128)(2,1)} concatenate(bf16[5,1536,1]{2,1,0:T(8,128)(2,1)} %get-tuple-element.66, bf16[5,1536,1]{2,1,0:T(8,128)(2,1)} %get-tuple-element.65, bf16[5,1536,1]{2,1,0:T(8,128)(2,1)} %get-tuple-element.64, bf16[5,1536,1]{2,1,0:T(8,128)(2,1)} %copy.179, bf16[5,1536,1]{2,1,0:T(8,128)(2,1)} %get-tuple-element.68, bf16[5,1536,1]{2,1,0:T(8,128)(2,1)} %get-tuple-element.67), dimensions={2} | concatenate | bytes 184320 | tf_op jit(solution)/shard_map/stack | solution.py:444
  388.6 69.4 %attention_backward.1 = (f32[5,1536,128]{2,1,0:T(8,128)}, bf16[5,4096,128]{2,1,0:T(8,128)(2,1)}) custom-call(s32[1]{0:T(128)} %bitcast.2.pair_ref, bf16[5,1536,128]{2,1,0:T(8,128)(2,1)S(1)} %pad.21.q_ref, bf16[5,1536,128]{2,1,0:T(8,128)(2,1)S(1)} %copy-done.2, bf16[5,1536,128]{2,1,0:T(8,128)(2,1)S(1)} %pad.23.extra_ref, ...), custom_call_target="tpu_custom_call" | custom-call | flops 10066329600 | bytes 20316160 | tf_op jit(solution)/shard_map/attention_backward/pallas_call | solution.py:211
  469.1 8.5 collective-permute-start.3
  477.7 19.0 %collective-permute-done.3 = bf16[256,960]{0,1:T(8,128)(2,1)S(1)} collective-permute-done((bf16[256,960]{0,1:T(8,128)(2,1)S(1)}, bf16[256,960]{0,1:T(8,128)(2,1)S(1)}, u32[]{:S(2)}, u32[]{:S(2)}) %collective-permute-start.3) | collective-permute-done | bytes 491552 | tf_op jit(solution)/shard_map/ppermute | solution.py:277
  513.2 31.9 %maximum_maximum_fusion = bf16[1920,1920]{1,0:T(8,128)(2,1)} fusion(bf16[960,640]{1,0:T(8,128)(2,1)S(1)} %convolution_convert_fusion.4, bf16[960,1280]{1,0:T(8,128)(2,1)S(1)} %convolution_convert_fusion, bf16[960,640]{1,0:T(8,128)(2,1)S(1)} %convolution_convert_fusion.5, bf16[960,1280]{1,0:T(8,128)(2,1)S(1)} %convolution_convert_fusion.1), kind=kLoop, calls=%fused_computation.1 | loop fusion | flops 29491200 | bytes 14745600 | tf_op jit(solution)/shard_map/concatenate | solution.py:485
  546.8 4.4 slice_multiply_fusion
  551.2 5.6 copy.180
  565.7 5.5 fusion.15
  576.0 9.2 reshape.308
  585.3 6.4 copy.193
  602.3 4.5 collective-permute-start.7
  606.9 10.1 collective-permute-done.7
  618.1 34.3 %reduce-scatter.11.cloned.1.call-done = bf16[1,240,120]{2,1,0:T(8,128)(2,1)} async-done(((bf16[32,240,120]{2,1,0:T(8,128)(2,1)}), bf16[1,240,120]{2,1,0:T(8,128)(2,1)}) %reduce-scatter.11.cloned.1.call-update) | async-done | bytes 57616 | tf_op jit(solution)/shard_map/reduce_scatter | solution.py:483
  653.8 32.1 %all-gather.18.cloned.1.call-done = bf16[8,256,960]{1,2,0:T(8,128)(2,1)} async-done(((bf16[2,256,960]{1,2,0:T(8,128)(2,1)}), bf16[8,256,960]{1,2,0:T(8,128)(2,1)}) %all-gather.18.cloned.1.call-update) | async-done | bytes 3932176 | tf_op jit(solution)/shard_map/all_gather | solution.py:331
  691.3 152.4 %reduce-scatter.13.cloned.1.call-done = bf16[120,1920]{1,0:T(8,128)(2,1)} async-done(((bf16[1920,1920]{1,0:T(8,128)(2,1)}), bf16[120,1920]{1,0:T(8,128)(2,1)}) %reduce-scatter.13.cloned.1.call-update) | async-done | bytes 460816
  846.5 143.9 %reduce-scatter.9.cloned.1.call-done = bf16[1,242,200]{1,2,0:T(8,128)(2,1)} async-done(((bf16[32,242,200]{1,2,0:T(8,128)(2,1)}), bf16[1,242,200]{1,2,0:T(8,128)(2,1)}) %reduce-scatter.9.cloned.1.call-update) | async-done | bytes 96816 | tf_op jit(solution)/shard_map/reduce_scatter | solution.py:479
  992.7 29.1 %all-gather.20.cloned.1.call-done = bf16[8,256,960]{1,2,0:T(8,128)(2,1)} async-done(((bf16[2,256,960]{1,2,0:T(8,128)(2,1)}), bf16[8,256,960]{1,2,0:T(8,128)(2,1)}) %all-gather.20.cloned.1.call-update) | async-done | bytes 3932176 | tf_op jit(solution)/shard_map/all_gather | solution.py:331
  1024.8 4.5 copy.202
  (250 shorter events, 170.8 us)
Async XLA Ops:
  7.2 71.0 %all-gather.22.cloned.1.call-start = ((), (), s32[]{:S(2)}) async-start(), calls=%async_computation.12 | async-start | bytes 3379200 | tf_op jit(solution)/shard_map/all_gather | solution.py:342
  9.6 135.5 %all-gather.16.cloned.1.call-start = ((), (), s32[]{:S(2)}) async-start(), calls=%async_computation.9 | async-start | bytes 2027520 | tf_op jit(solution)/shard_map/all_gather | solution.py:356
  10.4 191.8 %all-gather.12.cloned.1.call-start = ((), (), s32[]{:S(2)}) async-start(), calls=%async_computation.4 | async-start | bytes 5898240 | tf_op jit(solution)/shard_map/all_gather | solution.py:401
  12.1 67.8 %copy-start.10 = (bf16[256,960]{0,1:T(8,128)(2,1)}, bf16[256,960]{0,1:T(8,128)(2,1)S(1)}, u32[]{:S(2)}) copy-start(bf16[256,960]{0,1:T(8,128)(2,1)S(1)} %get-tuple-element.80) | copy-start | bytes 1474564
  12.2 17.2 %collective-permute-start = (bf16[256,960]{0,1:T(8,128)(2,1)S(1)}, bf16[256,960]{0,1:T(8,128)(2,1)S(1)}, u32[]{:S(2)}, u32[]{:S(2)}) collective-permute-start(bf16[256,960]{0,1:T(8,128)(2,1)S(1)} %get-tuple-element.79), channel_id=1, source_target_pairs={{0,12},{4,8},{8,4},{12,0},{1,13},{5,9},{9,5},{13,1},{2,14},{6,10},... | collective-permute-start | bytes 1474568 | tf_op jit(solution)/shard_map/ppermute | solution.py:277
  18.2 61.7 %copy-start.26 = (f32[512,32]{0,1:T(8,128)}, f32[512,32]{0,1:T(8,128)S(1)}, u32[]{:S(2)}) copy-start(f32[512,32]{0,1:T(8,128)S(1)} %get-tuple-element.105) | copy-start | bytes 196612
  18.2 61.7 %copy-start.33 = (f32[512,32]{0,1:T(8,128)}, f32[512,32]{0,1:T(8,128)S(1)}, u32[]{:S(2)}) copy-start(f32[512,32]{0,1:T(8,128)S(1)} %get-tuple-element.104) | copy-start | bytes 196612
  19.2 79.8 %copy-start.19 = (f32[512,32]{1,0:T(8,128)}, f32[512,32]{1,0:T(8,128)S(1)}, u32[]{:S(2)}) copy-start(f32[512,32]{1,0:T(8,128)S(1)} %copy.164) | copy-start | bytes 196612
  29.4 50.6 %copy-start.21 = (bf16[256,960]{0,1:T(8,128)(2,1)}, bf16[256,960]{0,1:T(8,128)(2,1)S(1)}, u32[]{:S(2)}) copy-start(bf16[256,960]{0,1:T(8,128)(2,1)S(1)} %collective-permute-done) | copy-start | bytes 1474564
  29.8 60.1 %copy-start.41 = (f32[512]{0:T(512)}, f32[512]{0:T(512)S(1)}, u32[]{:S(2)}) copy-start(f32[512]{0:T(512)S(1)} %add_rsqrt_fusion.1) | copy-start | bytes 6148
  89.8 4.5 copy-start.39
  101.8 205.8 %all-gather.14.cloned.1.call-start = ((), (), s32[]{:S(2)}) async-start(), calls=%async_computation.5 | async-start | bytes 7833600 | tf_op jit(solution)/shard_map/all_gather | solution.py:363
  102.7 459.2 %reduce-scatter.7.cloned.1.call-start = ((), (), s32[]{:S(2)}) async-start(), calls=%async_computation.6 | async-start | bytes 5898240 | tf_op jit(solution)/shard_map/reduce_scatter | solution.py:450
  105.5 173.8 %collective-permute-start.4 = (bf16[256,960]{0,1:T(8,128)(2,1)}, bf16[256,960]{0,1:T(8,128)(2,1)}, u32[]{:S(2)}, u32[]{:S(2)}) collective-permute-start(bf16[256,960]{0,1:T(8,128)(2,1)} %fusion.26), channel_id=1, source_target_pairs={{0,12},{4,8},{8,4},{12,0},{1,13},{5,9},{9,5},{13,1},{2,14},{6,10},... | collective-permute-start | bytes 1474568 | tf_op jit(solution)/shard_map/ppermute | solution.py:277
  268.4 4.1 copy-start.11
  277.6 30.1 %collective-permute-start.1 = (bf16[512,960]{0,1:T(8,128)(2,1)}, bf16[512,960]{0,1:T(8,128)(2,1)}, u32[]{:S(2)}, u32[]{:S(2)}) collective-permute-start(bf16[512,960]{0,1:T(8,128)(2,1)} %multiply_convert_fusion.6), channel_id=1, source_target_pairs={{0,1},{1,0},{2,3},{3,2},{4,5},{5,4},{6,7},{7,6},{8,9},{9,8},{10,11... | collective-permute-start | bytes 2949128 | tf_op jit(solution)/shard_map/ppermute | solution.py:284
  282.6 30.5 %collective-permute-start.5 = (bf16[512,960]{0,1:T(8,128)(2,1)}, bf16[512,960]{0,1:T(8,128)(2,1)}, u32[]{:S(2)}, u32[]{:S(2)}) collective-permute-start(bf16[512,960]{0,1:T(8,128)(2,1)} %fusion.20), channel_id=1, source_target_pairs={{0,1},{1,0},{2,3},{3,2},{4,5},{5,4},{6,7},{7,6},{8,9},{9,8},{10,11... | collective-permute-start | bytes 2949128 | tf_op jit(solution)/shard_map/ppermute | solution.py:284
  307.7 5.5 copy-start.35
  317.6 15.8 %copy-start.43 = (bf16[1024,640]{1,0:T(8,128)(2,1)}, bf16[1024,640]{1,0:T(8,128)(2,1)S(1)}, u32[]{:S(2)}) copy-start(bf16[1024,640]{1,0:T(8,128)(2,1)S(1)} %get-tuple-element.74) | copy-start | bytes 3932164
  329.3 5.8 copy-start.13
  333.3 7.4 collective-permute-start.6
  337.1 4.3 collective-permute-start.2
  458.0 194.4 %reduce-scatter.11.cloned.1.call-start = ((), (), s32[]{:S(2)}) async-start(), calls=%async_computation.8 | async-start | bytes 2027520 | tf_op jit(solution)/shard_map/reduce_scatter | solution.py:483
  467.9 218.1 %all-gather.18.cloned.1.call-start = ((), (), s32[]{:S(2)}) async-start(), calls=%async_computation.10 | async-start | bytes 4915200 | tf_op jit(solution)/shard_map/all_gather | solution.py:331
  469.1 28.7 %copy-start.14 = (bf16[1024,640]{1,0:T(8,128)(2,1)S(1)}, bf16[1024,640]{1,0:T(8,128)(2,1)}, u32[]{:S(2)}) copy-start(bf16[1024,640]{1,0:T(8,128)(2,1)} %copy-done.13) | copy-start | bytes 3932164
  469.1 27.5 %collective-permute-start.3 = (bf16[256,960]{0,1:T(8,128)(2,1)S(1)}, bf16[256,960]{0,1:T(8,128)(2,1)S(1)}, u32[]{:S(2)}, u32[]{:S(2)}) collective-permute-start(bf16[256,960]{0,1:T(8,128)(2,1)S(1)} %get-tuple-element.94), channel_id=1, source_target_pairs={{0,12},{4,8},{8,4},{12,0},{1,13},{5,9},{9,5},{13,1},{2,14},{6,10},... | collective-permute-start | bytes 1474568 | tf_op jit(solution)/shard_map/ppermute | solution.py:277
  497.8 345.9 %reduce-scatter.13.cloned.1.call-start = ((), (), s32[]{:S(2)}) async-start(), calls=%async_computation.13 | async-start | bytes 7833600
  504.6 4.4 copy-start.46
  504.6 4.4 copy-start.48
  545.2 445.2 %reduce-scatter.9.cloned.1.call-start = ((), (), s32[]{:S(2)}) async-start(), calls=%async_computation.7 | async-start | bytes 3379200 | tf_op jit(solution)/shard_map/reduce_scatter | solution.py:479
  598.4 423.4 %all-gather.20.cloned.1.call-start = ((), (), s32[]{:S(2)}) async-start(), calls=%async_computation.11 | async-start | bytes 4915200 | tf_op jit(solution)/shard_map/all_gather | solution.py:331
  602.3 14.6 %collective-permute-start.7 = (bf16[256,960]{0,1:T(8,128)(2,1)S(1)}, bf16[256,960]{0,1:T(8,128)(2,1)S(1)}, u32[]{:S(2)}, u32[]{:S(2)}) collective-permute-start(bf16[256,960]{0,1:T(8,128)(2,1)S(1)} %get-tuple-element.92), channel_id=1, source_target_pairs={{0,12},{4,8},{8,4},{12,0},{1,13},{5,9},{9,5},{13,1},{2,14},{6,10},... | collective-permute-start | bytes 1474568 | tf_op jit(solution)/shard_map/ppermute | solution.py:277
  (39 other events, 79.0 us)
Sparse Core Ops, SparseCore 0:
  11.4 66.7 all-gather.21
  81.1 64.0 all-gather.15
  147.3 54.8 all-gather.11
  204.8 102.8 all-gather.13
  458.1 85.1 reduce-scatter.6
  548.5 103.8 reduce-scatter.10
  653.9 31.9 all-gather.17
  692.1 151.5 reduce-scatter.12
  846.0 144.3 reduce-scatter.8
  991.8 29.9 all-gather.19

commit v2 on v1

v2 whole, which is shorter than its diff:
```python
import functools

import jax
import jax.numpy as jnp
from jax import lax
from jax.experimental import pallas as pl
from jax.experimental.pallas import tpu as pltpu
from jax.sharding import Mesh
from jax.sharding import PartitionSpec as P

HEADS = 15
KV_HEADS = 5
HEAD_DIM = 64
GROUP = 3
LANES = 128
HALF = HEAD_DIM


epsilon = 1e-05
rope_base = 100000.0
masked_score = -1e30


def pair_place(pair, ctx_count, sub):
    turn = pair // (2 * sub)
    spot = pair % (2 * sub)
    low = spot < sub
    return jnp.where(low, turn * sub + spot, (ctx_count - 1 - turn) * sub + 2 * sub - 1 - spot)


def dot_nt(a, b):
    return lax.dot_general(a, b, (((1,), (1,)), ((), ())), preferred_element_type=jnp.float32)


def dot_nn(a, b):
    return lax.dot_general(a, b, (((1,), (0,)), ((), ())), preferred_element_type=jnp.float32)


def dot_tn(a, b):
    return lax.dot_general(a, b, (((0,), (0,)), ((), ())), preferred_element_type=jnp.float32)


def causal(rows, cols, chunk, key_axis):
    shape = (rows, cols)
    query_axis = 1 - key_axis
    query = lax.broadcasted_iota(jnp.int32, shape, query_axis)
    key = lax.broadcasted_iota(jnp.int32, shape, key_axis)
    return key <= lax.rem(query, chunk)


def forward_kernel(ctx_count, sub, chunk, group, pair_ref, q_ref, kv_ref, out_ref, top, total):
    pairs = ctx_count * sub
    own = pair_ref[0]
    part = group * chunk
    lanes = lambda rows: lax.broadcasted_iota(jnp.int32, (rows, LANES), 1)

    def load(place, slot, count):
        return kv_ref[0, pl.ds(pl.multiple_of(place * 2 * chunk + slot * chunk, chunk), count * chunk), :]

    def weighted(powers, kv):
        ones = jnp.where(lanes(kv.shape[0]) < HALF, jnp.ones_like(kv), kv)
        return dot_nn(powers, ones)

    def update(start, rows, kv, first, mask):
        scores = dot_nt(q_ref[0, start : start + rows, :], kv)
        if mask is not None:
            scores = jnp.where(mask, scores, masked_score)
        best = jnp.max(scores, axis=1, keepdims=True)
        spot = slice(start, start + rows)
        if first:
            top[spot, :] = jnp.broadcast_to(best, (rows, LANES))
            powers = jnp.exp(scores - best).astype(jnp.bfloat16)
            total[spot, :] = weighted(powers, kv)
        else:
            old = top[spot, :]
            new = jnp.maximum(old, best)
            powers = jnp.exp(scores - new[:, :1]).astype(jnp.bfloat16)
            total[spot, :] = total[spot, :] * jnp.exp(old - new) + weighted(powers, kv)
            top[spot, :] = new

    place = pair_place(own, ctx_count, sub)
    near = load(place, 0, 1)
    both = load(place, 0, 2)
    near_mask = causal(chunk, chunk, chunk, 1)
    columns = lax.broadcasted_iota(jnp.int32, (chunk, 2 * chunk), 1)
    queries = lax.broadcasted_iota(jnp.int32, (chunk, 2 * chunk), 0)
    both_mask = columns <= queries + chunk
    for head in range(group):
        update(head * chunk, chunk, near, True, near_mask)
        update(part + head * chunk, chunk, both, True, both_mask)

    def sweep(first, last, count, start, heads):
        def load_at(pair):
            return load(pair_place(pair, ctx_count, sub), 0, count)

        def absorb(kv):
            for head in range(heads):
                update(start + head * chunk, chunk, kv, False, None)

        twos = (last - first) // 2

        @pl.loop(0, twos)
        def _(step):
            pair = first + 2 * step
            absorb(jnp.concatenate([load_at(pair), load_at(pair + 1)], axis=0))

        @pl.when(first + 2 * twos < last)
        def _():
            absorb(load_at(last - 1))

    sweep(0, own, 1, 0, 2 * group)
    sweep(own + 1, pairs, 2, part, group)

    for head in range(2 * group):
        spot = slice(head * chunk, (head + 1) * chunk)
        sums = total[spot, :]
        count = sums[:, :1]
        out_ref[0, spot, :] = jnp.where(
            lanes(chunk) < HALF, top[spot, :] + jnp.log(count), sums / count
        )


def attention_forward(own_pair, queries, pairs_all, base, ctx_count, sub, chunk, group):
    rows = queries.shape[1]
    heads, length, _ = pairs_all.shape
    grid_spec = pltpu.PrefetchScalarGridSpec(
        num_scalar_prefetch=1,
        grid=(heads,),
        in_specs=[
            pl.BlockSpec((1, rows, LANES), lambda h, p: (base + h, 0, 0)),
            pl.BlockSpec((1, length, LANES), lambda h, p: (h, 0, 0)),
        ],
        out_specs=pl.BlockSpec((1, rows, LANES), lambda h, p: (h, 0, 0)),
        scratch_shapes=[
            pltpu.VMEM((rows, LANES), jnp.float32),
            pltpu.VMEM((rows, LANES), jnp.float32),
        ],
    )
    cost = heads * rows * length // 2
    return pl.pallas_call(
        functools.partial(forward_kernel, ctx_count, sub, chunk, group),
        out_shape=jax.ShapeDtypeStruct((heads, rows, LANES), jnp.float32),
        grid_spec=grid_spec,
        compiler_params=pltpu.CompilerParams(vmem_limit_bytes=48 * 2**20),
        cost_estimate=pl.CostEstimate(
            flops=cost * 4 * HALF, bytes_accessed=heads * LANES * (rows * 6 + length * 2), transcendentals=cost
        ),
        name="attention_forward",
    )(own_pair, queries, pairs_all)


def backward_kernel(
    ctx_count, sub, chunk, group, pair_ref, q_ref, cot_ref, extra_ref, kv_ref, dq_ref, dkv_ref
):
    pairs = ctx_count * sub
    own = pair_ref[0]
    part = group * chunk

    def minus(rows, low, high):
        lane = lax.broadcasted_iota(jnp.int32, (rows, LANES), 1)
        return jnp.where((lane >= low) & (lane < high), -1.0, 0.0).astype(jnp.bfloat16)

    def load(place, slot, count):
        base = pl.multiple_of(place * 2 * chunk + slot * chunk, chunk)
        return kv_ref[0, pl.ds(base, count * chunk), :]

    def step(start, rows, kv, first, mask):
        keys = kv.shape[0]
        key_side = jnp.concatenate([kv, minus(keys, 0, 3)], axis=1)
        value_side = jnp.concatenate([kv, minus(keys, 3, 6)], axis=1)
        pair_sum = None
        for at in range(start, start + rows, chunk):
            spot = slice(at, at + chunk)
            query = q_ref[0, spot, :]
            cot = cot_ref[0, spot, :]
            extra = extra_ref[0, spot, :]
            powers = jnp.exp(dot_nt(key_side, jnp.concatenate([query, extra], axis=1)))
            if mask is not None:
                powers = jnp.where(mask, powers, 0.0)
            slope = dot_nt(value_side, jnp.concatenate([cot, extra], axis=1))
            grads = (powers * slope).astype(jnp.bfloat16)
            powers = powers.astype(jnp.bfloat16)
            term = dot_nn(powers, cot) + dot_nn(grads, query)
            pair_sum = term if pair_sum is None else pair_sum + term
            moved = dot_tn(grads, kv)
            if first:
                dq_ref[0, spot, :] = moved
            else:
                dq_ref[0, spot, :] += moved
        return pair_sum

    def store(place, slot, count, value):
        base = pl.multiple_of(place * 2 * chunk + slot * chunk, chunk)
        dkv_ref[0, pl.ds(base, count * chunk), :] = value.astype(jnp.bfloat16)

    place = pair_place(own, ctx_count, sub)
    near_mask = causal(chunk, chunk, chunk, 0)
    keys = lax.broadcasted_iota(jnp.int32, (2 * chunk, chunk), 0)
    queries = lax.broadcasted_iota(jnp.int32, (2 * chunk, chunk), 1)
    far = step(part, part, load(place, 0, 2), True, keys <= queries + chunk)
    near = step(0, part, load(place, 0, 1), True, near_mask)
    store(place, 0, 1, far[:chunk] + near)
    store(place, 1, 1, far[chunk:])

    def sweep(first, last, count, start, rows):
        twos = (last - first) // 2

        def put(at, value):
            store(at, 0, count, value)
            if count == 1:
                store(at, 1, 1, jnp.zeros((chunk, LANES), jnp.float32))

        @pl.loop(0, twos)
        def _(turn):
            one = pair_place(first + 2 * turn, ctx_count, sub)
            two = pair_place(first + 2 * turn + 1, ctx_count, sub)
            kv = jnp.concatenate([load(one, 0, count), load(two, 0, count)], axis=0)
            sums = step(start, rows, kv, False, None)
            put(one, sums[: count * chunk])
            put(two, sums[count * chunk :])

        @pl.when(first + 2 * twos < last)
        def _():
            at = pair_place(last - 1, ctx_count, sub)
            put(at, step(start, rows, load(at, 0, count), False, None))

    sweep(0, own, 1, 0, 2 * part)
    sweep(own + 1, pairs, 2, part, part)


def attention_backward(own_pair, queries, cots, extra, pairs_all, base, filled, ctx_count, sub, chunk, group):
    total_heads, rows, _ = queries.shape
    heads, length, _ = pairs_all.shape
    row_spec = pl.BlockSpec((1, rows, LANES), lambda h, p: (base + h, 0, 0))
    long_spec = pl.BlockSpec((1, length, LANES), lambda h, p: (base + h, 0, 0))
    part_spec = pl.BlockSpec((1, length, LANES), lambda h, p: (h, 0, 0))
    cost = heads * rows * length // 2
    kernel = functools.partial(backward_kernel, ctx_count, sub, chunk, group)

    def filling(pair_ref, q_ref, cot_ref, extra_ref, kv_ref, old_dq_ref, old_dkv_ref, dq_ref, dkv_ref):
        kernel(pair_ref, q_ref, cot_ref, extra_ref, kv_ref, dq_ref, dkv_ref)

    return pl.pallas_call(
        filling if filled else kernel,
        out_shape=(
            jax.ShapeDtypeStruct((total_heads, rows, LANES), jnp.float32),
            jax.ShapeDtypeStruct((total_heads, length, LANES), jnp.bfloat16),
        ),
        grid_spec=pltpu.PrefetchScalarGridSpec(
            num_scalar_prefetch=1,
            grid=(heads,),
            in_specs=[row_spec, row_spec, row_spec, part_spec]
            + [pl.BlockSpec(memory_space=pl.ANY)] * len(filled),
            out_specs=(row_spec, long_spec),
        ),
        input_output_aliases={5 + at: at for at in range(len(filled))},
        compiler_params=pltpu.CompilerParams(vmem_limit_bytes=48 * 2**20),
        cost_estimate=pl.CostEstimate(
            flops=cost * 10 * HALF, bytes_accessed=heads * LANES * (rows * 10 + length * 4), transcendentals=cost
        ),
        name="attention_backward",
    )(own_pair, queries, cots, extra, pairs_all, *filled)


def three_parts(values):
    high = values.astype(jnp.bfloat16)
    rest = values - high.astype(jnp.float32)
    middle = rest.astype(jnp.bfloat16)
    low = (rest - middle.astype(jnp.float32)).astype(jnp.bfloat16)
    return [high, middle, low]


def lane_index(rows):
    return lax.broadcasted_iota(jnp.int32, (rows, LANES), 1)


def swap_halves(tile):
    lane = lane_index(tile.shape[0])
    quarter = HALF // 2
    return jnp.where(
        lax.rem(lane, HALF) < quarter,
        pltpu.roll(tile, LANES - quarter, 1),
        pltpu.roll(tile, quarter, 1),
    )


def normalise(values):
    inv_rms = lax.rsqrt(jnp.mean(values * values, axis=-1, keepdims=True) + epsilon)
    return values * inv_rms, inv_rms


def norm_back(upstream, values, gain_row):
    unit_rows, inv_rms = normalise(values)
    shaped = upstream * gain_row
    inner_mean = jnp.mean(shaped * unit_rows, axis=-1, keepdims=True)
    return inv_rms * (shaped - unit_rows * inner_mean), upstream * unit_rows


def assemble_kernel(rows, in_ref, out_ref):
    tiles = [in_ref[at, :rows, :] for at in range(in_ref.shape[0])]
    used = len(tiles) * tiles[0].shape[1]
    if used < out_ref.shape[1]:
        tiles.append(jnp.zeros((rows, out_ref.shape[1] - used), tiles[0].dtype))
    out_ref[...] = jnp.concatenate(tiles, axis=1)


def assemble(gathered, teams, rows, cols):
    count = gathered.shape[0] // teams
    return pl.pallas_call(
        functools.partial(assemble_kernel, rows),
        grid=(teams,),
        in_specs=[pl.BlockSpec((count,) + gathered.shape[1:], lambda t: (t, 0, 0))],
        out_specs=pl.BlockSpec((rows, cols), lambda t: (t, 0)),
        out_shape=jax.ShapeDtypeStruct((teams * rows, cols), gathered.dtype),
        compiler_params=pltpu.CompilerParams(vmem_limit_bytes=48 * 2**20),
        name="assemble",
    )(gathered)


def project_kernel(token_ref, gain_ref, weight_ref, cos_ref, sin_ref, q_ref, kv_ref, normed_ref):
    rows = token_ref.shape[0]
    unit_rows, _ = normalise(token_ref[...].astype(jnp.float32))
    normed = (unit_rows * gain_ref[...]).astype(jnp.bfloat16)
    normed_ref[...] = normed
    projected = dot_nn(normed, weight_ref[...])
    cos, sin = cos_ref[...], sin_ref[...]
    low = lane_index(rows) < HALF

    def tile(column):
        return projected[:, column // 2 * LANES : (column // 2 + 1) * LANES]

    def turned(column):
        raw = tile(column)
        out = raw * cos + swap_halves(raw) * sin
        return pltpu.roll(out, HALF, 1) if column % 2 else out

    for head in range(HEADS):
        query = jnp.where(low, turned(head) * HEAD_DIM ** (-0.5), 0.0)
        q_ref[head // GROUP, 0, head % GROUP] = query.astype(jnp.bfloat16)
    for head in range(KV_HEADS):
        key = turned(HEADS + head)
        column = HEADS + KV_HEADS + head
        value = tile(column) if column % 2 else pltpu.roll(tile(column), HALF, 1)
        kv_ref[head] = jnp.where(low, key, value).astype(jnp.bfloat16)


def whole(shape):
    return pl.BlockSpec(shape, lambda c: (0,) * len(shape))


def row_call(kernel, chunk, ins, outs, name, flops):
    def spec(array):
        shape = array.shape
        if len(shape) == 5:
            return pl.BlockSpec((shape[0], 1) + shape[2:], lambda c: (0, c, 0, 0, 0))
        if len(shape) == 3:
            return pl.BlockSpec((shape[0], chunk, shape[2]), lambda c: (0, c, 0))
        if shape[0] != 2 * chunk:
            return pl.BlockSpec((shape[0], chunk), lambda c: (0, c))
        return pl.BlockSpec((chunk, shape[1]), lambda c: (c, 0))

    moved = sum(a.size * a.dtype.itemsize for a, _ in ins) + sum(o.size * o.dtype.itemsize for o, _ in outs)
    return pl.pallas_call(
        kernel,
        grid=(2,),
        in_specs=[whole(a.shape) if fixed else spec(a) for a, fixed in ins],
        out_specs=[whole(o.shape) if fixed else spec(o) for o, fixed in outs],
        out_shape=[o for o, _ in outs],
        compiler_params=pltpu.CompilerParams(vmem_limit_bytes=56 * 2**20),
        cost_estimate=pl.CostEstimate(flops=flops, bytes_accessed=moved, transcendentals=0),
        name=name,
    )(*[a for a, _ in ins])


def pick(refs, head):
    group, at = head // GROUP, 0
    for ref in refs:
        if group < at + ref.shape[0]:
            return ref[group - at, 0, head % GROUP]
        at += ref.shape[0]


def pick_pair(refs, group):
    at = 0
    for ref in refs:
        if group < at + ref.shape[0]:
            return ref[group - at]
        at += ref.shape[0]


def mix_kernel(count, *refs):
    attended_refs = refs[:count]
    weight_ref, token_ref, gain_ref, hidden_ref, normed_ref, attn_ref = refs[count:]
    total = token_ref[...].astype(jnp.float32)
    first = lane_index(token_ref.shape[0]) < HALF
    for head in range(HEADS):
        rows = pick(attended_refs, head)
        total = total + dot_nn(rows.astype(jnp.bfloat16), weight_ref[head])
        base = head // 2 * LANES
        if head % 2:
            both = jnp.where(first, pltpu.roll(before, HALF, 1), rows)
            attn_ref[:, base : base + LANES] = both.astype(jnp.bfloat16)
        elif head == HEADS - 1:
            alone = pltpu.roll(rows, HALF, 1)[:, :HALF]
            attn_ref[:, base : base + HALF] = alone.astype(jnp.bfloat16)
        before = rows
    hidden_ref[...] = total
    unit_rows, _ = normalise(total)
    normed_ref[:, : total.shape[1]] = (unit_rows * gain_ref[...]).astype(jnp.bfloat16)


def accumulate(ref, rows):
    summed = jnp.broadcast_to(jnp.sum(rows, axis=0, keepdims=True), ref.shape)

    @pl.when(pl.program_id(0) == 0)
    def _():
        ref[...] = summed

    @pl.when(pl.program_id(0) != 0)
    def _():
        ref[...] += summed


def unmix_kernel(count, parts, *refs):
    ups = refs[:count]
    attended_refs, refs = refs[count : count + parts], refs[count + parts :]
    (hidden_ref, cot_ref, gain_ref, weight_ref, grad_ref, low_ref, heads_ref, extra_ref, gain_grad_ref) = refs
    width = hidden_ref.shape[1]
    upstream = ups[0][:, :width].astype(jnp.float32)
    for ref in ups[1:]:
        upstream = upstream + ref[:, :width].astype(jnp.float32)
    back, gain_rows = norm_back(upstream, hidden_ref[...], gain_ref[...])
    accumulate(gain_grad_ref, gain_rows)
    hidden_grad = cot_ref[...] + back
    grad_ref[...] = hidden_grad
    hidden_low = hidden_grad.astype(jnp.bfloat16)
    low_ref[...] = hidden_low
    lane = lane_index(hidden_low.shape[0])
    for head in range(HEADS):
        spot = (head // GROUP, 0, head % GROUP)
        cots = dot_nt(hidden_low, weight_ref[head]).astype(jnp.bfloat16)
        heads_ref[spot] = cots
        attended = pick(attended_refs, head)
        delta = jnp.sum(cots.astype(jnp.float32) * attended, axis=1, keepdims=True)
        base = jnp.where(lane < 3, attended[:, :1], jnp.where(lane < 6, delta, 0.0))
        high, middle, low = three_parts(base)
        part = lax.rem(lane, 3)
        extra_ref[spot] = jnp.where(
            part == 0,
            high.astype(jnp.float32),
            jnp.where(part == 1, middle.astype(jnp.float32), low.astype(jnp.float32)),
        ).astype(jnp.bfloat16)


def turn_back(dq_ref, dkv_ref, cos_ref, sin_ref, proj_ref):
    rows = cos_ref.shape[0]
    cos, sin = cos_ref[...], sin_ref[...]
    low = lane_index(rows) < HALF

    def half(column):
        if column < HEADS:
            return dq_ref[column // GROUP, 0, column % GROUP] * HEAD_DIM ** (-0.5), 0
        if column < HEADS + KV_HEADS:
            return dkv_ref[column - HEADS].astype(jnp.float32), 0
        if column < HEADS + 2 * KV_HEADS:
            return dkv_ref[column - HEADS - KV_HEADS].astype(jnp.float32), 1
        return jnp.zeros((rows, LANES), jnp.float32), 0

    def placed(column):
        value, side = half(column)
        return value if side == column % 2 else pltpu.roll(value, HALF, 1)

    for at in range(proj_ref.shape[1] // LANES):
        raw = jnp.where(low, placed(2 * at), placed(2 * at + 1))
        if 2 * at < HEADS + KV_HEADS:
            raw = raw * cos - swap_halves(raw) * sin
        proj_ref[:, at * LANES : (at + 1) * LANES] = raw.astype(jnp.bfloat16)


def early_kernel(dq_ref, cos_ref, sin_ref, proj_ref):
    turn_back(dq_ref, None, cos_ref, sin_ref, proj_ref)


def block_kernel(count, *refs):
    hidden_ref, out_ref = refs[count], refs[count + 1]
    rows = hidden_ref[...]
    for ref in refs[:count]:
        rows = rows + ref[:, : rows.shape[1]].astype(jnp.float32)
    out_ref[...] = jnp.transpose(rows).astype(jnp.bfloat16)


def finish_kernel(
    dq_ref, dkv_ref, cos_ref, sin_ref, weight_ref, token_ref, grad_ref, gain_ref,
    proj_ref, input_ref, gain_grad_ref,
):
    turn_back(dq_ref, dkv_ref, cos_ref, sin_ref, proj_ref)
    upstream = dot_nt(proj_ref[...], weight_ref[...])
    back, gain_rows = norm_back(upstream, token_ref[...].astype(jnp.float32), gain_ref[...])
    accumulate(gain_grad_ref, gain_rows)
    input_ref[...] = jnp.transpose(grad_ref[...] + back).astype(jnp.bfloat16)


def feed_kernel(rows_ref, cot_ref, weight_ref, back_ref, feed_ref, inner_ref, grad_ref):
    part = inner_ref.shape[1]
    width = weight_ref.shape[0]
    rows, cots = rows_ref[:, :width], cot_ref[:, :width]
    gate_up, down = weight_ref[:, : 2 * part], weight_ref[:, 2 * part :]
    both = dot_nn(rows, gate_up)
    inner_grad = dot_nn(cots, down)
    gate_value, up_value = both[:, :part], both[:, part:]
    gate_sigmoid = jax.nn.sigmoid(gate_value)
    swish = gate_value * gate_sigmoid
    inner = (swish * up_value).astype(jnp.bfloat16)
    inner_ref[...] = inner
    gate_grad = inner_grad * up_value * (gate_sigmoid * (1.0 + gate_value * (1.0 - gate_sigmoid)))
    grad_ref[:, :part] = gate_grad.astype(jnp.bfloat16)
    grad_ref[:, part:] = (inner_grad * swish).astype(jnp.bfloat16)
    back_ref[:, :width] = dot_nt(grad_ref[...], gate_up).astype(back_ref.dtype)
    feed_ref[:, :width] = dot_nt(inner, down).astype(feed_ref.dtype)


def weight_grad_kernel(count, *refs):
    rows, cots = refs[:count], refs[count : 2 * count]
    inners, grads = refs[2 * count : 3 * count], refs[3 * count : 4 * count]
    out_ref = refs[4 * count]
    width = out_ref.shape[0]
    step = pl.program_id(0)

    @pl.when(step < 2)
    def _():
        out_ref[...] = sum(dot_tn(a[:, :width], b[...]) for a, b in zip(rows, grads)).astype(jnp.bfloat16)

    @pl.when(step == 2)
    def _():
        out_ref[...] = sum(dot_tn(a[:, :width], b[...]) for a, b in zip(cots, inners)).astype(jnp.bfloat16)


def weight_grads(width, rows, cots, inners, grads):
    count, size, part = len(rows), rows[0].shape[0], inners[0].shape[1]
    once = [pl.BlockSpec((size, rows[0].shape[1]), lambda j: (0, 0))] * (2 * count)
    once += [pl.BlockSpec((size, part), lambda j: (0, 0))] * count
    turns = [pl.BlockSpec((size, part), lambda j: (0, jnp.minimum(j, 1)))] * count
    return pl.pallas_call(
        functools.partial(weight_grad_kernel, count),
        grid=(3,),
        in_specs=once + turns,
        out_specs=pl.BlockSpec((width, part), lambda j: (0, j)),
        out_shape=jax.ShapeDtypeStruct((width, 3 * part), jnp.bfloat16),
        compiler_params=pltpu.CompilerParams(vmem_limit_bytes=56 * 2**20),
        cost_estimate=pl.CostEstimate(
            flops=6 * count * size * width * part,
            bytes_accessed=count * size * (4 * width + 6 * part) + 6 * width * part,
            transcendentals=0,
        ),
        name="weight_grads",
    )(*rows, *cots, *inners, *grads)


def matmul(spec, left, right):
    return jnp.einsum(spec, left, right, preferred_element_type=jnp.float32)


def pull(values, axis, ahead):
    count = lax.axis_size(axis)
    return lax.ppermute(values, axis, [((i + ahead) % count, i) for i in range(count)])


def swap_ends(values):
    count = lax.axis_size("ctx")
    return lax.ppermute(values, "ctx", [(i, count - 1 - i) for i in range(count)])


def spread(values, axis):
    return [values] + [pull(values, axis, ahead) for ahead in range(1, lax.axis_size(axis))]


def gather(values, axis):
    count = lax.axis_size(axis)
    ahead = jnp.stack(spread(values, axis))
    return lax.dynamic_slice_in_dim(
        jnp.concatenate([ahead, ahead]), count - lax.axis_index(axis), count, 0
    )


def collect(parts, axis):
    received = [parts[0]]
    for ahead in range(1, len(parts)):
        received.append(pull(parts[ahead].astype(jnp.bfloat16), axis, len(parts) - ahead))
    return received


def total(parts):
    return sum(part.astype(jnp.float32) for part in parts)


def reduce_blocks(values, axis, dim):
    count = lax.axis_size(axis)
    at = lax.axis_index(axis)
    blocks = [
        lax.dynamic_index_in_dim(values, (at + ahead) % count, dim, keepdims=False)
        for ahead in range(count)
    ]
    return total(collect(blocks, axis)).astype(jnp.bfloat16)


def reduce_to(values, axis, base):
    count, at = lax.axis_size(axis), lax.axis_index(axis)
    size = values.shape[0]
    summed = 0.0
    for ahead in range(count):
        target = jnp.clip((at + ahead) % count - base, 0, size - 1)
        block = lax.dynamic_index_in_dim(values, target, 0, keepdims=False)
        if ahead:
            ways = [(i, (i + ahead) % count) for i in range(count)]
            block = lax.ppermute(block, axis, [w for w in ways if base <= w[1] < base + size])
        summed = summed + block.astype(jnp.float32)
    return summed.astype(jnp.bfloat16)


def place_kernel(seq_ref, chunk_ref, in_ref, out_ref):
    out_ref[...] = in_ref[...].astype(out_ref.dtype)


def place_rows(stacked, seqs, chunks, seq_count, chunk_count, kind):
    pieces, width, chunk = stacked.shape
    return pl.pallas_call(
        place_kernel,
        out_shape=jax.ShapeDtypeStruct((seq_count, width, chunk_count * chunk), kind),
        grid_spec=pltpu.PrefetchScalarGridSpec(
            num_scalar_prefetch=2,
            grid=(pieces,),
            in_specs=[pl.BlockSpec((1, width, chunk), lambda i, s, c: (i, 0, 0))],
            out_specs=pl.BlockSpec((1, width, chunk), lambda i, s, c: (s[i], 0, c[i])),
        ),
        name="place_rows",
    )(seqs, chunks, stacked)


def shards(tokens, gains, qkv_weight, out_weight, gate_weight, up_weight, down_weight, cotangent):
    seq_count, span_len, width = tokens.shape
    ctx_count, sub_count = lax.axis_size("ctx"), lax.axis_size("sub")
    pair_count = ctx_count * sub_count
    chunk = span_len // (2 * sub_count)
    row_count = 2 * chunk
    owners = lax.axis_size(("shard", "ctx"))
    tensor_count = lax.axis_size(("seq", "sub"))
    everyone = ("seq", "sub", "shard", "ctx")
    own_seq, own_sub, own_ctx = lax.axis_index("seq"), lax.axis_index("sub"), lax.axis_index("ctx")
    is_low = own_ctx < ctx_count // 2
    own_pair = jnp.where(
        is_low,
        2 * sub_count * own_ctx + own_sub,
        2 * pair_count - 1 - 2 * sub_count * own_ctx - own_sub,
    ).astype(jnp.int32)

    def take_rows(values):
        span = lax.dynamic_index_in_dim(values, own_seq, 0, keepdims=False)
        kept = lax.dynamic_slice_in_dim(span, own_sub * chunk, chunk, 0)
        moved = lax.dynamic_slice_in_dim(span, (2 * sub_count - 1 - own_sub) * chunk, chunk, 0)
        return kept, moved

    def in_order(kept, moved):
        return jnp.where(is_low, jnp.concatenate([kept, moved]), jnp.concatenate([moved, kept]))

    def owner_sums(grad, cols, base):
        count = grad.shape[1] // cols
        grad = jnp.transpose(grad.reshape(grad.shape[0], count, cols), (1, 0, 2))
        grad = grad.reshape(count // ctx_count, ctx_count, -1, cols)
        here = reduce_blocks(grad, "shard", 0) if base is None else reduce_to(grad, "shard", base)
        return reduce_blocks(here, "ctx", 0)

    def deliver(home, kind):
        stacked = jnp.concatenate(
            [part for seq_rows in spread(home, "seq") for part in spread(seq_rows, "sub")]
        )
        seqs, chunks = [], []
        for seq_ahead in range(seq_count):
            for sub_ahead in range(sub_count):
                sub = (own_sub + sub_ahead) % sub_count
                seqs += [(own_seq + seq_ahead) % seq_count] * 2
                chunks += [sub, 2 * sub_count - 1 - sub]
        placed = place_rows(
            stacked,
            jnp.stack(seqs).astype(jnp.int32),
            jnp.stack(chunks).astype(jnp.int32),
            seq_count,
            2 * sub_count,
            kind,
        )
        return jnp.transpose(placed, (0, 2, 1))

    def back_home(columns):
        low, high = columns[:, :chunk], columns[:, chunk:]
        kept = jnp.where(is_low, low, high)
        moved = swap_ends(jnp.where(is_low, high, low))
        return jnp.stack([kept, moved])

    tile_rows, tile_cols = qkv_weight.shape
    gain_part = gains.shape[1]
    first_tile = jnp.concatenate(
        [qkv_weight, jnp.pad(gains, ((0, 0), (0, tile_cols - gain_part)))], axis=0
    )
    first_all = lax.all_gather(first_tile, everyone, axis=0, tiled=False)
    qkv_cols = owners * tile_cols
    padded_cols = -(-qkv_cols // LANES) * LANES
    qkv_all = assemble(first_all, tensor_count, tile_rows, padded_cols)
    gain_all = (
        jnp.transpose(first_all[:owners, tile_rows:, :gain_part], (1, 0, 2))
        .reshape(2, 1, width)
        .astype(jnp.float32)
    )
    gain_one, gain_two = gain_all[0], gain_all[1]
    out_rows, out_cols = out_weight.shape
    out_tiles = gather(gather(gather(gather(out_weight, "ctx"), "shard"), "seq"), "sub")
    out_heads = jnp.pad(
        jnp.transpose(out_tiles, (1, 0, 4, 2, 3, 5)).reshape(HEADS, HEAD_DIM, width),
        ((0, 0), (HEAD_DIM, 0), (0, 0)),
    )

    qkv_all, out_heads = lax.optimization_barrier((qkv_all, out_heads))

    kept_tokens, moved_tokens = take_rows(tokens)
    kept_cot, moved_cot = take_rows(cotangent)
    rows_low = in_order(kept_tokens, swap_ends(moved_tokens))
    wide = -(-width // LANES) * LANES
    step = jnp.arange(chunk, dtype=jnp.int32)
    positions = jnp.concatenate([own_pair * chunk + step, (2 * pair_count - 1 - own_pair) * chunk + step])
    half_dim = HEAD_DIM // 2
    frequency = rope_base ** (-2.0 * jnp.arange(half_dim, dtype=jnp.float32) / HEAD_DIM)
    angles = positions.astype(jnp.float32)[:, None] * frequency[None, :]
    cosine, sine = jnp.cos(angles), jnp.sin(angles)
    cosine_table = jnp.concatenate([cosine] * 4, axis=1)
    sine_table = jnp.concatenate([-sine, sine] * 2, axis=1)

    def shape(*dims, kind=jnp.bfloat16):
        return jax.ShapeDtypeStruct(dims, kind)

    head_rows = (KV_HEADS, 2, GROUP, chunk, LANES)
    qkv_flops = 2 * row_count * width * padded_cols
    query_heads, pair_own, normed = row_call(
        project_kernel,
        chunk,
        [(rows_low, 0), (gain_one, 1), (qkv_all, 1), (cosine_table, 0), (sine_table, 0)],
        [(shape(*head_rows), 0), (shape(KV_HEADS, row_count, LANES), 0), (shape(row_count, width), 0)],
        "project",
        qkv_flops,
    )
    query_heads = query_heads.reshape(KV_HEADS, GROUP * row_count, LANES)
    cuts = [slice(0, 3), slice(3, KV_HEADS)]
    pairs = []
    for cut in cuts:
        own_part = pair_own[cut]
        if pairs:
            own_part, pairs[-1] = lax.optimization_barrier((own_part, pairs[-1]))
        pairs.append(lax.all_gather(own_part, ("ctx", "sub"), axis=1, tiled=True))
    hidden_part = gate_weight.shape[1]
    place = own_pair[None]
    first = attention_forward(place, query_heads, pairs[0], 0, ctx_count, sub_count, chunk, GROUP)
    ffn_tile = jnp.concatenate([gate_weight, up_weight, down_weight.T], axis=1)
    first, pairs[1], ffn_tile, moved_low = lax.optimization_barrier(
        (first, pairs[1], ffn_tile, moved_cot.astype(jnp.bfloat16))
    )
    swapped_cot = swap_ends(moved_low)
    ffn_all = lax.all_gather(ffn_tile, ("shard", "ctx"), axis=0, tiled=True)
    second = attention_forward(
        place, query_heads, pairs[1], cuts[1].start, ctx_count, sub_count, chunk, GROUP
    )
    second, swapped_cot = lax.optimization_barrier((second, swapped_cot))
    attended = [rows.reshape((-1,) + head_rows[1:]) for rows in (first, second)]
    cot = in_order(kept_cot, swapped_cot.astype(jnp.float32))
    far_cots = spread(jnp.pad(cot.astype(jnp.bfloat16), ((0, 0), (0, wide - width))), "seq")
    cot_low = [spread(seq_rows, "sub") for seq_rows in far_cots]
    mix_flops = 4 * row_count * width * width
    hidden, normed_own, attn_low = row_call(
        functools.partial(mix_kernel, len(attended)),
        chunk,
        [(rows, 0) for rows in attended]
        + [(out_heads, 1), (rows_low, 0), (gain_two, 1)],
        [
            (shape(row_count, width, kind=jnp.float32), 0),
            (shape(row_count, wide), 0),
            (shape(row_count, width), 0),
        ],
        "mix",
        mix_flops,
    )
    far_rows = spread(normed_own, "seq")
    feeds, backs, pieces = [], [], []
    for seq_ahead, near_rows in enumerate(far_rows):
        if seq_ahead:
            near_rows, backs[-1] = lax.optimization_barrier((near_rows, backs[-1]))
        seq_feeds, seq_backs = [], []
        for sub_ahead, rows in enumerate(spread(near_rows, "sub")):
            kind = jnp.bfloat16 if sub_ahead else jnp.float32
            cots = cot_low[seq_ahead][sub_ahead]
            back, feed, inner, grad = row_call(
                feed_kernel,
                chunk,
                [(rows, 0), (cots, 0), (ffn_all, 1)],
                [
                    (shape(row_count, wide, kind=kind), 0),
                    (shape(row_count, wide, kind=kind), 0),
                    (shape(row_count, hidden_part), 0),
                    (shape(row_count, 2 * hidden_part), 0),
                ],
                "feed",
                8 * row_count * width * 2 * hidden_part,
            )
            seq_feeds.append(feed)
            seq_backs.append(back)
            pieces.append((rows, cots, inner, grad))
        backs.append(collect(seq_backs, "sub"))
        feeds.append(collect(seq_feeds, "sub"))
    backs = backs[0] + collect([backs[0]] + [total(parts) for parts in backs[1:]], "seq")[1:]
    feed_sent = [total(parts).astype(jnp.bfloat16) for parts in feeds[1:]]
    ffn_grad = weight_grads(width, *zip(*pieces))
    backs, ffn_grad = lax.optimization_barrier((backs, ffn_grad))
    ffn_out = lax.psum_scatter(ffn_grad, ("shard", "ctx"), scatter_dimension=0, tiled=True)
    hidden_grad, hidden_low, grad_heads, extra, gain_two_grad = row_call(
        functools.partial(unmix_kernel, len(backs), len(attended)),
        chunk,
        [(part, 0) for part in backs + attended]
        + [(hidden, 0), (cot, 0), (gain_two, 1), (out_heads, 1)],
        [
            (shape(row_count, width, kind=jnp.float32), 0),
            (shape(row_count, width), 0),
            (shape(*head_rows), 0),
            (shape(*head_rows), 0),
            (shape(8, width, kind=jnp.float32), 1),
        ],
        "unmix",
        mix_flops,
    )
    flat = (KV_HEADS, GROUP * row_count, LANES)
    grad_heads, extra = grad_heads.reshape(flat), extra.reshape(flat)
    grad_heads, feed_sent = lax.optimization_barrier((grad_heads, feed_sent))
    feeds = feeds[0] + collect([feeds[0]] + feed_sent, "seq")[1:]
    filled = attention_backward(
        place, query_heads, grad_heads, extra, pairs[0], 0, (), ctx_count, sub_count, chunk, GROUP
    )
    filled, feeds = lax.optimization_barrier((filled, feeds))
    (block_low,) = row_call(
        functools.partial(block_kernel, len(feeds)),
        chunk,
        [(part, 0) for part in feeds] + [(hidden, 0)],
        [(shape(width, row_count), 0)],
        "block",
        0,
    )
    block_low, filled = lax.optimization_barrier((block_low, filled))
    block_home = back_home(block_low)
    query_grad, pair_grad = attention_backward(
        place,
        query_heads,
        grad_heads,
        extra,
        pairs[1],
        cuts[1].start,
        filled,
        ctx_count,
        sub_count,
        chunk,
        GROUP,
    )
    block_home, query_grad, pair_grad, hidden_low, ffn_out = lax.optimization_barrier(
        (block_home, query_grad, pair_grad, hidden_low, ffn_out)
    )
    pair_grad = lax.psum_scatter(pair_grad, ("ctx", "sub"), scatter_dimension=1, tiled=True)
    query_grad = query_grad.reshape(head_rows)
    half_cols, extra_rows = qkv_cols // 2, 16
    (proj_early,) = row_call(
        early_kernel,
        chunk,
        [(query_grad, 0), (cosine_table, 0), (sine_table, 0)],
        [(shape(row_count, -(-half_cols // LANES) * LANES), 0)],
        "early",
        0,
    )
    early_grad = jnp.concatenate(
        [
            matmul("rf,re->fe", attn_low, hidden_low).astype(jnp.bfloat16),
            matmul("rd,re->de", normed, proj_early).astype(jnp.bfloat16),
        ],
        axis=1,
    )
    early_grad = early_grad.reshape(seq_count, sub_count, tile_rows, early_grad.shape[1])
    early_grad = reduce_blocks(reduce_blocks(early_grad, "sub", 1), "seq", 0)
    out_out = owner_sums(early_grad[:, :width], out_cols, None)
    qkv_early = owner_sums(early_grad[:, width : width + half_cols], tile_cols, 0)
    block_out = deliver(block_home, jnp.bfloat16)
    pair_grad, out_out, qkv_early, block_out = lax.optimization_barrier(
        (pair_grad, out_out, qkv_early, block_out)
    )
    out_out = out_out.astype(jnp.float32)
    proj_grad, input_low, gain_one_grad = row_call(
        finish_kernel,
        chunk,
        [
            (query_grad, 0),
            (pair_grad, 0),
            (cosine_table, 0),
            (sine_table, 0),
            (qkv_all, 1),
            (rows_low, 0),
            (hidden_grad, 0),
            (gain_one, 1),
        ],
        [
            (shape(row_count, padded_cols), 0),
            (shape(width, row_count), 0),
            (shape(8, width, kind=jnp.float32), 1),
        ],
        "finish",
        qkv_flops,
    )
    input_grad = deliver(back_home(input_low), jnp.float32)

    late_cols = qkv_cols - half_cols
    qkv_grad = matmul("rd,re->de", normed, proj_grad[:, half_cols:qkv_cols]).astype(jnp.bfloat16)
    gains_grad = jnp.concatenate([gain_one_grad[:1], gain_two_grad[:1]]).astype(jnp.bfloat16)
    folded = -(-width // late_cols)
    gains_rows = jnp.pad(gains_grad, ((0, 0), (0, folded * late_cols - width)))
    gains_rows = jnp.pad(
        gains_rows.reshape(2 * folded, late_cols), ((0, extra_rows - 2 * folded), (0, 0))
    )
    last = jnp.concatenate(
        [
            qkv_grad.reshape(seq_count, sub_count, tile_rows, late_cols),
            jnp.broadcast_to(gains_rows, (seq_count, sub_count) + gains_rows.shape),
        ],
        axis=2,
    )
    last = reduce_blocks(reduce_blocks(last, "sub", 1), "seq", 0)
    gains_sum = last[tile_rows : tile_rows + 2 * folded].reshape(2, folded * late_cols)[:, :width]
    gains_out = reduce_blocks(
        reduce_blocks(
            jnp.transpose(gains_sum.reshape(2, owners, gain_part), (1, 0, 2)).reshape(
                owners // ctx_count, ctx_count, 2, gain_part
            ),
            "shard",
            0,
        ),
        "ctx",
        0,
    ).astype(jnp.float32)
    qkv_late = owner_sums(last[:tile_rows], tile_cols, owners // ctx_count // 2)
    is_early = lax.axis_index("shard") < owners // ctx_count // 2
    qkv_out = jnp.where(is_early, qkv_early, qkv_late).astype(jnp.float32)
    ffn_out = ffn_out.astype(jnp.float32)
    return (
        block_out,
        input_grad,
        gains_out,
        qkv_out,
        out_out,
        ffn_out[:, :hidden_part],
        ffn_out[:, hidden_part : 2 * hidden_part],
        ffn_out[:, 2 * hidden_part :].T,
    )


def solution(mesh):
    shard_count, ctx_count, tensor_count = (mesh.shape[axis] for axis in ("shard", "ctx", "tensor"))

    def run(tokens, *rest):
        seq_count = tokens.shape[0] // shard_count
        split = Mesh(
            mesh.devices.reshape(shard_count, ctx_count, seq_count, tensor_count // seq_count),
            ("shard", "ctx", "seq", "sub"),
        )
        rows = P("shard", "ctx", None)
        pool = ("shard", "ctx")
        team = ("seq", "sub")
        weights = (P(None, pool), P(team, pool), P(team, pool), P(pool, team), P(pool, team), P(team, pool))
        return jax.shard_map(
            shards,
            mesh=split,
            in_specs=(rows,) + weights + (rows,),
            out_specs=(rows, rows) + weights,
            check_vma=False,
        )(tokens, *rest)

    return run
```

time: 1050 us -> 630 us (0.60)
  waiting for transfers between devices: 586 us -> 195 us
  Pallas kernels: 133 us -> 226 us
  local copies, waits for them, and re-layouts: 135 us -> 58.1 us
  matrix products: 64.2 us -> 6.3 us
  starting transfers between devices: 22.7 us -> 78 us
  other arithmetic: 80 us -> 42.8 us
    reduce_scatter x2 -> x0, waiting for transfers between devices: 178 us -> none  [the longest x1 144 us: shards(): lax.psum_scatter(last, everyone, scatter_dimension=0, tiled=False)]
    unnamed x11 -> x6, waiting for transfers between devices: 153 us -> 0.1 us
    all_gather x6 -> x4, waiting for transfers between devices: 215 us -> 85.8 us  [the longest x2 35.6 us: shards(): pairs.append(lax.all_gather(own_part, ('ctx', 'sub'), axis=1, tiled=True))]
    pallas_call x1 -> x16, Pallas kernels: 69.4 us -> 176 us  [the longest x10 79.1 us: row_call(): pl.pallas_call(kernel, grid=(2,), in_specs=[whole(a.shape) if fixed else...]
    ppermute x4 -> x44, waiting for transfers between devices: 0.01 us -> 87.8 us  [the longest x42 87.8 us: pull(): lax.ppermute(values, axis, [((i + ahead) % count, i) for i in range(count)])]
    ppermute x4 -> x44, starting transfers between devices: 1.14 us -> 67 us  [the longest x42 61.8 us: pull(): lax.ppermute(values, axis, [((i + ahead) % count, i) for i in range(count)])]
    dot_general x18 -> x3, matrix products: 64.2 us -> 6.3 us  [matmul(): return jnp.einsum(spec, left, right, preferred_element_type=jnp.float32)]
    reshape x13 -> x8, local copies, waits for them, and re-layouts: 49.7 us -> 5.94 us  [the longest x1 2.99 us: shards(): jnp.transpose(out_tiles, (1, 0, 4, 2, 3, 5)).reshape(HEADS, HEAD_DIM, width)]
  transfers between devices with their start and end apart: 18 -> 54, of which waited for: 12 -> 26; matrix products, arithmetic and copies ran while one was open for 19% -> 12% of each run, Pallas kernels for 6% -> 31%
where the time goes in v2:
time: 630 us; the launch traced here: 621 us
  Pallas kernels  226 us (36%)
  waiting for transfers between devices  195 us (31%)
  starting transfers between devices  78 us (12%)
  local copies, waits for them, and re-layouts  58.1 us (9%)
  other arithmetic  42.8 us (7%)
  between operations  15.3 us (2%)
  matrix products  6.3 us (1%)
    ppermute x42, waiting for transfers between devices, pull(): lax.ppermute(values, axis, [((i + ahead) % count, i) for i in range(count)])  87.8 us
    pallas_call x10, Pallas kernels, row_call(): pl.pallas_call(kernel, grid=(2,), in_specs=[whole(a.shape) if fixed else...  79.1 us
    pallas_call x2, Pallas kernels, attention_backward(): pl.pallas_call(filling if filled else kernel, out_shape=(jax.ShapeDtypeSt...  62.3 us
    ppermute x42, starting transfers between devices, pull(): lax.ppermute(values, axis, [((i + ahead) % count, i) for i in range(count)])  61.8 us
    pallas_call x2, Pallas kernels, attention_forward(): pl.pallas_call(functools.partial(forward_kernel, ctx_count, sub, chunk, g...  49.8 us
    all_gather x2, waiting for transfers between devices, shards(): pairs.append(lax.all_gather(own_part, ('ctx', 'sub'), axis=1, tiled=True))  35.6 us
    all_gather x1, waiting for transfers between devices, shards(): ffn_all = lax.all_gather(ffn_tile, ('shard', 'ctx'), axis=0, tiled=True)  34.4 us
    unnamed x79, local copies, waits for them, and re-layouts  20.6 us
  transfers between devices with their start and end apart: 54, of which 26 were waited for; matrix products, arithmetic and copies ran while one was open for 12% of the time, Pallas kernels for 31%

profile of v2, /device:TPU:0, one launch (start us, length us, event | category | flops | bytes accessed | tf_op | source)
XLA Modules:
  0.0 621.2 jit_solution(4639676386818499217)
XLA Ops:
  9.7 5.1 collective-permute-start.1
  23.7 6.0 collective-permute-done.4
  37.5 7.1 %collective-permute-done.5 = bf16[2,4,240,120]{3,2,1,0:T(8,128)(2,1)S(1)} collective-permute-done((bf16[2,4,240,120]{3,2,1,0:T(8,128)(2,1)}, bf16[2,4,240,120]{3,2,1,0:T(8,128)(2,1)S(1)}, u32[]{:S(2)}, u32[]{:S(2)}) %collective-permute-start.5) | collective-permute-done | bytes 460832 | tf_op jit(solution)/shard_map/ppermute | solution.py:565
  65.4 15.8 %all-gather.13.cloned.1.call-done = bf16[32,242,200]{1,2,0:T(8,128)(2,1)} async-done(((bf16[1,242,200]{1,2,0:T(8,128)(2,1)}), bf16[32,242,200]{1,2,0:T(8,128)(2,1)}) %all-gather.13.cloned.1.call-update) | async-done | bytes 3097616 | tf_op jit(solution)/shard_map/all_gather | solution.py:703
  83.5 6.1 copy.71.in_ref
  94.7 6.7 %project.1 = (bf16[5,2,3,256,128]{4,3,2,1,0:T(8,128)(2,1)}, bf16[5,512,128]{2,1,0:T(8,128)(2,1)}, bf16[512,960]{1,0:T(8,128)(2,1)}) custom-call(bf16[512,960]{1,0:T(8,128)(2,1)} %maximum_select_fusion.1.token_ref.refs_3_, f32[1,960]{1,0:T(1,128)} %squeeze.92.gain_ref, bf16[960,1664]{1,0:T(8,128)(2,1)} %copy-done, f32[512,128]{1,0:T(8,128)} %pad_maximum_fusion.5.cos_ref, ...), custom_call_target="tpu_custom_call" | custom-call | flops 1635778560 | bytes 8310528 | tf_op jit(solution)/shard_map/project/pallas_call | solution.py:363
  105.1 35.6 %all-gather.7.cloned.1.call-done.kv_ref = bf16[3,4096,128]{2,1,0:T(8,128)(2,1)} async-done(((bf16[3,512,128]{2,1,0:T(8,128)(2,1)}), bf16[3,4096,128]{2,1,0:T(8,128)(2,1)}) %all-gather.7.cloned.1.call-update) | async-done | bytes 3145744 | tf_op jit(solution)/shard_map/all_gather | solution.py:755
  142.6 30.1 %attention_forward.2 = f32[3,1536,128]{2,1,0:T(8,128)S(1)} custom-call(s32[1]{0:T(128)} %bitcast.pair_ref, bf16[5,1536,128]{2,1,0:T(8,128)(2,1)S(1)} %bitcast.158, bf16[3,4096,128]{2,1,0:T(8,128)(2,1)} %all-gather.7.cloned.1.call-done.kv_ref), custom_call_target="tpu_custom_call" | custom-call | flops 2415919104 | bytes 6684672 | tf_op jit(solution)/shard_map/attention_forward/pallas_call | solution.py:140
  184.0 19.6 %attention_forward.3 = f32[2,1536,128]{2,1,0:T(8,128)S(1)} custom-call(s32[1]{0:T(128)} %bitcast.pair_ref, bf16[5,1536,128]{2,1,0:T(8,128)(2,1)S(1)} %bitcast.159, bf16[2,4096,128]{2,1,0:T(8,128)(2,1)S(1)} %copy-done.3), custom_call_target="tpu_custom_call" | custom-call | flops 1610612736 | bytes 4456448 | tf_op jit(solution)/shard_map/attention_forward/pallas_call | solution.py:140
  207.1 9.2 %mix.1 = (f32[512,960]{1,0:T(8,128)}, bf16[512,1024]{1,0:T(8,128)(2,1)}, bf16[512,960]{1,0:T(8,128)(2,1)}) custom-call(f32[3,2,3,256,128]{4,3,2,1,0:T(8,128)} %bitcast.154, f32[2,2,3,256,128]{4,3,2,1,0:T(8,128)} %bitcast.156, bf16[15,128,960]{2,1,0:T(8,128)(2,1)} %pad.21.refs_2_.refs_8_, bf16[512,960]{1,0:T(8,128)(2,1)} %maximum_select_fusion.1.token_ref.refs_3_, ...), custom_call_target="tpu_custom_call" | custom-call | flops 1887436800 | bytes 12603136 | tf_op jit(solution)/shard_map/mix/pallas_call | solution.py:363
  220.5 34.4 %all-gather.11.cloned.1.call-done.weight_ref = bf16[960,1920]{1,0:T(8,128)(2,1)} async-done(((bf16[120,1920]{1,0:T(8,128)(2,1)}), bf16[960,1920]{1,0:T(8,128)(2,1)}) %all-gather.11.cloned.1.call-update) | async-done | bytes 3686416 | tf_op jit(solution)/shard_map/all_gather | solution.py:764
  255.0 8.2 %feed.5 = (bf16[512,1024]{1,0:T(8,128)(2,1)}, bf16[512,1024]{1,0:T(8,128)(2,1)}, bf16[512,640]{1,0:T(8,128)(2,1)}, bf16[512,1280]{1,0:T(8,128)(2,1)}) custom-call(bf16[512,1024]{1,0:T(8,128)(2,1)} %copy-done.27, bf16[512,1024]{1,0:T(8,128)(2,1)} %copy-done.28, bf16[960,1920]{1,0:T(8,128)(2,1)} %all-gather.11.cloned.1.call-done.weight_ref), custom_call_target="tpu_custom_call" | custom-call | flops 5033164800 | bytes 9846784 | tf_op jit(solution)/shard_map/feed/pallas_call | solution.py:363
  264.8 8.6 %feed.4 = (f32[512,1024]{1,0:T(8,128)}, f32[512,1024]{1,0:T(8,128)}, bf16[512,640]{1,0:T(8,128)(2,1)}, bf16[512,1280]{1,0:T(8,128)(2,1)}) custom-call(bf16[512,1024]{1,0:T(8,128)(2,1)} %get-tuple-element.88.rows_ref.refs_0_, bf16[512,1024]{1,0:T(8,128)(2,1)} %copy-done.19, bf16[960,1920]{1,0:T(8,128)(2,1)} %all-gather.11.cloned.1.call-done.weight_ref), custom_call_target="tpu_custom_call" | custom-call | flops 5033164800 | bytes 11943936 | tf_op jit(solution)/shard_map/feed/pallas_call | solution.py:363
  277.5 8.2 %feed.7 = (bf16[512,1024]{1,0:T(8,128)(2,1)}, bf16[512,1024]{1,0:T(8,128)(2,1)}, bf16[512,640]{1,0:T(8,128)(2,1)}, bf16[512,1280]{1,0:T(8,128)(2,1)}) custom-call(bf16[512,1024]{1,0:T(8,128)(2,1)} %copy-done.30, bf16[512,1024]{1,0:T(8,128)(2,1)} %copy-done.29, bf16[960,1920]{1,0:T(8,128)(2,1)} %all-gather.11.cloned.1.call-done.weight_ref), custom_call_target="tpu_custom_call" | custom-call | flops 5033164800 | bytes 9846784 | tf_op jit(solution)/shard_map/feed/pallas_call | solution.py:363
  286.1 8.5 %feed.6 = (f32[512,1024]{1,0:T(8,128)}, f32[512,1024]{1,0:T(8,128)}, bf16[512,640]{1,0:T(8,128)(2,1)}, bf16[512,1280]{1,0:T(8,128)(2,1)}) custom-call(bf16[512,1024]{1,0:T(8,128)(2,1)} %collective-permute-done.8.rows_ref.refs_2_, bf16[512,1024]{1,0:T(8,128)(2,1)} %collective-permute-done.12.cot_ref.refs_6_, ...), custom_call_target="tpu_custom_call" | custom-call | flops 5033164800 | bytes 11943936 | tf_op jit(solution)/shard_map/feed/pallas_call | solution.py:363
  298.9 16.4 %weight_grads.1 = bf16[960,1920]{1,0:T(8,128)(2,1)} custom-call(bf16[512,1024]{1,0:T(8,128)(2,1)} %get-tuple-element.88.rows_ref.refs_0_, bf16[512,1024]{1,0:T(8,128)(2,1)} %copy-done.27, bf16[512,1024]{1,0:T(8,128)(2,1)} %collective-permute-done.8.rows_ref.refs_2_, bf16[512,1024]{1,0:T(8,128)(2,1)} %copy-done.30, bf16[512,1024]{1,0:T(8,128)(2,1)} %copy-done.19, ...), custom_call_target="tpu_custom_call" | custom-call | flops 7549747200 | bytes 19415040 | tf_op jit(solution)/shard_map/weight_grads/pallas_call | solution.py:543
  315.4 7.5 %collective-permute-done.16.refs_2_ = bf16[512,1024]{1,0:T(8,128)(2,1)S(1)} collective-permute-done((bf16[512,1024]{1,0:T(8,128)(2,1)}, bf16[512,1024]{1,0:T(8,128)(2,1)S(1)}, u32[]{:S(2)}, u32[]{:S(2)}) %collective-permute-start.16) | collective-permute-done | bytes 1048608 | tf_op jit(solution)/shard_map/ppermute | solution.py:565
  327.3 11.6 %unmix.1 = (f32[512,960]{1,0:T(8,128)}, bf16[512,960]{1,0:T(8,128)(2,1)}, bf16[5,2,3,256,128]{4,3,2,1,0:T(8,128)(2,1)}, bf16[5,2,3,256,128]{4,3,2,1,0:T(8,128)(2,1)}, f32[8,960]{1,0:T(8,128)}) custom-call(f32[512,1024]{1,0:T(8,128)} %get-tuple-element.106.refs_0_, bf16[512,1024]{1,0:T(8,128)(2,1)} %copy-done.15, bf16[512,1024]{1,0:T(8,128)(2,1)} %copy-done.16, ...), custom_call_target="tpu_custom_call" | custom-call | flops 1887436800 | bytes 22660864 | tf_op jit(solution)/shard_map/unmix/pallas_call | solution.py:363
  343.7 36.9 %attention_backward.2 = (f32[5,1536,128]{2,1,0:T(8,128)}, bf16[5,4096,128]{2,1,0:T(8,128)(2,1)}) custom-call(s32[1]{0:T(128)} %bitcast.pair_ref, bf16[5,1536,128]{2,1,0:T(8,128)(2,1)S(1)} %bitcast.160, bf16[5,1536,128]{2,1,0:T(8,128)(2,1)S(1)} %bitcast.162, bf16[5,1536,128]{2,1,0:T(8,128)(2,1)S(1)} %bitcast.164, ...), custom_call_target="tpu_custom_call" | custom-call | flops 6039797760 | bytes 12189696 | tf_op jit(solution)/shard_map/attention_backward/pallas_call | solution.py:243
  392.4 25.4 %attention_backward.3 = (f32[5,1536,128]{2,1,0:T(8,128)}, bf16[5,4096,128]{2,1,0:T(8,128)(2,1)}) custom-call(s32[1]{0:T(128)} %bitcast.pair_ref, bf16[5,1536,128]{2,1,0:T(8,128)(2,1)S(1)} %bitcast.161, bf16[5,1536,128]{2,1,0:T(8,128)(2,1)S(1)} %bitcast.163, bf16[5,1536,128]{2,1,0:T(8,128)(2,1)S(1)} %bitcast.165, ...), custom_call_target="tpu_custom_call", output_to_operand_aliasing={{0}: (5, {}), {1}: (6, {})} | custom-call | flops 4026531840 | bytes 8126464 | tf_op jit(solution)/shard_map/attention_backward/pallas_call | solution.py:243
  417.8 6.8 %reduce-scatter.7.cloned.1.call-done = bf16[120,1920]{1,0:T(8,128)(2,1)} async-done(((bf16[960,1920]{1,0:T(8,128)(2,1)}), bf16[120,1920]{1,0:T(8,128)(2,1)}) %reduce-scatter.7.cloned.1.call-update) | async-done | bytes 460816 | tf_op jit(solution)/shard_map/optimization_barrier | solution.py:865
  444.9 16.3 %collective-permute-done.32 = bf16[2,960,256]{2,1,0:T(8,128)(2,1)} collective-permute-done((bf16[2,960,256]{2,1,0:T(8,128)(2,1)S(1)}, bf16[2,960,256]{2,1,0:T(8,128)(2,1)}, u32[]{:S(2)}, u32[]{:S(2)}) %collective-permute-start.32) | collective-permute-done | bytes 983072 | tf_op jit(solution)/shard_map/ppermute | solution.py:565
  463.1 17.2 %collective-permute-done.22 = bf16[240,1856]{1,0:T(8,128)(2,1)} collective-permute-done((bf16[240,1856]{1,0:T(8,128)(2,1)}, bf16[240,1856]{1,0:T(8,128)(2,1)}, u32[]{:S(2)}, u32[]{:S(2)}) %collective-permute-start.22) | collective-permute-done | bytes 890912 | tf_op jit(solution)/shard_map/ppermute | solution.py:565
  489.1 7.2 %place_rows.2 = bf16[2,960,1024]{2,1,0:T(8,128)(2,1)} custom-call(s32[8]{0:T(128)} %stack.119.seq_ref, s32[8]{0:T(128)} %stack.124.chunk_ref, bf16[8,960,256]{2,1,0:T(8,128)(2,1)} %pad_maximum_fusion.in_ref), custom_call_target="tpu_custom_call" | custom-call | tf_op jit(solution)/shard_map/place_rows/pallas_call | solution.py:626
  498.3 12.4 %collective-permute-start.25 = (bf16[240,120]{1,0:T(8,128)(2,1)S(1)}, bf16[240,120]{1,0:T(8,128)(2,1)S(1)}, u32[]{:S(2)}, u32[]{:S(2)}) collective-permute-start(bf16[240,120]{1,0:T(8,128)(2,1)S(1)} %get-tuple-element.168), channel_id=1, source_target_pairs={{8,0},{12,4},{0,8},{4,12},{9,1},{13,5},{1,9},{5,13},{10,2},{14,6},... | collective-permute-start | bytes 172808 | tf_op jit(solution)/shard_map/ppermute | solution.py:565
  518.2 6.8 %collective-permute-done.29 = bf16[240,200]{0,1:T(8,128)(2,1)S(1)} collective-permute-done((bf16[240,200]{0,1:T(8,128)(2,1)S(1)}, bf16[240,200]{0,1:T(8,128)(2,1)S(1)}, u32[]{:S(2)}, u32[]{:S(2)}) %collective-permute-start.29) | collective-permute-done | bytes 96032 | tf_op jit(solution)/shard_map/ppermute | solution.py:565
  525.1 9.2 %finish.1 = (bf16[512,1664]{1,0:T(8,128)(2,1)}, bf16[960,512]{1,0:T(8,128)(2,1)}, f32[8,960]{1,0:T(8,128)}) custom-call(f32[5,2,3,256,128]{4,3,2,1,0:T(8,128)} %bitcast.167, bf16[5,512,128]{2,1,0:T(8,128)(2,1)} %reduce-scatter.5.cloned.1.call-done.dkv_ref, f32[512,128]{1,0:T(8,128)} %pad_maximum_fusion.5.cos_ref, f32[512,128]{1,0:T(8,128)} %pad_maximum_fusion.6.sin_ref, ...), custom_call_target="tpu_custom_call" | custom-call | flops 1635778560 | bytes 13977344 | tf_op jit(solution)/shard_map/finish/pallas_call | solution.py:363
  545.0 12.2 %collective-permute-done.34 = bf16[960,256]{1,0:T(8,128)(2,1)} collective-permute-done((bf16[960,256]{1,0:T(8,128)(2,1)}, bf16[960,256]{1,0:T(8,128)(2,1)}, u32[]{:S(2)}, u32[]{:S(2)}) %collective-permute-start.34) | collective-permute-done | bytes 491552 | tf_op jit(solution)/shard_map/ppermute | solution.py:570
  571.9 9.2 %collective-permute-start.42 = (bf16[2,120]{1,0:T(2,128)(2,1)S(1)}, bf16[2,120]{1,0:T(2,128)(2,1)S(1)}, u32[]{:S(2)}, u32[]{:S(2)}) collective-permute-start(bf16[2,120]{1,0:T(2,128)(2,1)S(1)} %get-tuple-element.176), channel_id=1, source_target_pairs={{8,0},{12,4},{0,8},{4,12},{9,1},{13,5},{1,9},{5,13},{10,2},{14,6},... | collective-permute-start | bytes 1448 | tf_op jit(solution)/shard_map/ppermute | solution.py:565
  588.9 5.5 collective-permute-start.46
  597.2 7.1 %collective-permute-done.46 = bf16[240,200]{0,1:T(8,128)(2,1)S(1)} collective-permute-done((bf16[240,200]{0,1:T(8,128)(2,1)S(1)}, bf16[240,200]{0,1:T(8,128)(2,1)S(1)}, u32[]{:S(2)}, u32[]{:S(2)}) %collective-permute-start.46) | collective-permute-done | bytes 96032 | tf_op jit(solution)/shard_map/ppermute | solution.py:565
  606.1 7.8 %place_rows.3 = f32[2,960,1024]{2,1,0:T(8,128)} custom-call(s32[8]{0:T(128)} %stack.119.seq_ref, s32[8]{0:T(128)} %stack.124.chunk_ref, bf16[8,960,256]{2,1,0:T(8,128)(2,1)} %constant_dynamic-update-slice_fusion.in_ref), custom_call_target="tpu_custom_call" | custom-call | tf_op jit(solution)/shard_map/place_rows/pallas_call | solution.py:626
  (274 shorter events, 181.0 us)
Async XLA Ops:
  7.2 74.1 %all-gather.13.cloned.1.call-start = ((), (), s32[]{:S(2)}) async-start(), calls=%async_computation.6 | async-start | bytes 3379200 | tf_op jit(solution)/shard_map/all_gather | solution.py:703
  9.6 131.1 %all-gather.7.cloned.1.call-start = ((), (), s32[]{:S(2)}) async-start(), calls=%async_computation.2 | async-start | bytes 3538944 | tf_op jit(solution)/shard_map/all_gather | solution.py:755
  31.0 13.6 %collective-permute-start.5 = (bf16[2,4,240,120]{3,2,1,0:T(8,128)(2,1)}, bf16[2,4,240,120]{3,2,1,0:T(8,128)(2,1)S(1)}, u32[]{:S(2)}, u32[]{:S(2)}) collective-permute-start(bf16[2,4,240,120]{3,2,1,0:T(8,128)(2,1)} %fusion.18), channel_id=1, source_target_pairs={{2,0},{0,2},{3,1},{1,3},{6,4},{4,6},{7,5},{5,7},{10,8},{8,10},{11,... | collective-permute-start | bytes 1382408 | tf_op jit(solution)/shard_map/ppermute | solution.py:565
  35.6 16.1 %collective-permute-start = (bf16[256,960]{1,0:T(8,128)(2,1)}, bf16[256,960]{1,0:T(8,128)(2,1)S(1)}, u32[]{:S(2)}, u32[]{:S(2)}) collective-permute-start(bf16[256,960]{1,0:T(8,128)(2,1)} %bitcast.184), channel_id=1, source_target_pairs={{0,12},{4,8},{8,4},{12,0},{1,13},{5,9},{9,5},{13,1},{2,14},{6,10},... | collective-permute-start | bytes 1474568 | tf_op jit(solution)/shard_map/ppermute | solution.py:570
  103.4 70.8 %all-gather.9.cloned.1.call-start = ((), (), s32[]{:S(2)}) async-start(), calls=%async_computation.3 | async-start | bytes 2359296 | tf_op jit(solution)/shard_map/all_gather | solution.py:755
  140.8 114.2 %all-gather.11.cloned.1.call-start = ((), (), s32[]{:S(2)}) async-start(), calls=%async_computation.4 | async-start | bytes 4147200 | tf_op jit(solution)/shard_map/all_gather | solution.py:764
  174.2 250.5 %reduce-scatter.7.cloned.1.call-start = ((), (), s32[]{:S(2)}) async-start(), calls=%async_computation.7 | async-start | bytes 4147200
  174.3 29.4 %collective-permute-start.7 = (bf16[256,960]{1,0:T(8,128)(2,1)}, bf16[256,960]{1,0:T(8,128)(2,1)}, u32[]{:S(2)}, u32[]{:S(2)}) collective-permute-start(bf16[256,960]{1,0:T(8,128)(2,1)} %bitcast.185), channel_id=1, source_target_pairs={{0,12},{4,8},{8,4},{12,0},{1,13},{5,9},{9,5},{13,1},{2,14},{6,10},... | collective-permute-start | bytes 1474568 | tf_op jit(solution)/shard_map/ppermute | solution.py:570
  216.9 56.5 %collective-permute-start.8 = (bf16[512,1024]{1,0:T(8,128)(2,1)}, bf16[512,1024]{1,0:T(8,128)(2,1)}, u32[]{:S(2)}, u32[]{:S(2)}) collective-permute-start(bf16[512,1024]{1,0:T(8,128)(2,1)} %get-tuple-element.88.rows_ref.refs_0_), channel_id=1, source_target_pairs={{2,0},{0,2},{3,1},{1,3},{6,4},{4,6},{7,5},{5,7},{10,8},{8,10},{11,... | collective-permute-start | bytes 3145736 | tf_op jit(solution)/shard_map/ppermute | solution.py:565
  218.3 46.5 %collective-permute-start.12 = (bf16[512,1024]{1,0:T(8,128)(2,1)S(1)}, bf16[512,1024]{1,0:T(8,128)(2,1)}, u32[]{:S(2)}, u32[]{:S(2)}) collective-permute-start(bf16[512,1024]{1,0:T(8,128)(2,1)S(1)} %pad.22.cot_ref.refs_4_), channel_id=1, source_target_pairs={{2,0},{0,2},{3,1},{1,3},{6,4},{4,6},{7,5},{5,7},{10,8},{8,10},{11,... | collective-permute-start | bytes 3145736 | tf_op jit(solution)/shard_map/ppermute | solution.py:565
  297.5 25.4 %collective-permute-start.16 = (bf16[512,1024]{1,0:T(8,128)(2,1)}, bf16[512,1024]{1,0:T(8,128)(2,1)S(1)}, u32[]{:S(2)}, u32[]{:S(2)}) collective-permute-start(bf16[512,1024]{1,0:T(8,128)(2,1)} %add_convert_fusion.1), channel_id=1, source_target_pairs={{2,0},{0,2},{3,1},{1,3},{6,4},{4,6},{7,5},{5,7},{10,8},{8,10},{11,... | collective-permute-start | bytes 3145736 | tf_op jit(solution)/shard_map/ppermute | solution.py:565
  322.9 202.1 %reduce-scatter.5.cloned.1.call-start = ((), (), s32[]{:S(2)}) async-start(), calls=%async_computation.5 | async-start | bytes 5898240 | tf_op jit(solution)/shard_map/reduce_scatter | solution.py:868
  323.1 57.6 %collective-permute-start.18 = (bf16[512,1024]{1,0:T(8,128)(2,1)}, bf16[512,1024]{1,0:T(8,128)(2,1)S(1)}, u32[]{:S(2)}, u32[]{:S(2)}) collective-permute-start(bf16[512,1024]{1,0:T(8,128)(2,1)} %get-tuple-element.118), channel_id=1, source_target_pairs={{1,0},{0,1},{3,2},{2,3},{5,4},{4,5},{7,6},{6,7},{9,8},{8,9},{11,10... | collective-permute-start | bytes 3145736 | tf_op jit(solution)/shard_map/ppermute | solution.py:565
  338.9 41.8 %collective-permute-start.19 = (bf16[512,1024]{1,0:T(8,128)(2,1)S(1)}, bf16[512,1024]{1,0:T(8,128)(2,1)S(1)}, u32[]{:S(2)}, u32[]{:S(2)}) collective-permute-start(bf16[512,1024]{1,0:T(8,128)(2,1)S(1)} %copy-done.20), channel_id=1, source_target_pairs={{2,0},{0,2},{3,1},{1,3},{6,4},{4,6},{7,5},{5,7},{10,8},{8,10},{11,... | collective-permute-start | bytes 3145736 | tf_op jit(solution)/shard_map/ppermute | solution.py:565
  387.5 30.2 %collective-permute-start.20 = (bf16[960,256]{1,0:T(8,128)(2,1)S(1)}, bf16[960,256]{1,0:T(8,128)(2,1)S(1)}, u32[]{:S(2)}, u32[]{:S(2)}) collective-permute-start(bf16[960,256]{1,0:T(8,128)(2,1)S(1)} %get-tuple-element.157), channel_id=1, source_target_pairs={{0,12},{4,8},{8,4},{12,0},{1,13},{5,9},{9,5},{13,1},{2,14},{6,10},... | collective-permute-start | bytes 1474568 | tf_op jit(solution)/shard_map/ppermute | solution.py:570
  436.5 24.7 %collective-permute-start.32 = (bf16[2,960,256]{2,1,0:T(8,128)(2,1)S(1)}, bf16[2,960,256]{2,1,0:T(8,128)(2,1)}, u32[]{:S(2)}, u32[]{:S(2)}) collective-permute-start(bf16[2,960,256]{2,1,0:T(8,128)(2,1)S(1)} %pad_maximum_fusion.2), channel_id=1, source_target_pairs={{2,0},{0,2},{3,1},{1,3},{6,4},{4,6},{7,5},{5,7},{10,8},{8,10},{11,... | collective-permute-start | bytes 2949128 | tf_op jit(solution)/shard_map/ppermute | solution.py:565
  444.2 36.2 %collective-permute-start.22 = (bf16[240,1856]{1,0:T(8,128)(2,1)}, bf16[240,1856]{1,0:T(8,128)(2,1)}, u32[]{:S(2)}, u32[]{:S(2)}) collective-permute-start(bf16[240,1856]{1,0:T(8,128)(2,1)} %dynamic-slice_bitcast_fusion.1), channel_id=1, source_target_pairs={{2,0},{0,2},{3,1},{1,3},{6,4},{4,6},{7,5},{5,7},{10,8},{8,10},{11,... | collective-permute-start | bytes 2672648 | tf_op jit(solution)/shard_map/ppermute | solution.py:565
  444.9 40.6 %collective-permute-start.31 = (bf16[2,960,256]{2,1,0:T(8,128)(2,1)S(1)}, bf16[2,960,256]{2,1,0:T(8,128)(2,1)}, u32[]{:S(2)}, u32[]{:S(2)}) collective-permute-start(bf16[2,960,256]{2,1,0:T(8,128)(2,1)S(1)} %pad_maximum_fusion.2), channel_id=1, source_target_pairs={{1,0},{0,1},{3,2},{2,3},{5,4},{4,5},{7,6},{6,7},{9,8},{8,9},{11,10... | collective-permute-start | bytes 2949128 | tf_op jit(solution)/shard_map/ppermute | solution.py:565
  461.2 24.3 %collective-permute-start.33 = (bf16[2,960,256]{2,1,0:T(8,128)(2,1)}, bf16[2,960,256]{2,1,0:T(8,128)(2,1)}, u32[]{:S(2)}, u32[]{:S(2)}) collective-permute-start(bf16[2,960,256]{2,1,0:T(8,128)(2,1)} %collective-permute-done.32), channel_id=1, source_target_pairs={{1,0},{0,1},{3,2},{2,3},{5,4},{4,5},{7,6},{6,7},{9,8},{8,9},{11,10... | collective-permute-start | bytes 2949128 | tf_op jit(solution)/shard_map/ppermute | solution.py:565
  482.8 13.5 %collective-permute-start.23 = (bf16[4,240,120]{2,1,0:T(8,128)(2,1)S(1)}, bf16[4,240,120]{2,1,0:T(8,128)(2,1)S(1)}, u32[]{:S(2)}, u32[]{:S(2)}) collective-permute-start(bf16[4,240,120]{2,1,0:T(8,128)(2,1)S(1)} %dynamic-slice_bitcast_fusion.3), channel_id=1, source_target_pairs={{16,0},{0,16},{17,1},{1,17},{18,2},{2,18},{19,3},{3,19},{20,4},{4,... | collective-permute-start | bytes 691208 | tf_op jit(solution)/shard_map/ppermute | solution.py:565
  484.2 28.5 %collective-permute-start.27 = (bf16[4,240,200]{1,2,0:T(8,128)(2,1)S(1)}, bf16[4,240,200]{1,2,0:T(8,128)(2,1)S(1)}, u32[]{:S(2)}, u32[]{:S(2)}) collective-permute-start(bf16[4,240,200]{1,2,0:T(8,128)(2,1)S(1)} %bitcast.180), channel_id=1, source_target_pairs={{16,0},{17,1},{18,2},{19,3},{20,4},{21,5},{22,6},{23,7},{24,8},{25... | collective-permute-start | bytes 1152008 | tf_op jit(solution)/shard_map/ppermute | solution.py:615
  496.4 18.4 %collective-permute-start.26 = (bf16[240,120]{1,0:T(8,128)(2,1)S(1)}, bf16[240,120]{1,0:T(8,128)(2,1)S(1)}, u32[]{:S(2)}, u32[]{:S(2)}) collective-permute-start(bf16[240,120]{1,0:T(8,128)(2,1)S(1)} %get-tuple-element.167), channel_id=1, source_target_pairs={{4,0},{8,4},{12,8},{0,12},{5,1},{9,5},{13,9},{1,13},{6,2},{10,6},{... | collective-permute-start | bytes 172808 | tf_op jit(solution)/shard_map/ppermute | solution.py:565
  498.3 17.6 %collective-permute-start.25 = (bf16[240,120]{1,0:T(8,128)(2,1)S(1)}, bf16[240,120]{1,0:T(8,128)(2,1)S(1)}, u32[]{:S(2)}, u32[]{:S(2)}) collective-permute-start(bf16[240,120]{1,0:T(8,128)(2,1)S(1)} %get-tuple-element.168), channel_id=1, source_target_pairs={{8,0},{12,4},{0,8},{4,12},{9,1},{13,5},{1,9},{5,13},{10,2},{14,6},... | collective-permute-start | bytes 172808 | tf_op jit(solution)/shard_map/ppermute | solution.py:565
  542.0 15.1 %collective-permute-start.34 = (bf16[960,256]{1,0:T(8,128)(2,1)}, bf16[960,256]{1,0:T(8,128)(2,1)}, u32[]{:S(2)}, u32[]{:S(2)}) collective-permute-start(bf16[960,256]{1,0:T(8,128)(2,1)} %broadcast_select_fusion), channel_id=1, source_target_pairs={{0,12},{4,8},{8,4},{12,0},{1,13},{5,9},{9,5},{13,1},{2,14},{6,10},... | collective-permute-start | bytes 1474568 | tf_op jit(solution)/shard_map/ppermute | solution.py:570
  543.6 15.9 %collective-permute-start.39 = (bf16[256,800]{0,1:T(8,128)(2,1)S(1)}, bf16[256,800]{0,1:T(8,128)(2,1)}, u32[]{:S(2)}, u32[]{:S(2)}) collective-permute-start(bf16[256,800]{0,1:T(8,128)(2,1)S(1)} %dynamic-slice_bitcast_fusion.2), channel_id=1, source_target_pairs={{2,0},{0,2},{3,1},{1,3},{6,4},{4,6},{7,5},{5,7},{10,8},{8,10},{11,... | collective-permute-start | bytes 1228808 | tf_op jit(solution)/shard_map/ppermute | solution.py:565
  559.2 25.4 %collective-permute-start.36 = (bf16[2,960,256]{2,1,0:T(8,128)(2,1)}, bf16[2,960,256]{2,1,0:T(8,128)(2,1)S(1)}, u32[]{:S(2)}, u32[]{:S(2)}) collective-permute-start(bf16[2,960,256]{2,1,0:T(8,128)(2,1)} %pad_maximum_fusion.3), channel_id=1, source_target_pairs={{2,0},{0,2},{3,1},{1,3},{6,4},{4,6},{7,5},{5,7},{10,8},{8,10},{11,... | collective-permute-start | bytes 2949128 | tf_op jit(solution)/shard_map/ppermute | solution.py:565
  564.8 22.1 %collective-permute-start.35 = (bf16[2,960,256]{2,1,0:T(8,128)(2,1)}, bf16[2,960,256]{2,1,0:T(8,128)(2,1)S(1)}, u32[]{:S(2)}, u32[]{:S(2)}) collective-permute-start(bf16[2,960,256]{2,1,0:T(8,128)(2,1)} %pad_maximum_fusion.3), channel_id=1, source_target_pairs={{1,0},{0,1},{3,2},{2,3},{5,4},{4,5},{7,6},{6,7},{9,8},{8,9},{11,10... | collective-permute-start | bytes 2949128 | tf_op jit(solution)/shard_map/ppermute | solution.py:565
  565.5 15.5 %collective-permute-start.43 = (bf16[2,120]{1,0:T(2,128)(2,1)S(1)}, bf16[2,120]{1,0:T(2,128)(2,1)S(1)}, u32[]{:S(2)}, u32[]{:S(2)}) collective-permute-start(bf16[2,120]{1,0:T(2,128)(2,1)S(1)} %get-tuple-element.175), channel_id=1, source_target_pairs={{4,0},{8,4},{12,8},{0,12},{5,1},{9,5},{13,9},{1,13},{6,2},{10,6},{... | collective-permute-start | bytes 1448 | tf_op jit(solution)/shard_map/ppermute | solution.py:565
  567.9 20.1 %collective-permute-start.44 = (bf16[4,240,200]{1,2,0:T(8,128)(2,1)S(1)}, bf16[4,240,200]{1,2,0:T(8,128)(2,1)S(1)}, u32[]{:S(2)}, u32[]{:S(2)}) collective-permute-start(bf16[4,240,200]{1,2,0:T(8,128)(2,1)S(1)} %bitcast.173), channel_id=1, source_target_pairs={{0,16},{1,17},{2,18},{3,19},{4,20},{5,21},{6,22},{7,23},{8,24},{9,... | collective-permute-start | bytes 1152008 | tf_op jit(solution)/shard_map/ppermute | solution.py:615
  571.9 12.8 %collective-permute-start.42 = (bf16[2,120]{1,0:T(2,128)(2,1)S(1)}, bf16[2,120]{1,0:T(2,128)(2,1)S(1)}, u32[]{:S(2)}, u32[]{:S(2)}) collective-permute-start(bf16[2,120]{1,0:T(2,128)(2,1)S(1)} %get-tuple-element.176), channel_id=1, source_target_pairs={{8,0},{12,4},{0,8},{4,12},{9,1},{13,5},{1,9},{5,13},{10,2},{14,6},... | collective-permute-start | bytes 1448 | tf_op jit(solution)/shard_map/ppermute | solution.py:565
  584.6 20.4 %collective-permute-start.37 = (bf16[2,960,256]{2,1,0:T(8,128)(2,1)S(1)}, bf16[2,960,256]{2,1,0:T(8,128)(2,1)S(1)}, u32[]{:S(2)}, u32[]{:S(2)}) collective-permute-start(bf16[2,960,256]{2,1,0:T(8,128)(2,1)S(1)} %collective-permute-done.36), channel_id=1, source_target_pairs={{1,0},{0,1},{3,2},{2,3},{5,4},{4,5},{7,6},{6,7},{9,8},{8,9},{11,10... | collective-permute-start | bytes 2949128 | tf_op jit(solution)/shard_map/ppermute | solution.py:565
  588.9 15.4 %collective-permute-start.46 = (bf16[240,200]{0,1:T(8,128)(2,1)S(1)}, bf16[240,200]{0,1:T(8,128)(2,1)S(1)}, u32[]{:S(2)}, u32[]{:S(2)}) collective-permute-start(bf16[240,200]{0,1:T(8,128)(2,1)S(1)} %get-tuple-element.162), channel_id=1, source_target_pairs={{8,0},{12,4},{0,8},{4,12},{9,1},{13,5},{1,9},{5,13},{10,2},{14,6},... | collective-permute-start | bytes 288008 | tf_op jit(solution)/shard_map/ppermute | solution.py:565
  (55 other events, 529.5 us)
Sparse Core Ops, SparseCore 0:
  11.4 69.7 all-gather.12
  103.5 37.1 all-gather.6
  142.9 28.0 all-gather.8
  174.3 80.5 all-gather.10
  323.1 101.5 reduce-scatter.6
  427.4 67.7 reduce-scatter.4

commit v3 on v2

--- a/solution.py
+++ b/solution.py
@@ -120,14 +120,14 @@
         )
 
 
-def attention_forward(own_pair, queries, pairs_all, base, ctx_count, sub, chunk, group):
+def attention_forward(own_pair, queries, pairs_all, ctx_count, sub, chunk, group):
     rows = queries.shape[1]
     heads, length, _ = pairs_all.shape
     grid_spec = pltpu.PrefetchScalarGridSpec(
         num_scalar_prefetch=1,
         grid=(heads,),
         in_specs=[
-            pl.BlockSpec((1, rows, LANES), lambda h, p: (base + h, 0, 0)),
+            pl.BlockSpec((1, rows, LANES), lambda h, p: (h, 0, 0)),
             pl.BlockSpec((1, length, LANES), lambda h, p: (h, 0, 0)),
         ],
         out_specs=pl.BlockSpec((1, rows, LANES), lambda h, p: (h, 0, 0)),
@@ -228,12 +228,13 @@
     sweep(own + 1, pairs, 2, part, part)
 
 
-def attention_backward(own_pair, queries, cots, extra, pairs_all, base, filled, ctx_count, sub, chunk, group):
+def attention_backward(
+    own_pair, queries, cots, extra, pairs_all, base, stop, filled, ctx_count, sub, chunk, group
+):
     total_heads, rows, _ = queries.shape
-    heads, length, _ = pairs_all.shape
+    heads, length = stop - base, pairs_all.shape[1]
     row_spec = pl.BlockSpec((1, rows, LANES), lambda h, p: (base + h, 0, 0))
     long_spec = pl.BlockSpec((1, length, LANES), lambda h, p: (base + h, 0, 0))
-    part_spec = pl.BlockSpec((1, length, LANES), lambda h, p: (h, 0, 0))
     cost = heads * rows * length // 2
     kernel = functools.partial(backward_kernel, ctx_count, sub, chunk, group)
 
@@ -249,7 +250,7 @@
         grid_spec=pltpu.PrefetchScalarGridSpec(
             num_scalar_prefetch=1,
             grid=(heads,),
-            in_specs=[row_spec, row_spec, row_spec, part_spec]
+            in_specs=[row_spec, row_spec, row_spec, long_spec]
             + [pl.BlockSpec(memory_space=pl.ANY)] * len(filled),
             out_specs=(row_spec, long_spec),
         ),
@@ -395,7 +396,13 @@
     first = lane_index(token_ref.shape[0]) < HALF
     for head in range(HEADS):
         rows = pick(attended_refs, head)
-        total = total + dot_nn(rows.astype(jnp.bfloat16), weight_ref[head])
+        low = rows.astype(jnp.bfloat16)
+        if head % 2:
+            both = jnp.concatenate([low_before, low], axis=1)
+            total = total + dot_nn(both, weight_ref[head - 1 : head + 1].reshape(2 * LANES, -1))
+        elif head == HEADS - 1:
+            total = total + dot_nn(low, weight_ref[head])
+        low_before = low
         base = head // 2 * LANES
         if head % 2:
             both = jnp.where(first, pltpu.roll(before, HALF, 1), rows)
@@ -438,7 +445,11 @@
     lane = lane_index(hidden_low.shape[0])
     for head in range(HEADS):
         spot = (head // GROUP, 0, head % GROUP)
-        cots = dot_nt(hidden_low, weight_ref[head]).astype(jnp.bfloat16)
+        if head % 2 == 0:
+            many = weight_ref[head : head + 2].reshape(-1, weight_ref.shape[2])
+            cots_two = dot_nt(hidden_low, many).astype(jnp.bfloat16)
+        side = head % 2 * LANES
+        cots = cots_two[:, side : side + LANES]
         heads_ref[spot] = cots
         attended = pick(attended_refs, head)
         delta = jnp.sum(cots.astype(jnp.float32) * attended, axis=1, keepdims=True)
@@ -500,7 +511,14 @@
     input_ref[...] = jnp.transpose(grad_ref[...] + back).astype(jnp.bfloat16)
 
 
-def feed_kernel(rows_ref, cot_ref, weight_ref, back_ref, feed_ref, inner_ref, grad_ref):
+def feed_kernel(count, *refs):
+    weight_ref = refs[2 * count]
+    for at in range(count):
+        outs = refs[2 * count + 1 + 4 * at : 2 * count + 5 + 4 * at]
+        feed_rows(refs[2 * at], refs[2 * at + 1], weight_ref, *outs)
+
+
+def feed_rows(rows_ref, cot_ref, weight_ref, back_ref, feed_ref, inner_ref, grad_ref):
     part = inner_ref.shape[1]
     width = weight_ref.shape[0]
     rows, cots = rows_ref[:, :width], cot_ref[:, :width]
@@ -617,23 +635,29 @@
     return summed.astype(jnp.bfloat16)
 
 
-def place_kernel(seq_ref, chunk_ref, in_ref, out_ref):
-    out_ref[...] = in_ref[...].astype(out_ref.dtype)
-
-
-def place_rows(stacked, seqs, chunks, seq_count, chunk_count, kind):
-    pieces, width, chunk = stacked.shape
+def place_kernel(seq_ref, chunk_ref, *refs):
+    out_ref = refs[-1]
+    for at, ref in enumerate(refs[:-1]):
+
+        @pl.when(pl.program_id(0) == at)
+        def _(ref=ref):
+            out_ref[0] = ref[...].astype(out_ref.dtype)
+
+
+def place_rows(pieces, seqs, chunks, seq_count, chunk_count, kind):
+    width, chunk = pieces[0].shape
     return pl.pallas_call(
         place_kernel,
         out_shape=jax.ShapeDtypeStruct((seq_count, width, chunk_count * chunk), kind),
         grid_spec=pltpu.PrefetchScalarGridSpec(
             num_scalar_prefetch=2,
-            grid=(pieces,),
-            in_specs=[pl.BlockSpec((1, width, chunk), lambda i, s, c: (i, 0, 0))],
+            grid=(len(pieces),),
+            in_specs=[pl.BlockSpec((width, chunk), lambda i, s, c: (0, 0))] * len(pieces),
             out_specs=pl.BlockSpec((1, width, chunk), lambda i, s, c: (s[i], 0, c[i])),
         ),
+        compiler_params=pltpu.CompilerParams(vmem_limit_bytes=32 * 2**20),
         name="place_rows",
-    )(seqs, chunks, stacked)
+    )(seqs, chunks, *pieces)
 
 
 def shards(tokens, gains, qkv_weight, out_weight, gate_weight, up_weight, down_weight, cotangent):
@@ -666,21 +690,22 @@
         count = grad.shape[1] // cols
         grad = jnp.transpose(grad.reshape(grad.shape[0], count, cols), (1, 0, 2))
         grad = grad.reshape(count // ctx_count, ctx_count, -1, cols)
-        here = reduce_blocks(grad, "shard", 0) if base is None else reduce_to(grad, "shard", base)
-        return reduce_blocks(here, "ctx", 0)
-
-    def deliver(home, kind):
-        stacked = jnp.concatenate(
-            [part for seq_rows in spread(home, "seq") for part in spread(seq_rows, "sub")]
-        )
+        return reduce_blocks(grad, "shard", 0) if base is None else reduce_to(grad, "shard", base)
+
+    def exchange(home):
+        far = [spread(rows, "seq") for rows in home]
+        return [part for rows in far for seq_rows in rows for part in spread(seq_rows, "sub")]
+
+    def deliver(pieces, kind):
         seqs, chunks = [], []
-        for seq_ahead in range(seq_count):
-            for sub_ahead in range(sub_count):
-                sub = (own_sub + sub_ahead) % sub_count
-                seqs += [(own_seq + seq_ahead) % seq_count] * 2
-                chunks += [sub, 2 * sub_count - 1 - sub]
+        for moved in range(2):
+            for seq_ahead in range(seq_count):
+                for sub_ahead in range(sub_count):
+                    sub = (own_sub + sub_ahead) % sub_count
+                    seqs.append((own_seq + seq_ahead) % seq_count)
+                    chunks.append(2 * sub_count - 1 - sub if moved else sub)
         placed = place_rows(
-            stacked,
+            pieces,
             jnp.stack(seqs).astype(jnp.int32),
             jnp.stack(chunks).astype(jnp.int32),
             seq_count,
@@ -693,7 +718,7 @@
         low, high = columns[:, :chunk], columns[:, chunk:]
         kept = jnp.where(is_low, low, high)
         moved = swap_ends(jnp.where(is_low, high, low))
-        return jnp.stack([kept, moved])
+        return [kept, moved]
 
     tile_rows, tile_cols = qkv_weight.shape
     gain_part = gains.shape[1]
@@ -722,7 +747,10 @@
     kept_tokens, moved_tokens = take_rows(tokens)
     kept_cot, moved_cot = take_rows(cotangent)
     rows_low = in_order(kept_tokens, swap_ends(moved_tokens))
+    cot = in_order(kept_cot, swap_ends(moved_cot.astype(jnp.bfloat16)).astype(jnp.float32))
+    qkv_all, cot = lax.optimization_barrier((qkv_all, cot))
     wide = -(-width // LANES) * LANES
+    far_cots = spread(jnp.pad(cot.astype(jnp.bfloat16), ((0, 0), (0, wide - width))), "seq")
     step = jnp.arange(chunk, dtype=jnp.int32)
     positions = jnp.concatenate([own_pair * chunk + step, (2 * pair_count - 1 - own_pair) * chunk + step])
     half_dim = HEAD_DIM // 2
@@ -746,29 +774,14 @@
         qkv_flops,
     )
     query_heads = query_heads.reshape(KV_HEADS, GROUP * row_count, LANES)
-    cuts = [slice(0, 3), slice(3, KV_HEADS)]
-    pairs = []
-    for cut in cuts:
-        own_part = pair_own[cut]
-        if pairs:
-            own_part, pairs[-1] = lax.optimization_barrier((own_part, pairs[-1]))
-        pairs.append(lax.all_gather(own_part, ("ctx", "sub"), axis=1, tiled=True))
+    pair_all = lax.all_gather(pair_own, ("ctx", "sub"), axis=1, tiled=True)
+    ffn_tile = jnp.concatenate([gate_weight, up_weight, down_weight.T], axis=1)
+    pair_all, far_cots, ffn_tile = lax.optimization_barrier((pair_all, far_cots, ffn_tile))
+    ffn_all = lax.all_gather(ffn_tile, ("shard", "ctx"), axis=0, tiled=True)
     hidden_part = gate_weight.shape[1]
     place = own_pair[None]
-    first = attention_forward(place, query_heads, pairs[0], 0, ctx_count, sub_count, chunk, GROUP)
-    ffn_tile = jnp.concatenate([gate_weight, up_weight, down_weight.T], axis=1)
-    first, pairs[1], ffn_tile, moved_low = lax.optimization_barrier(
-        (first, pairs[1], ffn_tile, moved_cot.astype(jnp.bfloat16))
-    )
-    swapped_cot = swap_ends(moved_low)
-    ffn_all = lax.all_gather(ffn_tile, ("shard", "ctx"), axis=0, tiled=True)
-    second = attention_forward(
-        place, query_heads, pairs[1], cuts[1].start, ctx_count, sub_count, chunk, GROUP
-    )
-    second, swapped_cot = lax.optimization_barrier((second, swapped_cot))
-    attended = [rows.reshape((-1,) + head_rows[1:]) for rows in (first, second)]
-    cot = in_order(kept_cot, swapped_cot.astype(jnp.float32))
-    far_cots = spread(jnp.pad(cot.astype(jnp.bfloat16), ((0, 0), (0, wide - width))), "seq")
+    attended = attention_forward(place, query_heads, pair_all, ctx_count, sub_count, chunk, GROUP)
+    attended = [attended.reshape(head_rows)]
     cot_low = [spread(seq_rows, "sub") for seq_rows in far_cots]
     mix_flops = 4 * row_count * width * width
     hidden, normed_own, attn_low = row_call(
@@ -789,26 +802,27 @@
     for seq_ahead, near_rows in enumerate(far_rows):
         if seq_ahead:
             near_rows, backs[-1] = lax.optimization_barrier((near_rows, backs[-1]))
-        seq_feeds, seq_backs = [], []
-        for sub_ahead, rows in enumerate(spread(near_rows, "sub")):
-            kind = jnp.bfloat16 if sub_ahead else jnp.float32
-            cots = cot_low[seq_ahead][sub_ahead]
-            back, feed, inner, grad = row_call(
-                feed_kernel,
-                chunk,
-                [(rows, 0), (cots, 0), (ffn_all, 1)],
-                [
-                    (shape(row_count, wide, kind=kind), 0),
-                    (shape(row_count, wide, kind=kind), 0),
-                    (shape(row_count, hidden_part), 0),
-                    (shape(row_count, 2 * hidden_part), 0),
-                ],
-                "feed",
-                8 * row_count * width * 2 * hidden_part,
-            )
-            seq_feeds.append(feed)
-            seq_backs.append(back)
-            pieces.append((rows, cots, inner, grad))
+        near = list(zip(spread(near_rows, "sub"), cot_low[seq_ahead]))
+        kinds = [jnp.bfloat16 if sub_ahead else jnp.float32 for sub_ahead in range(sub_count)]
+        found = row_call(
+            functools.partial(feed_kernel, sub_count),
+            chunk,
+            [(array, 0) for both in near for array in both] + [(ffn_all, 1)],
+            [
+                (out, 0)
+                for kind in kinds
+                for out in (
+                    shape(row_count, wide, kind=kind),
+                    shape(row_count, wide, kind=kind),
+                    shape(row_count, hidden_part),
+                    shape(row_count, 2 * hidden_part),
+                )
+            ],
+            "feed",
+            8 * sub_count * row_count * width * 2 * hidden_part,
+        )
+        seq_backs, seq_feeds = found[0::4], found[1::4]
+        pieces += [both + tuple(rest) for both, *rest in zip(near, found[2::4], found[3::4])]
         backs.append(collect(seq_backs, "sub"))
         feeds.append(collect(seq_feeds, "sub"))
     backs = backs[0] + collect([backs[0]] + [total(parts) for parts in backs[1:]], "seq")[1:]
@@ -836,7 +850,7 @@
     grad_heads, feed_sent = lax.optimization_barrier((grad_heads, feed_sent))
     feeds = feeds[0] + collect([feeds[0]] + feed_sent, "seq")[1:]
     filled = attention_backward(
-        place, query_heads, grad_heads, extra, pairs[0], 0, (), ctx_count, sub_count, chunk, GROUP
+        place, query_heads, grad_heads, extra, pair_all, 0, 3, (), ctx_count, sub_count, chunk, GROUP
     )
     filled, feeds = lax.optimization_barrier((filled, feeds))
     (block_low,) = row_call(
@@ -854,8 +868,9 @@
         query_heads,
         grad_heads,
         extra,
-        pairs[1],
-        cuts[1].start,
+        pair_all,
+        3,
+        KV_HEADS,
         filled,
         ctx_count,
         sub_count,
@@ -885,13 +900,12 @@
     )
     early_grad = early_grad.reshape(seq_count, sub_count, tile_rows, early_grad.shape[1])
     early_grad = reduce_blocks(reduce_blocks(early_grad, "sub", 1), "seq", 0)
-    out_out = owner_sums(early_grad[:, :width], out_cols, None)
+    out_sums = owner_sums(early_grad[:, :width], out_cols, None)
     qkv_early = owner_sums(early_grad[:, width : width + half_cols], tile_cols, 0)
-    block_out = deliver(block_home, jnp.bfloat16)
-    pair_grad, out_out, qkv_early, block_out = lax.optimization_barrier(
-        (pair_grad, out_out, qkv_early, block_out)
-    )
-    out_out = out_out.astype(jnp.float32)
+    pair_grad, out_sums, qkv_early, block_pieces = lax.optimization_barrier(
+        (pair_grad, out_sums, qkv_early, exchange(block_home))
+    )
+    block_out = deliver(block_pieces, jnp.bfloat16)
     proj_grad, input_low, gain_one_grad = row_call(
         finish_kernel,
         chunk,
@@ -913,7 +927,7 @@
         "finish",
         qkv_flops,
     )
-    input_grad = deliver(back_home(input_low), jnp.float32)
+    input_grad = deliver(exchange(back_home(input_low)), jnp.float32)
 
     late_cols = qkv_cols - half_cols
     qkv_grad = matmul("rd,re->de", normed, proj_grad[:, half_cols:qkv_cols]).astype(jnp.bfloat16)
@@ -932,20 +946,25 @@
     )
     last = reduce_blocks(reduce_blocks(last, "sub", 1), "seq", 0)
     gains_sum = last[tile_rows : tile_rows + 2 * folded].reshape(2, folded * late_cols)[:, :width]
-    gains_out = reduce_blocks(
-        reduce_blocks(
-            jnp.transpose(gains_sum.reshape(2, owners, gain_part), (1, 0, 2)).reshape(
-                owners // ctx_count, ctx_count, 2, gain_part
-            ),
-            "shard",
-            0,
-        ),
-        "ctx",
-        0,
-    ).astype(jnp.float32)
+    gains_tiles = jnp.transpose(gains_sum.reshape(2, owners, gain_part), (1, 0, 2))
+    gains_tiles = reduce_blocks(
+        gains_tiles.reshape(owners // ctx_count, ctx_count, 2, gain_part), "shard", 0
+    )
     qkv_late = owner_sums(last[:tile_rows], tile_cols, owners // ctx_count // 2)
     is_early = lax.axis_index("shard") < owners // ctx_count // 2
-    qkv_out = jnp.where(is_early, qkv_early, qkv_late).astype(jnp.float32)
+    qkv_sums = jnp.where(is_early, qkv_early, qkv_late)
+    final = jnp.concatenate(
+        [
+            jnp.concatenate(
+                [out_sums, jnp.pad(gains_tiles, ((0, 0), (0, extra_rows - 2), (0, 0)))], axis=1
+            ),
+            jnp.pad(qkv_sums, ((0, 0), (0, extra_rows), (0, 0))),
+        ],
+        axis=2,
+    )
+    final = reduce_blocks(final, "ctx", 0).astype(jnp.float32)
+    gains_out = final[tile_rows : tile_rows + 2, :gain_part]
+    out_out, qkv_out = final[:tile_rows, :out_cols], final[:tile_rows, out_cols:]
     ffn_out = ffn_out.astype(jnp.float32)
     return (
         block_out,

time: 630 us -> 583 us (0.925)
  waiting for transfers between devices: 195 us -> 173 us
  starting transfers between devices: 78 us -> 58.5 us
  local copies, waits for them, and re-layouts: 58.1 us -> 74.8 us
  Pallas kernels: 226 us -> 211 us
  other arithmetic: 42.8 us -> 33.9 us
    all_gather x1, waiting for transfers between devices: 34.4 us -> 4.34 us  [shards(): ffn_all = lax.all_gather(ffn_tile, ('shard', 'ctx'), axis=0, tiled=True)]
    ppermute x42 -> x39, starting transfers between devices: 61.8 us -> 40.3 us  [pull(): lax.ppermute(values, axis, [((i + ahead) % count, i) for i in range(count)])]
    all_gather x1, waiting for transfers between devices: 15.8 us -> 28.6 us  [shards(): first_all = lax.all_gather(first_tile, everyone, axis=0, tiled=False)]
    pallas_call x10 -> x8, Pallas kernels: 79.1 us -> 68.5 us  [row_call(): pl.pallas_call(kernel, grid=(2,), in_specs=[whole(a.shape) if fixed else...]
    ppermute x42 -> x39, waiting for transfers between devices: 87.8 us -> 97.2 us  [pull(): lax.ppermute(values, axis, [((i + ahead) % count, i) for i in range(count)])]
    all_gather x2 -> x1, waiting for transfers between devices: 35.6 us -> 28.1 us  [shards(): pair_all = lax.all_gather(pair_own, ('ctx', 'sub'), axis=1, tiled=True)]
    reshape x2, local copies, waits for them, and re-layouts: 2.01 us -> 9.47 us  [shards(): qkv_grad.reshape(seq_count, sub_count, tile_rows, late_cols)]
    pallas_call x2 -> x1, Pallas kernels: 49.8 us -> 49.4 us  [attention_forward(): pl.pallas_call(functools.partial(forward_kernel, ctx_count, sub, chunk, g...]
  transfers between devices with their start and end apart: 54 -> 50, of which waited for: 26 -> 22; matrix products, arithmetic and copies ran while one was open for 12% -> 12% of each run, Pallas kernels for 31% -> 31%
where the time goes in v3:
time: 583 us; the launch traced here: 574 us
  Pallas kernels  211 us (36%)
  waiting for transfers between devices  173 us (30%)
  local copies, waits for them, and re-layouts  74.8 us (13%)
  starting transfers between devices  58.5 us (10%)
  other arithmetic  33.9 us (6%)
  between operations  15 us (3%)
  matrix products  7.79 us (1%)
    ppermute x39, waiting for transfers between devices, pull(): lax.ppermute(values, axis, [((i + ahead) % count, i) for i in range(count)])  97.2 us
    pallas_call x8, Pallas kernels, row_call(): pl.pallas_call(kernel, grid=(2,), in_specs=[whole(a.shape) if fixed else...  68.5 us
    pallas_call x2, Pallas kernels, attention_backward(): pl.pallas_call(filling if filled else kernel, out_shape=(jax.ShapeDtypeSt...  62.5 us
    pallas_call x1, Pallas kernels, attention_forward(): pl.pallas_call(functools.partial(forward_kernel, ctx_count, sub, chunk, g...  49.4 us
    ppermute x39, starting transfers between devices, pull(): lax.ppermute(values, axis, [((i + ahead) % count, i) for i in range(count)])  40.3 us
    all_gather x1, waiting for transfers between devices, shards(): first_all = lax.all_gather(first_tile, everyone, axis=0, tiled=False)  28.6 us
    all_gather x1, waiting for transfers between devices, shards(): pair_all = lax.all_gather(pair_own, ('ctx', 'sub'), axis=1, tiled=True)  28.1 us
    unnamed x82, local copies, waits for them, and re-layouts  20.6 us
  transfers between devices with their start and end apart: 50, of which 22 were waited for; matrix products, arithmetic and copies ran while one was open for 12% of the time, Pallas kernels for 31%

profile of v3, /device:TPU:0, one launch (start us, length us, event | category | flops | bytes accessed | tf_op | source)
XLA Modules:
  0.0 574.0 jit_solution(5091287334932121066)
XLA Ops:
  9.7 5.1 collective-permute-start.1
  33.9 9.7 %collective-permute-done.5 = bf16[2,4,240,120]{3,2,1,0:T(8,128)(2,1)S(1)} collective-permute-done((bf16[2,4,240,120]{3,2,1,0:T(8,128)(2,1)S(1)}, bf16[2,4,240,120]{3,2,1,0:T(8,128)(2,1)S(1)}, u32[]{:S(2)}, u32[]{:S(2)}) %collective-permute-start.5) | collective-permute-done | bytes 460832 | tf_op jit(solution)/shard_map/ppermute | solution.py:583
  56.6 5.3 reshape.129
  61.9 4.1 pad.29.refs_1_.refs_7_
  66.0 28.6 %all-gather.10.cloned.1.call-done = bf16[32,242,200]{1,2,0:T(8,128)(2,1)} async-done(((bf16[1,242,200]{1,2,0:T(8,128)(2,1)}), bf16[32,242,200]{1,2,0:T(8,128)(2,1)}) %all-gather.10.cloned.1.call-update) | async-done | bytes 3097616 | tf_op jit(solution)/shard_map/all_gather | solution.py:728
  94.7 6.1 %copy.76.in_ref = bf16[32,242,200]{2,1,0:T(8,128)(2,1)} copy(bf16[32,242,200]{1,2,0:T(8,128)(2,1)} %all-gather.10.cloned.1.call-done) | data formatting | bytes 6195200 | tf_op jit(solution)/shard_map/all_gather | solution.py:728
  108.1 6.7 %project.1 = (bf16[5,2,3,256,128]{4,3,2,1,0:T(8,128)(2,1)}, bf16[5,512,128]{2,1,0:T(8,128)(2,1)}, bf16[512,960]{1,0:T(8,128)(2,1)}) custom-call(bf16[512,960]{1,0:T(8,128)(2,1)} %maximum_select_fusion.1.token_ref.refs_2_, f32[1,960]{1,0:T(1,128)} %squeeze.60.gain_ref, bf16[960,1664]{1,0:T(8,128)(2,1)} %copy-done.1, f32[512,128]{1,0:T(8,128)} %pad_maximum_fusion.2.cos_ref, ...), custom_call_target="tpu_custom_call" | custom-call | flops 1635778560 | bytes 8310528 | tf_op jit(solution)/shard_map/project/pallas_call | solution.py:364
  118.5 23.4 %collective-permute-done.8.refs_1_.refs_6_ = bf16[512,1024]{1,0:T(8,128)(2,1)} collective-permute-done((bf16[512,1024]{1,0:T(8,128)(2,1)}, bf16[512,1024]{1,0:T(8,128)(2,1)}, u32[]{:S(2)}, u32[]{:S(2)}) %collective-permute-start.8) | collective-permute-done | bytes 1048608 | tf_op jit(solution)/shard_map/ppermute | solution.py:583
  141.9 28.1 %all-gather.6.cloned.1.call-done.kv_ref = bf16[5,4096,128]{2,1,0:T(8,128)(2,1)} async-done(((bf16[5,512,128]{2,1,0:T(8,128)(2,1)}), bf16[5,4096,128]{2,1,0:T(8,128)(2,1)}) %all-gather.6.cloned.1.call-update) | async-done | bytes 5242896 | tf_op jit(solution)/shard_map/all_gather | solution.py:777
  170.7 49.4 %attention_forward.1 = f32[5,1536,128]{2,1,0:T(8,128)S(1)} custom-call(s32[1]{0:T(128)} %bitcast.6.pair_ref, bf16[5,1536,128]{2,1,0:T(8,128)(2,1)S(1)} %bitcast.115, bf16[5,4096,128]{2,1,0:T(8,128)(2,1)} %all-gather.6.cloned.1.call-done.kv_ref), custom_call_target="tpu_custom_call" | custom-call | flops 4026531840 | bytes 11141120 | tf_op jit(solution)/shard_map/attention_forward/pallas_call | solution.py:140
  222.1 7.0 %mix.1 = (f32[512,960]{1,0:T(8,128)}, bf16[512,1024]{1,0:T(8,128)(2,1)}, bf16[512,960]{1,0:T(8,128)(2,1)}) custom-call(f32[5,2,3,256,128]{4,3,2,1,0:T(8,128)} %bitcast.113, bf16[15,128,960]{2,1,0:T(8,128)(2,1)} %pad.29.refs_1_.refs_7_, bf16[512,960]{1,0:T(8,128)(2,1)} %maximum_select_fusion.1.token_ref.refs_2_, f32[1,960]{1,0:T(1,128)} %squeeze.61.refs_3_.refs_6_), custom_call_target="tpu_custom_call" | custom-call | flops 1887436800 | bytes 12603136 | tf_op jit(solution)/shard_map/mix/pallas_call | solution.py:364
  233.5 4.3 all-gather.8.cloned.1.call-done.refs_4_
  237.9 13.4 %feed.2 = (f32[512,1024]{1,0:T(8,128)}, f32[512,1024]{1,0:T(8,128)}, bf16[512,640]{1,0:T(8,128)(2,1)}, bf16[512,1280]{1,0:T(8,128)(2,1)}, bf16[512,1024]{1,0:T(8...) custom-call(bf16[512,1024]{1,0:T(8,128)(2,1)} %get-tuple-element.91.refs_0_, ...), custom_call_target="tpu_custom_call" | custom-call | flops 10066329600 | bytes 18104320 | tf_op jit(solution)/shard_map/feed/pallas_call | solution.py:364
  259.0 13.3 %feed.3 = (f32[512,1024]{1,0:T(8,128)}, f32[512,1024]{1,0:T(8,128)}, bf16[512,640]{1,0:T(8,128)(2,1)}, bf16[512,1280]{1,0:T(8,128)(2,1)}, bf16[512,1024]{1,0:T(8...) custom-call(bf16[512,1024]{1,0:T(8,128)(2,1)} %collective-permute-done.9.refs_0_.refs_2_,, ...), custom_call_target="tpu_custom_call" | custom-call | flops 10066329600 | bytes 18104320 | tf_op jit(solution)/shard_map/feed/pallas_call | solution.py:364
  279.6 16.5 %weight_grads.1 = bf16[960,1920]{1,0:T(8,128)(2,1)} custom-call(bf16[512,1024]{1,0:T(8,128)(2,1)} %get-tuple-element.91.refs_0_, bf16[512,1024]{1,0:T(8,128)(2,1)} %collective-permute-done.10.refs_2_.refs_1_, bf16[512,1024]{1,0:T(8,128)(2,1)} %collective-permute-done.9.refs_0_.refs_2_, bf16[512,1024]{1,0:T(8,128)(2,1)} %copy-done.33, ...), custom_call_target="tpu_custom_call" | custom-call | flops 7549747200 | bytes 19415040 | tf_op jit(solution)/shard_map/weight_grads/pallas_call | solution.py:561
  296.1 7.6 %collective-permute-done.16.refs_2_ = bf16[512,1024]{1,0:T(8,128)(2,1)} collective-permute-done((bf16[512,1024]{1,0:T(8,128)(2,1)}, bf16[512,1024]{1,0:T(8,128)(2,1)}, u32[]{:S(2)}, u32[]{:S(2)}) %collective-permute-start.16) | collective-permute-done | bytes 1048608 | tf_op jit(solution)/shard_map/ppermute | solution.py:583
  308.6 10.0 %unmix.1 = (f32[512,960]{1,0:T(8,128)}, bf16[512,960]{1,0:T(8,128)(2,1)}, bf16[5,2,3,256,128]{4,3,2,1,0:T(8,128)(2,1)}, bf16[5,2,3,256,128]{4,3,2,1,0:T(8,128)(2,1)}, f32[8,960]{1,0:T(8,128)}) custom-call(f32[512,1024]{1,0:T(8,128)} %get-tuple-element.110.refs_0_, bf16[512,1024]{1,0:T(8,128)(2,1)} %collective-permute-done.12.refs_1_, ...), custom_call_target="tpu_custom_call" | custom-call | flops 1887436800 | bytes 22660864 | tf_op jit(solution)/shard_map/unmix/pallas_call | solution.py:364
  323.6 36.9 %attention_backward.2 = (f32[5,1536,128]{2,1,0:T(8,128)}, bf16[5,4096,128]{2,1,0:T(8,128)(2,1)}) custom-call(s32[1]{0:T(128)} %bitcast.6.pair_ref, bf16[5,1536,128]{2,1,0:T(8,128)(2,1)S(1)} %bitcast.116, bf16[5,1536,128]{2,1,0:T(8,128)(2,1)S(1)} %bitcast.118, bf16[5,1536,128]{2,1,0:T(8,128)(2,1)S(1)} %bitcast.120, ...), custom_call_target="tpu_custom_call" | custom-call | flops 6039797760 | bytes 12189696 | tf_op jit(solution)/shard_map/attention_backward/pallas_call | solution.py:244
  361.8 4.2 block.1
  367.4 7.7 %collective-permute-start.20 = (bf16[960,256]{1,0:T(8,128)(2,1)S(1)}, bf16[960,256]{1,0:T(8,128)(2,1)S(1)}, u32[]{:S(2)}, u32[]{:S(2)}) collective-permute-start(bf16[960,256]{1,0:T(8,128)(2,1)S(1)} %get-tuple-element.206), channel_id=1, source_target_pairs={{0,12},{4,8},{8,4},{12,0},{1,13},{5,9},{9,5},{13,1},{2,14},{6,10},... | collective-permute-start | bytes 1474568 | tf_op jit(solution)/shard_map/ppermute | solution.py:588
  375.1 25.6 %attention_backward.3 = (f32[5,1536,128]{2,1,0:T(8,128)}, bf16[5,4096,128]{2,1,0:T(8,128)(2,1)}) custom-call(s32[1]{0:T(128)} %bitcast.6.pair_ref, bf16[5,1536,128]{2,1,0:T(8,128)(2,1)S(1)} %bitcast.117, bf16[5,1536,128]{2,1,0:T(8,128)(2,1)S(1)} %bitcast.119, bf16[5,1536,128]{2,1,0:T(8,128)(2,1)S(1)} %bitcast.121, ...), custom_call_target="tpu_custom_call", output_to_operand_aliasing={{0}: (5, {}), {1}: (6, {})} | custom-call | flops 4026531840 | bytes 8126464 | tf_op jit(solution)/shard_map/attention_backward/pallas_call | solution.py:244
  400.7 6.6 %reduce-scatter.7.cloned.1.call-done = bf16[120,1920]{1,0:T(8,128)(2,1)} async-done(((bf16[960,1920]{1,0:T(8,128)(2,1)}), bf16[120,1920]{1,0:T(8,128)(2,1)}) %reduce-scatter.7.cloned.1.call-update) | async-done | bytes 460816 | tf_op jit(solution)/shard_map/optimization_barrier | solution.py:880
  407.4 4.7 early.1
  430.2 20.8 %collective-permute-done.22 = bf16[240,1856]{1,0:T(8,128)(2,1)} collective-permute-done((bf16[240,1856]{1,0:T(8,128)(2,1)S(1)}, bf16[240,1856]{1,0:T(8,128)(2,1)}, u32[]{:S(2)}, u32[]{:S(2)}) %collective-permute-start.22) | collective-permute-done | bytes 890912 | tf_op jit(solution)/shard_map/ppermute | solution.py:583
  463.2 8.0 %collective-permute-done.29.refs_6_ = bf16[960,256]{1,0:T(8,128)(2,1)S(1)} collective-permute-done((bf16[960,256]{1,0:T(8,128)(2,1)S(1)}, bf16[960,256]{1,0:T(8,128)(2,1)S(1)}, u32[]{:S(2)}, u32[]{:S(2)}) %collective-permute-start.29) | collective-permute-done | bytes 491552 | tf_op jit(solution)/shard_map/ppermute | solution.py:583
  477.0 9.2 %finish.1 = (bf16[512,1664]{1,0:T(8,128)(2,1)}, bf16[960,512]{1,0:T(8,128)(2,1)}, f32[8,960]{1,0:T(8,128)}) custom-call(f32[5,2,3,256,128]{4,3,2,1,0:T(8,128)} %bitcast.123, bf16[5,512,128]{2,1,0:T(8,128)(2,1)} %reduce-scatter.5.cloned.1.call-done.dkv_ref, f32[512,128]{1,0:T(8,128)} %pad_maximum_fusion.2.cos_ref, f32[512,128]{1,0:T(8,128)} %pad_maximum_fusion.3.sin_ref, ...), custom_call_target="tpu_custom_call" | custom-call | flops 1635778560 | bytes 13977344 | tf_op jit(solution)/shard_map/finish/pallas_call | solution.py:364
  491.3 7.8 %reshape.139 = bf16[2,2,240,800]{2,1,0,3:T(2,128)(2,1)} reshape(bf16[960,800]{0,1:T(8,128)(2,1)} %convolution_convert_fusion.2) | data formatting | bytes 3072000 | tf_op jit(solution)/shard_map/reshape | solution.py:942
  509.8 8.3 %collective-permute-done.34.refs_4_ = bf16[960,256]{1,0:T(8,128)(2,1)} collective-permute-done((bf16[960,256]{1,0:T(8,128)(2,1)}, bf16[960,256]{1,0:T(8,128)(2,1)}, u32[]{:S(2)}, u32[]{:S(2)}) %collective-permute-start.34) | collective-permute-done | bytes 491552 | tf_op jit(solution)/shard_map/ppermute | solution.py:588
  533.8 6.3 %collective-permute-done.36.refs_6_ = bf16[960,256]{1,0:T(8,128)(2,1)} collective-permute-done((bf16[960,256]{1,0:T(8,128)(2,1)}, bf16[960,256]{1,0:T(8,128)(2,1)}, u32[]{:S(2)}, u32[]{:S(2)}) %collective-permute-start.36) | collective-permute-done | bytes 491552 | tf_op jit(solution)/shard_map/ppermute | solution.py:583
  541.1 8.2 %collective-permute-start.42 = (bf16[256,320]{0,1:T(8,128)(2,1)S(1)}, bf16[256,320]{0,1:T(8,128)(2,1)S(1)}, u32[]{:S(2)}, u32[]{:S(2)}) collective-permute-start(bf16[256,320]{0,1:T(8,128)(2,1)S(1)} %get-tuple-element.208), channel_id=1, source_target_pairs={{12,0},{0,4},{4,8},{8,12},{13,1},{1,5},{5,9},{9,13},{14,2},{2,6},{... | collective-permute-start | bytes 491528 | tf_op jit(solution)/shard_map/ppermute | solution.py:583
  554.3 4.1 place_rows.2
  558.4 6.3 %place_rows.3 = f32[2,960,1024]{2,1,0:T(8,128)} custom-call(s32[8]{0:T(128)S(1)} %stack.38.seq_ref, s32[8]{0:T(128)S(1)} %stack.43.chunk_ref, bf16[960,256]{1,0:T(8,128)(2,1)S(1)} %get-tuple-element.205.refs_0_, bf16[960,256]{1,0:T(8,128)(2,1)S(1)} %collective-permute-done.31.refs_1_, bf16[960,256]{1,0:T(8,128)(2,1)} %collective-permute-done.32.refs_2_, ...), custom_call_target="tpu_custom_call" | custom-call | tf_op jit(solution)/shard_map/place_rows/pallas_call | solution.py:649
  (256 shorter events, 155.6 us)
Async XLA Ops:
  7.2 87.5 %all-gather.10.cloned.1.call-start = ((), (), s32[]{:S(2)}) async-start(), calls=%async_computation.5 | async-start | bytes 3379200 | tf_op jit(solution)/shard_map/all_gather | solution.py:728
  9.6 160.3 %all-gather.6.cloned.1.call-start = ((), (), s32[]{:S(2)}) async-start(), calls=%async_computation.2 | async-start | bytes 5898240 | tf_op jit(solution)/shard_map/all_gather | solution.py:777
  9.7 14.1 %collective-permute-start.1 = (bf16[240,120]{1,0:T(8,128)(2,1)}, bf16[240,120]{1,0:T(8,128)(2,1)S(1)}, u32[]{:S(2)}, u32[]{:S(2)}) collective-permute-start(bf16[240,120]{1,0:T(8,128)(2,1)} %param.11), channel_id=1, source_target_pairs={{4,0},{8,4},{12,8},{0,12},{5,1},{9,5},{13,9},{1,13},{6,2},{10,6},{... | collective-permute-start | bytes 172808 | tf_op jit(solution)/shard_map/ppermute | solution.py:583
  19.0 28.7 %collective-permute-start.7 = (bf16[256,960]{1,0:T(8,128)(2,1)}, bf16[256,960]{1,0:T(8,128)(2,1)S(1)}, u32[]{:S(2)}, u32[]{:S(2)}) collective-permute-start(bf16[256,960]{1,0:T(8,128)(2,1)} %bitcast.103), channel_id=1, source_target_pairs={{0,12},{4,8},{8,4},{12,0},{1,13},{5,9},{9,5},{13,1},{2,14},{6,10},... | collective-permute-start | bytes 1474568 | tf_op jit(solution)/shard_map/ppermute | solution.py:588
  22.8 25.0 %collective-permute-start = (bf16[256,960]{1,0:T(8,128)(2,1)}, bf16[256,960]{1,0:T(8,128)(2,1)}, u32[]{:S(2)}, u32[]{:S(2)}) collective-permute-start(bf16[256,960]{1,0:T(8,128)(2,1)} %bitcast.8), channel_id=1, source_target_pairs={{0,12},{4,8},{8,4},{12,0},{1,13},{5,9},{9,5},{13,1},{2,14},{6,10},... | collective-permute-start | bytes 1474568 | tf_op jit(solution)/shard_map/ppermute | solution.py:588
  114.9 122.9 %all-gather.8.cloned.1.call-start = ((), (), s32[]{:S(2)}) async-start(), calls=%async_computation.3 | async-start | bytes 4147200 | tf_op jit(solution)/shard_map/all_gather | solution.py:780
  116.2 25.6 %collective-permute-start.8 = (bf16[512,1024]{1,0:T(8,128)(2,1)}, bf16[512,1024]{1,0:T(8,128)(2,1)}, u32[]{:S(2)}, u32[]{:S(2)}) collective-permute-start(bf16[512,1024]{1,0:T(8,128)(2,1)} %pad.30.refs_1_.refs_4_), channel_id=1, source_target_pairs={{2,0},{0,2},{3,1},{1,3},{6,4},{4,6},{7,5},{5,7},{10,8},{8,10},{11,... | collective-permute-start | bytes 3145736 | tf_op jit(solution)/shard_map/ppermute | solution.py:583
  170.0 237.4 %reduce-scatter.7.cloned.1.call-start = ((), (), s32[]{:S(2)}) async-start(), calls=%async_computation.6 | async-start | bytes 4147200
  229.6 25.4 %collective-permute-start.9 = (bf16[512,1024]{1,0:T(8,128)(2,1)}, bf16[512,1024]{1,0:T(8,128)(2,1)}, u32[]{:S(2)}, u32[]{:S(2)}) collective-permute-start(bf16[512,1024]{1,0:T(8,128)(2,1)} %get-tuple-element.91.refs_0_), channel_id=1, source_target_pairs={{2,0},{0,2},{3,1},{1,3},{6,4},{4,6},{7,5},{5,7},{10,8},{8,10},{11,... | collective-permute-start | bytes 3145736 | tf_op jit(solution)/shard_map/ppermute | solution.py:583
  278.2 25.5 %collective-permute-start.16 = (bf16[512,1024]{1,0:T(8,128)(2,1)}, bf16[512,1024]{1,0:T(8,128)(2,1)}, u32[]{:S(2)}, u32[]{:S(2)}) collective-permute-start(bf16[512,1024]{1,0:T(8,128)(2,1)} %add_convert_fusion.1), channel_id=1, source_target_pairs={{2,0},{0,2},{3,1},{1,3},{6,4},{4,6},{7,5},{5,7},{10,8},{8,10},{11,... | collective-permute-start | bytes 3145736 | tf_op jit(solution)/shard_map/ppermute | solution.py:583
  303.7 173.2 %reduce-scatter.5.cloned.1.call-start = ((), (), s32[]{:S(2)}) async-start(), calls=%async_computation.4 | async-start | bytes 5898240 | tf_op jit(solution)/shard_map/reduce_scatter | solution.py:883
  303.8 56.7 %collective-permute-start.18 = (bf16[512,1024]{1,0:T(8,128)(2,1)}, bf16[512,1024]{1,0:T(8,128)(2,1)S(1)}, u32[]{:S(2)}, u32[]{:S(2)}) collective-permute-start(bf16[512,1024]{1,0:T(8,128)(2,1)} %get-tuple-element.122), channel_id=1, source_target_pairs={{1,0},{0,1},{3,2},{2,3},{5,4},{4,5},{7,6},{6,7},{9,8},{8,9},{11,10... | collective-permute-start | bytes 3145736 | tf_op jit(solution)/shard_map/ppermute | solution.py:583
  318.6 41.9 %collective-permute-start.19 = (bf16[512,1024]{1,0:T(8,128)(2,1)S(1)}, bf16[512,1024]{1,0:T(8,128)(2,1)S(1)}, u32[]{:S(2)}, u32[]{:S(2)}) collective-permute-start(bf16[512,1024]{1,0:T(8,128)(2,1)S(1)} %add_convert_fusion), channel_id=1, source_target_pairs={{2,0},{0,2},{3,1},{1,3},{6,4},{4,6},{7,5},{5,7},{10,8},{8,10},{11,... | collective-permute-start | bytes 3145736 | tf_op jit(solution)/shard_map/ppermute | solution.py:583
  367.4 33.3 %collective-permute-start.20 = (bf16[960,256]{1,0:T(8,128)(2,1)S(1)}, bf16[960,256]{1,0:T(8,128)(2,1)S(1)}, u32[]{:S(2)}, u32[]{:S(2)}) collective-permute-start(bf16[960,256]{1,0:T(8,128)(2,1)S(1)} %get-tuple-element.206), channel_id=1, source_target_pairs={{0,12},{4,8},{8,4},{12,0},{1,13},{5,9},{9,5},{13,1},{2,14},{6,10},... | collective-permute-start | bytes 1474568 | tf_op jit(solution)/shard_map/ppermute | solution.py:588
  427.6 23.5 %collective-permute-start.22 = (bf16[240,1856]{1,0:T(8,128)(2,1)S(1)}, bf16[240,1856]{1,0:T(8,128)(2,1)}, u32[]{:S(2)}, u32[]{:S(2)}) collective-permute-start(bf16[240,1856]{1,0:T(8,128)(2,1)S(1)} %dynamic-slice_bitcast_fusion.1), channel_id=1, source_target_pairs={{2,0},{0,2},{3,1},{1,3},{6,4},{4,6},{7,5},{5,7},{10,8},{8,10},{11,... | collective-permute-start | bytes 2672648 | tf_op jit(solution)/shard_map/ppermute | solution.py:583
  428.2 34.5 %collective-permute-start.26 = (bf16[960,256]{1,0:T(8,128)(2,1)S(1)}, bf16[960,256]{1,0:T(8,128)(2,1)S(1)}, u32[]{:S(2)}, u32[]{:S(2)}) collective-permute-start(bf16[960,256]{1,0:T(8,128)(2,1)S(1)} %get-tuple-element.143.refs_0_), channel_id=1, source_target_pairs={{2,0},{0,2},{3,1},{1,3},{6,4},{4,6},{7,5},{5,7},{10,8},{8,10},{11,... | collective-permute-start | bytes 1474568 | tf_op jit(solution)/shard_map/ppermute | solution.py:583
  429.7 41.5 %collective-permute-start.29 = (bf16[960,256]{1,0:T(8,128)(2,1)S(1)}, bf16[960,256]{1,0:T(8,128)(2,1)S(1)}, u32[]{:S(2)}, u32[]{:S(2)}) collective-permute-start(bf16[960,256]{1,0:T(8,128)(2,1)S(1)} %collective-permute-done.20.refs_4_), channel_id=1, source_target_pairs={{2,0},{0,2},{3,1},{1,3},{6,4},{4,6},{7,5},{5,7},{10,8},{8,10},{11,... | collective-permute-start | bytes 1474568 | tf_op jit(solution)/shard_map/ppermute | solution.py:583
  456.2 15.0 %collective-permute-start.23 = (bf16[4,240,120]{1,2,0:T(8,128)(2,1)}, bf16[4,240,120]{1,2,0:T(8,128)(2,1)}, u32[]{:S(2)}, u32[]{:S(2)}) collective-permute-start(bf16[4,240,120]{1,2,0:T(8,128)(2,1)} %dynamic-slice_bitcast_fusion.3), channel_id=1, source_target_pairs={{16,0},{0,16},{17,1},{1,17},{18,2},{2,18},{19,3},{3,19},{20,4},{4,... | collective-permute-start | bytes 691208 | tf_op jit(solution)/shard_map/ppermute | solution.py:583
  460.6 12.8 %collective-permute-start.24 = (bf16[4,240,200]{1,2,0:T(8,128)(2,1)}, bf16[4,240,200]{1,2,0:T(8,128)(2,1)}, u32[]{:S(2)}, u32[]{:S(2)}) collective-permute-start(bf16[4,240,200]{1,2,0:T(8,128)(2,1)} %bitcast.40), channel_id=1, source_target_pairs={{16,0},{17,1},{18,2},{19,3},{20,4},{21,5},{22,6},{23,7},{24,8},{25... | collective-permute-start | bytes 1152008 | tf_op jit(solution)/shard_map/ppermute | solution.py:633
  462.7 12.7 %collective-permute-start.25 = (bf16[960,256]{1,0:T(8,128)(2,1)S(1)}, bf16[960,256]{1,0:T(8,128)(2,1)S(1)}, u32[]{:S(2)}, u32[]{:S(2)}) collective-permute-start(bf16[960,256]{1,0:T(8,128)(2,1)S(1)} %get-tuple-element.143.refs_0_), channel_id=1, source_target_pairs={{1,0},{0,1},{3,2},{2,3},{5,4},{4,5},{7,6},{6,7},{9,8},{8,9},{11,10... | collective-permute-start | bytes 1474568 | tf_op jit(solution)/shard_map/ppermute | solution.py:583
  462.7 12.7 %collective-permute-start.28 = (bf16[960,256]{1,0:T(8,128)(2,1)S(1)}, bf16[960,256]{1,0:T(8,128)(2,1)S(1)}, u32[]{:S(2)}, u32[]{:S(2)}) collective-permute-start(bf16[960,256]{1,0:T(8,128)(2,1)S(1)} %collective-permute-done.20.refs_4_), channel_id=1, source_target_pairs={{1,0},{0,1},{3,2},{2,3},{5,4},{4,5},{7,6},{6,7},{9,8},{8,9},{11,10... | collective-permute-start | bytes 1474568 | tf_op jit(solution)/shard_map/ppermute | solution.py:583
  502.8 15.3 %collective-permute-start.34 = (bf16[960,256]{1,0:T(8,128)(2,1)}, bf16[960,256]{1,0:T(8,128)(2,1)}, u32[]{:S(2)}, u32[]{:S(2)}) collective-permute-start(bf16[960,256]{1,0:T(8,128)(2,1)} %get-tuple-element.204), channel_id=1, source_target_pairs={{0,12},{4,8},{8,4},{12,0},{1,13},{5,9},{9,5},{13,1},{2,14},{6,10},... | collective-permute-start | bytes 1474568 | tf_op jit(solution)/shard_map/ppermute | solution.py:588
  508.5 24.8 %collective-permute-start.32 = (bf16[960,256]{1,0:T(8,128)(2,1)S(1)}, bf16[960,256]{1,0:T(8,128)(2,1)}, u32[]{:S(2)}, u32[]{:S(2)}) collective-permute-start(bf16[960,256]{1,0:T(8,128)(2,1)S(1)} %get-tuple-element.205.refs_0_), channel_id=1, source_target_pairs={{2,0},{0,2},{3,1},{1,3},{6,4},{4,6},{7,5},{5,7},{10,8},{8,10},{11,... | collective-permute-start | bytes 1474568 | tf_op jit(solution)/shard_map/ppermute | solution.py:583
  518.1 21.9 %collective-permute-start.36 = (bf16[960,256]{1,0:T(8,128)(2,1)}, bf16[960,256]{1,0:T(8,128)(2,1)}, u32[]{:S(2)}, u32[]{:S(2)}) collective-permute-start(bf16[960,256]{1,0:T(8,128)(2,1)} %collective-permute-done.34.refs_4_), channel_id=1, source_target_pairs={{2,0},{0,2},{3,1},{1,3},{6,4},{4,6},{7,5},{5,7},{10,8},{8,10},{11,... | collective-permute-start | bytes 1474568 | tf_op jit(solution)/shard_map/ppermute | solution.py:583
  526.2 13.9 %collective-permute-start.40 = (bf16[4,2,120]{1,2,0:T(8,128)(2,1)S(1)}, bf16[4,2,120]{1,2,0:T(8,128)(2,1)S(1)}, u32[]{:S(2)}, u32[]{:S(2)}) collective-permute-start(bf16[4,2,120]{1,2,0:T(8,128)(2,1)S(1)} %dynamic-slice_bitcast_fusion.7), channel_id=1, source_target_pairs={{16,0},{0,16},{17,1},{1,17},{18,2},{2,18},{19,3},{3,19},{20,4},{4,... | collective-permute-start | bytes 5768 | tf_op jit(solution)/shard_map/ppermute | solution.py:583
  527.8 12.9 %collective-permute-start.41 = (bf16[4,240,200]{1,2,0:T(8,128)(2,1)}, bf16[4,240,200]{1,2,0:T(8,128)(2,1)S(1)}, u32[]{:S(2)}, u32[]{:S(2)}) collective-permute-start(bf16[4,240,200]{1,2,0:T(8,128)(2,1)} %bitcast.129), channel_id=1, source_target_pairs={{0,16},{1,17},{2,18},{3,19},{4,20},{5,21},{6,22},{7,23},{8,24},{9,... | collective-permute-start | bytes 1152008 | tf_op jit(solution)/shard_map/ppermute | solution.py:633
  533.2 16.1 %collective-permute-start.31 = (bf16[960,256]{1,0:T(8,128)(2,1)S(1)}, bf16[960,256]{1,0:T(8,128)(2,1)S(1)}, u32[]{:S(2)}, u32[]{:S(2)}) collective-permute-start(bf16[960,256]{1,0:T(8,128)(2,1)S(1)} %get-tuple-element.205.refs_0_), channel_id=1, source_target_pairs={{1,0},{0,1},{3,2},{2,3},{5,4},{4,5},{7,6},{6,7},{9,8},{8,9},{11,10... | collective-permute-start | bytes 1474568 | tf_op jit(solution)/shard_map/ppermute | solution.py:583
  533.3 25.1 %collective-permute-start.35 = (bf16[960,256]{1,0:T(8,128)(2,1)}, bf16[960,256]{1,0:T(8,128)(2,1)S(1)}, u32[]{:S(2)}, u32[]{:S(2)}) collective-permute-start(bf16[960,256]{1,0:T(8,128)(2,1)} %collective-permute-done.34.refs_4_), channel_id=1, source_target_pairs={{1,0},{0,1},{3,2},{2,3},{5,4},{4,5},{7,6},{6,7},{9,8},{8,9},{11,10... | collective-permute-start | bytes 1474568 | tf_op jit(solution)/shard_map/ppermute | solution.py:583
  540.1 18.3 %collective-permute-start.37 = (bf16[960,256]{1,0:T(8,128)(2,1)}, bf16[960,256]{1,0:T(8,128)(2,1)S(1)}, u32[]{:S(2)}, u32[]{:S(2)}) collective-permute-start(bf16[960,256]{1,0:T(8,128)(2,1)} %collective-permute-done.36.refs_6_), channel_id=1, source_target_pairs={{1,0},{0,1},{3,2},{2,3},{5,4},{4,5},{7,6},{6,7},{9,8},{8,9},{11,10... | collective-permute-start | bytes 1474568 | tf_op jit(solution)/shard_map/ppermute | solution.py:583
  541.1 23.7 %collective-permute-start.42 = (bf16[256,320]{0,1:T(8,128)(2,1)S(1)}, bf16[256,320]{0,1:T(8,128)(2,1)S(1)}, u32[]{:S(2)}, u32[]{:S(2)}) collective-permute-start(bf16[256,320]{0,1:T(8,128)(2,1)S(1)} %get-tuple-element.208), channel_id=1, source_target_pairs={{12,0},{0,4},{4,8},{8,12},{13,1},{1,5},{5,9},{9,13},{14,2},{2,6},{... | collective-permute-start | bytes 491528 | tf_op jit(solution)/shard_map/ppermute | solution.py:583
  549.3 15.5 %collective-permute-start.43 = (bf16[256,320]{0,1:T(8,128)(2,1)S(1)}, bf16[256,320]{0,1:T(8,128)(2,1)S(1)}, u32[]{:S(2)}, u32[]{:S(2)}) collective-permute-start(bf16[256,320]{0,1:T(8,128)(2,1)S(1)} %get-tuple-element.210), channel_id=1, source_target_pairs={{8,0},{12,4},{0,8},{4,12},{9,1},{13,5},{1,9},{5,13},{10,2},{14,6},... | collective-permute-start | bytes 491528 | tf_op jit(solution)/shard_map/ppermute | solution.py:583
  550.8 14.0 %collective-permute-start.44 = (bf16[256,320]{0,1:T(8,128)(2,1)S(1)}, bf16[256,320]{0,1:T(8,128)(2,1)S(1)}, u32[]{:S(2)}, u32[]{:S(2)}) collective-permute-start(bf16[256,320]{0,1:T(8,128)(2,1)S(1)} %get-tuple-element.209), channel_id=1, source_target_pairs={{4,0},{8,4},{12,8},{0,12},{5,1},{9,5},{13,9},{1,13},{6,2},{10,6},{... | collective-permute-start | bytes 491528 | tf_op jit(solution)/shard_map/ppermute | solution.py:583
  (53 other events, 388.3 us)
Sparse Core Ops, SparseCore 0:
  11.4 83.2 all-gather.9
  115.0 54.8 all-gather.5
  172.1 65.7 all-gather.7
  303.8 103.4 reduce-scatter.6
  410.1 62.2 reduce-scatter.4

commit v4 on v3

--- a/solution.py
+++ b/solution.py
@@ -97,16 +97,16 @@
             for head in range(heads):
                 update(start + head * chunk, chunk, kv, False, None)
 
-        twos = (last - first) // 2
-
-        @pl.loop(0, twos)
-        def _(step):
-            pair = first + 2 * step
-            absorb(jnp.concatenate([load_at(pair), load_at(pair + 1)], axis=0))
-
-        @pl.when(first + 2 * twos < last)
-        def _():
-            absorb(load_at(last - 1))
+        for size in (4, 2, 1) if count == 1 else (2, 1):
+            turns = (last - first) // size
+
+            @pl.loop(0, turns)
+            def _(step, first=first, size=size):
+                pair = first + size * step
+                found = [load_at(pair + at) for at in range(size)]
+                absorb(found[0] if size == 1 else jnp.concatenate(found, axis=0))
+
+            first = first + size * turns
 
     sweep(0, own, 1, 0, 2 * group)
     sweep(own + 1, pairs, 2, part, group)
@@ -203,26 +203,24 @@
     store(place, 1, 1, far[chunk:])
 
     def sweep(first, last, count, start, rows):
-        twos = (last - first) // 2
-
         def put(at, value):
             store(at, 0, count, value)
             if count == 1:
                 store(at, 1, 1, jnp.zeros((chunk, LANES), jnp.float32))
 
-        @pl.loop(0, twos)
-        def _(turn):
-            one = pair_place(first + 2 * turn, ctx_count, sub)
-            two = pair_place(first + 2 * turn + 1, ctx_count, sub)
-            kv = jnp.concatenate([load(one, 0, count), load(two, 0, count)], axis=0)
-            sums = step(start, rows, kv, False, None)
-            put(one, sums[: count * chunk])
-            put(two, sums[count * chunk :])
-
-        @pl.when(first + 2 * twos < last)
-        def _():
-            at = pair_place(last - 1, ctx_count, sub)
-            put(at, step(start, rows, load(at, 0, count), False, None))
+        for size in (4, 2, 1) if count == 1 else (2, 1):
+            turns = (last - first) // size
+
+            @pl.loop(0, turns)
+            def _(turn, first=first, size=size):
+                places = [pair_place(first + size * turn + at, ctx_count, sub) for at in range(size)]
+                found = [load(at, 0, count) for at in places]
+                kv = found[0] if size == 1 else jnp.concatenate(found, axis=0)
+                sums = step(start, rows, kv, False, None)
+                for at, spot in enumerate(places):
+                    put(spot, sums[at * count * chunk : (at + 1) * count * chunk])
+
+            first = first + size * turns
 
     sweep(0, own, 1, 0, 2 * part)
     sweep(own + 1, pairs, 2, part, part)
@@ -714,11 +712,9 @@
         )
         return jnp.transpose(placed, (0, 2, 1))
 
-    def back_home(columns):
+    def to_send(columns):
         low, high = columns[:, :chunk], columns[:, chunk:]
-        kept = jnp.where(is_low, low, high)
-        moved = swap_ends(jnp.where(is_low, high, low))
-        return [kept, moved]
+        return jnp.where(is_low, low, high), jnp.where(is_low, high, low)
 
     tile_rows, tile_cols = qkv_weight.shape
     gain_part = gains.shape[1]
@@ -862,7 +858,8 @@
         0,
     )
     block_low, filled = lax.optimization_barrier((block_low, filled))
-    block_home = back_home(block_low)
+    block_kept, block_moved = to_send(block_low)
+    block_home = [block_kept, swap_ends(block_moved)]
     query_grad, pair_grad = attention_backward(
         place,
         query_heads,
@@ -927,30 +924,25 @@
         "finish",
         qkv_flops,
     )
-    input_grad = deliver(exchange(back_home(input_low)), jnp.float32)
+    input_kept, input_moved = to_send(input_low)
+    input_kept, input_moved, proj_grad = lax.optimization_barrier((input_kept, input_moved, proj_grad))
+    input_moved, block_out = lax.optimization_barrier((swap_ends(input_moved), block_out))
+    input_grad = deliver(exchange([input_kept, input_moved]), jnp.float32)
 
     late_cols = qkv_cols - half_cols
     qkv_grad = matmul("rd,re->de", normed, proj_grad[:, half_cols:qkv_cols]).astype(jnp.bfloat16)
     gains_grad = jnp.concatenate([gain_one_grad[:1], gain_two_grad[:1]]).astype(jnp.bfloat16)
-    folded = -(-width // late_cols)
-    gains_rows = jnp.pad(gains_grad, ((0, 0), (0, folded * late_cols - width)))
-    gains_rows = jnp.pad(
-        gains_rows.reshape(2 * folded, late_cols), ((0, extra_rows - 2 * folded), (0, 0))
-    )
-    last = jnp.concatenate(
-        [
-            qkv_grad.reshape(seq_count, sub_count, tile_rows, late_cols),
-            jnp.broadcast_to(gains_rows, (seq_count, sub_count) + gains_rows.shape),
-        ],
-        axis=2,
-    )
+    gains_rows = jnp.pad(gains_grad, ((0, extra_rows - 2), (0, wide - width)))
+    for axis in ("sub", "seq"):
+        gains_rows = total(spread(gains_rows, axis)).astype(jnp.bfloat16)
+    gains_sum = gains_rows[:2, :width]
+    last = qkv_grad.reshape(seq_count, sub_count, tile_rows, late_cols)
     last = reduce_blocks(reduce_blocks(last, "sub", 1), "seq", 0)
-    gains_sum = last[tile_rows : tile_rows + 2 * folded].reshape(2, folded * late_cols)[:, :width]
     gains_tiles = jnp.transpose(gains_sum.reshape(2, owners, gain_part), (1, 0, 2))
     gains_tiles = reduce_blocks(
         gains_tiles.reshape(owners // ctx_count, ctx_count, 2, gain_part), "shard", 0
     )
-    qkv_late = owner_sums(last[:tile_rows], tile_cols, owners // ctx_count // 2)
+    qkv_late = owner_sums(last, tile_cols, owners // ctx_count // 2)
     is_early = lax.axis_index("shard") < owners // ctx_count // 2
     qkv_sums = jnp.where(is_early, qkv_early, qkv_late)
     final = jnp.concatenate(

time: 583 us -> 591 us (1.014)
  Pallas kernels: 211 us -> 222 us
    ppermute x39 -> x41, waiting for transfers between devices: 97.2 us -> 114 us  [pull(): lax.ppermute(values, axis, [((i + ahead) % count, i) for i in range(count)])]
    pallas_call x8, Pallas kernels: 68.5 us -> 80 us  [row_call(): pl.pallas_call(kernel, grid=(2,), in_specs=[whole(a.shape) if fixed else...]
    ppermute x4, waiting for transfers between devices: 8.35 us -> 0.01 us  [swap_ends(): lax.ppermute(values, 'ctx', [(i, count - 1 - i) for i in range(count)])]
    ppermute x39 -> x41, starting transfers between devices: 40.3 us -> 38.1 us  [pull(): lax.ppermute(values, axis, [((i + ahead) % count, i) for i in range(count)])]
    unnamed x82 -> x84, local copies, waits for them, and re-layouts: 20.6 us -> 21.8 us
  transfers between devices with their start and end apart: 50 -> 52, of which waited for: 22 -> 20; matrix products, arithmetic and copies ran while one was open for 12% -> 11% of each run, Pallas kernels for 31% -> 33%
where the time goes in v4:
time: 591 us; the launch traced here: 581 us
  Pallas kernels  222 us (38%)
  waiting for transfers between devices  173 us (29%)
  local copies, waits for them, and re-layouts  74.6 us (13%)
  starting transfers between devices  55.5 us (9%)
  other arithmetic  34.8 us (6%)
  between operations  14.9 us (3%)
  matrix products  6.3 us (1%)
    ppermute x41, waiting for transfers between devices, pull(): lax.ppermute(values, axis, [((i + ahead) % count, i) for i in range(count)])  114 us
    pallas_call x8, Pallas kernels, row_call(): pl.pallas_call(kernel, grid=(2,), in_specs=[whole(a.shape) if fixed else...  80 us
    pallas_call x2, Pallas kernels, attention_backward(): pl.pallas_call(filling if filled else kernel, out_shape=(jax.ShapeDtypeSt...  62.6 us
    pallas_call x1, Pallas kernels, attention_forward(): pl.pallas_call(functools.partial(forward_kernel, ctx_count, sub, chunk, g...  49.6 us
    ppermute x41, starting transfers between devices, pull(): lax.ppermute(values, axis, [((i + ahead) % count, i) for i in range(count)])  38.1 us
    all_gather x1, waiting for transfers between devices, shards(): first_all = lax.all_gather(first_tile, everyone, axis=0, tiled=False)  28.1 us
    all_gather x1, waiting for transfers between devices, shards(): pair_all = lax.all_gather(pair_own, ('ctx', 'sub'), axis=1, tiled=True)  28 us
    unnamed x84, local copies, waits for them, and re-layouts  21.8 us
  transfers between devices with their start and end apart: 52, of which 20 were waited for; matrix products, arithmetic and copies ran while one was open for 11% of the time, Pallas kernels for 33%

profile of v4, /device:TPU:0, one launch (start us, length us, event | category | flops | bytes accessed | tf_op | source)
XLA Modules:
  0.0 581.3 jit_solution(12170088045087806445)
XLA Ops:
  9.7 5.1 collective-permute-start.1
  34.4 9.0 %collective-permute-done.5 = bf16[2,4,240,120]{3,2,1,0:T(8,128)(2,1)S(1)} collective-permute-done((bf16[2,4,240,120]{3,2,1,0:T(8,128)(2,1)S(1)}, bf16[2,4,240,120]{3,2,1,0:T(8,128)(2,1)S(1)}, u32[]{:S(2)}, u32[]{:S(2)}) %collective-permute-start.5) | collective-permute-done | bytes 460832 | tf_op jit(solution)/shard_map/ppermute | solution.py:581
  57.4 5.1 reshape.123
  62.5 4.1 pad.25.refs_1_.refs_7_
  66.6 28.1 %all-gather.10.cloned.1.call-done = bf16[32,242,200]{1,2,0:T(8,128)(2,1)} async-done(((bf16[1,242,200]{1,2,0:T(8,128)(2,1)}), bf16[32,242,200]{1,2,0:T(8,128)(2,1)}) %all-gather.10.cloned.1.call-update) | async-done | bytes 3097616 | tf_op jit(solution)/shard_map/all_gather | solution.py:724
  96.9 6.1 %copy.73.in_ref = bf16[32,242,200]{2,1,0:T(8,128)(2,1)} copy(bf16[32,242,200]{1,2,0:T(8,128)(2,1)} %all-gather.10.cloned.1.call-done) | data formatting | bytes 6195200 | tf_op jit(solution)/shard_map/all_gather | solution.py:724
  108.1 6.8 %project.1 = (bf16[5,2,3,256,128]{4,3,2,1,0:T(8,128)(2,1)}, bf16[5,512,128]{2,1,0:T(8,128)(2,1)}, bf16[512,960]{1,0:T(8,128)(2,1)}) custom-call(bf16[512,960]{1,0:T(8,128)(2,1)} %maximum_select_fusion.1.token_ref.refs_2_, f32[1,960]{1,0:T(1,128)} %squeeze.60.gain_ref, bf16[960,1664]{1,0:T(8,128)(2,1)} %copy-done.1, f32[512,128]{1,0:T(8,128)} %pad_maximum_fusion.2.cos_ref, ...), custom_call_target="tpu_custom_call" | custom-call | flops 1635778560 | bytes 8310528 | tf_op jit(solution)/shard_map/project/pallas_call | solution.py:362
  118.5 23.4 %collective-permute-done.8.refs_1_.refs_6_ = bf16[512,1024]{1,0:T(8,128)(2,1)} collective-permute-done((bf16[512,1024]{1,0:T(8,128)(2,1)}, bf16[512,1024]{1,0:T(8,128)(2,1)}, u32[]{:S(2)}, u32[]{:S(2)}) %collective-permute-start.8) | collective-permute-done | bytes 1048608 | tf_op jit(solution)/shard_map/ppermute | solution.py:581
  141.9 28.0 %all-gather.6.cloned.1.call-done.kv_ref = bf16[5,4096,128]{2,1,0:T(8,128)(2,1)} async-done(((bf16[5,512,128]{2,1,0:T(8,128)(2,1)}), bf16[5,4096,128]{2,1,0:T(8,128)(2,1)}) %all-gather.6.cloned.1.call-update) | async-done | bytes 5242896 | tf_op jit(solution)/shard_map/all_gather | solution.py:773
  170.7 49.6 %attention_forward.1 = f32[5,1536,128]{2,1,0:T(8,128)S(1)} custom-call(s32[1]{0:T(128)} %bitcast.pair_ref, bf16[5,1536,128]{2,1,0:T(8,128)(2,1)S(1)} %bitcast.115, bf16[5,4096,128]{2,1,0:T(8,128)(2,1)} %all-gather.6.cloned.1.call-done.kv_ref), custom_call_target="tpu_custom_call" | custom-call | flops 4026531840 | bytes 11141120 | tf_op jit(solution)/shard_map/attention_forward/pallas_call | solution.py:140
  222.2 19.0 %mix.1 = (f32[512,960]{1,0:T(8,128)}, bf16[512,1024]{1,0:T(8,128)(2,1)}, bf16[512,960]{1,0:T(8,128)(2,1)}) custom-call(f32[5,2,3,256,128]{4,3,2,1,0:T(8,128)} %bitcast.113, bf16[15,128,960]{2,1,0:T(8,128)(2,1)} %pad.25.refs_1_.refs_7_, bf16[512,960]{1,0:T(8,128)(2,1)} %maximum_select_fusion.1.token_ref.refs_2_, f32[1,960]{1,0:T(1,128)} %squeeze.61.refs_3_.refs_6_), custom_call_target="tpu_custom_call" | custom-call | flops 1887436800 | bytes 12603136 | tf_op jit(solution)/shard_map/mix/pallas_call | solution.py:362
  245.8 13.2 %feed.2 = (f32[512,1024]{1,0:T(8,128)}, f32[512,1024]{1,0:T(8,128)}, bf16[512,640]{1,0:T(8,128)(2,1)}, bf16[512,1280]{1,0:T(8,128)(2,1)}, bf16[512,1024]{1,0:T(8...) custom-call(bf16[512,1024]{1,0:T(8,128)(2,1)} %get-tuple-element.96.refs_0_, ...), custom_call_target="tpu_custom_call" | custom-call | flops 10066329600 | bytes 18104320 | tf_op jit(solution)/shard_map/feed/pallas_call | solution.py:362
  259.6 7.6 %collective-permute-done.9.refs_0_.refs_2_ = bf16[512,1024]{1,0:T(8,128)(2,1)} collective-permute-done((bf16[512,1024]{1,0:T(8,128)(2,1)}, bf16[512,1024]{1,0:T(8,128)(2,1)}, u32[]{:S(2)}, u32[]{:S(2)}) %collective-permute-start.9) | collective-permute-done | bytes 1048608 | tf_op jit(solution)/shard_map/ppermute | solution.py:581
  271.1 13.3 %feed.3 = (f32[512,1024]{1,0:T(8,128)}, f32[512,1024]{1,0:T(8,128)}, bf16[512,640]{1,0:T(8,128)(2,1)}, bf16[512,1280]{1,0:T(8,128)(2,1)}, bf16[512,1024]{1,0:T(8...) custom-call(bf16[512,1024]{1,0:T(8,128)(2,1)} %collective-permute-done.9.refs_0_.refs_2_,, ...), custom_call_target="tpu_custom_call" | custom-call | flops 10066329600 | bytes 18104320 | tf_op jit(solution)/shard_map/feed/pallas_call | solution.py:362
  291.8 16.3 %weight_grads.1 = bf16[960,1920]{1,0:T(8,128)(2,1)} custom-call(bf16[512,1024]{1,0:T(8,128)(2,1)} %get-tuple-element.96.refs_0_, bf16[512,1024]{1,0:T(8,128)(2,1)} %collective-permute-done.10.refs_2_.refs_1_, bf16[512,1024]{1,0:T(8,128)(2,1)} %collective-permute-done.9.refs_0_.refs_2_, bf16[512,1024]{1,0:T(8,128)(2,1)} %copy-done.33, ...), custom_call_target="tpu_custom_call" | custom-call | flops 7549747200 | bytes 19415040 | tf_op jit(solution)/shard_map/weight_grads/pallas_call | solution.py:559
  308.1 7.7 %collective-permute-done.16.refs_2_ = bf16[512,1024]{1,0:T(8,128)(2,1)} collective-permute-done((bf16[512,1024]{1,0:T(8,128)(2,1)}, bf16[512,1024]{1,0:T(8,128)(2,1)}, u32[]{:S(2)}, u32[]{:S(2)}) %collective-permute-start.16) | collective-permute-done | bytes 1048608 | tf_op jit(solution)/shard_map/ppermute | solution.py:581
  320.8 10.0 %unmix.1 = (f32[512,960]{1,0:T(8,128)}, bf16[512,960]{1,0:T(8,128)(2,1)}, bf16[5,2,3,256,128]{4,3,2,1,0:T(8,128)(2,1)}, bf16[5,2,3,256,128]{4,3,2,1,0:T(8,128)(2,1)}, f32[8,960]{1,0:T(8,128)}) custom-call(f32[512,1024]{1,0:T(8,128)} %get-tuple-element.115.refs_0_, bf16[512,1024]{1,0:T(8,128)(2,1)} %collective-permute-done.12.refs_1_, ...), custom_call_target="tpu_custom_call" | custom-call | flops 1887436800 | bytes 22660864 | tf_op jit(solution)/shard_map/unmix/pallas_call | solution.py:362
  335.5 37.0 %attention_backward.2 = (f32[5,1536,128]{2,1,0:T(8,128)}, bf16[5,4096,128]{2,1,0:T(8,128)(2,1)}) custom-call(s32[1]{0:T(128)} %bitcast.pair_ref, bf16[5,1536,128]{2,1,0:T(8,128)(2,1)S(1)} %bitcast.116, bf16[5,1536,128]{2,1,0:T(8,128)(2,1)S(1)} %bitcast.118, bf16[5,1536,128]{2,1,0:T(8,128)(2,1)S(1)} %bitcast.120, ...), custom_call_target="tpu_custom_call" | custom-call | flops 6039797760 | bytes 12189696 | tf_op jit(solution)/shard_map/attention_backward/pallas_call | solution.py:242
  373.9 4.1 block.1
  379.4 8.6 %collective-permute-start.20 = (bf16[960,256]{1,0:T(8,128)(2,1)S(1)}, bf16[960,256]{1,0:T(8,128)(2,1)S(1)}, u32[]{:S(2)}, u32[]{:S(2)}) collective-permute-start(bf16[960,256]{1,0:T(8,128)(2,1)S(1)} %get-tuple-element.218), channel_id=1, source_target_pairs={{0,12},{4,8},{8,4},{12,0},{1,13},{5,9},{9,5},{13,1},{2,14},{6,10},... | collective-permute-start | bytes 1474568 | tf_op jit(solution)/shard_map/ppermute | solution.py:586
  388.0 25.6 %attention_backward.3 = (f32[5,1536,128]{2,1,0:T(8,128)}, bf16[5,4096,128]{2,1,0:T(8,128)(2,1)}) custom-call(s32[1]{0:T(128)} %bitcast.pair_ref, bf16[5,1536,128]{2,1,0:T(8,128)(2,1)S(1)} %bitcast.117, bf16[5,1536,128]{2,1,0:T(8,128)(2,1)S(1)} %bitcast.119, bf16[5,1536,128]{2,1,0:T(8,128)(2,1)S(1)} %bitcast.121, ...), custom_call_target="tpu_custom_call", output_to_operand_aliasing={{0}: (5, {}), {1}: (6, {})} | custom-call | flops 4026531840 | bytes 8126464 | tf_op jit(solution)/shard_map/attention_backward/pallas_call | solution.py:242
  416.7 4.5 early.1
  429.4 4.0 collective-permute-done.21
  440.7 19.4 %collective-permute-done.22 = bf16[240,1856]{1,0:T(8,128)(2,1)} collective-permute-done((bf16[240,1856]{1,0:T(8,128)(2,1)S(1)}, bf16[240,1856]{1,0:T(8,128)(2,1)}, u32[]{:S(2)}, u32[]{:S(2)}) %collective-permute-start.22) | collective-permute-done | bytes 890912 | tf_op jit(solution)/shard_map/ppermute | solution.py:581
  471.7 8.9 %collective-permute-done.29.refs_6_ = bf16[960,256]{1,0:T(8,128)(2,1)S(1)} collective-permute-done((bf16[960,256]{1,0:T(8,128)(2,1)S(1)}, bf16[960,256]{1,0:T(8,128)(2,1)S(1)}, u32[]{:S(2)}, u32[]{:S(2)}) %collective-permute-start.29) | collective-permute-done | bytes 491552 | tf_op jit(solution)/shard_map/ppermute | solution.py:581
  486.5 9.0 %finish.1 = (bf16[512,1664]{1,0:T(8,128)(2,1)}, bf16[960,512]{1,0:T(8,128)(2,1)}, f32[8,960]{1,0:T(8,128)}) custom-call(f32[5,2,3,256,128]{4,3,2,1,0:T(8,128)} %bitcast.123, bf16[5,512,128]{2,1,0:T(8,128)(2,1)} %reduce-scatter.5.cloned.1.call-done.dkv_ref, f32[512,128]{1,0:T(8,128)} %pad_maximum_fusion.2.cos_ref, f32[512,128]{1,0:T(8,128)} %pad_maximum_fusion.3.sin_ref, ...), custom_call_target="tpu_custom_call" | custom-call | flops 1635778560 | bytes 13977344 | tf_op jit(solution)/shard_map/finish/pallas_call | solution.py:362
  500.2 7.8 %reshape.135 = bf16[2,2,240,800]{2,1,0,3:T(2,128)(2,1)} reshape(bf16[960,800]{0,1:T(8,128)(2,1)} %convolution_convert_fusion.2) | data formatting | bytes 3072000 | tf_op jit(solution)/shard_map/reshape | solution.py:939
  508.1 5.4 constant_dynamic-slice_fusion.1
  525.4 4.1 place_rows.2
  542.2 9.8 %collective-permute-done.36.refs_6_ = bf16[960,256]{1,0:T(8,128)(2,1)S(1)} collective-permute-done((bf16[960,256]{1,0:T(8,128)(2,1)S(1)}, bf16[960,256]{1,0:T(8,128)(2,1)S(1)}, u32[]{:S(2)}, u32[]{:S(2)}) %collective-permute-start.36) | collective-permute-done | bytes 491552 | tf_op jit(solution)/shard_map/ppermute | solution.py:581
  559.4 6.0 %place_rows.3 = f32[2,960,1024]{2,1,0:T(8,128)} custom-call(s32[8]{0:T(128)S(1)} %stack.48.seq_ref, s32[8]{0:T(128)S(1)} %stack.103.chunk_ref, bf16[960,256]{1,0:T(8,128)(2,1)S(1)} %get-tuple-element.162.refs_0_, bf16[960,256]{1,0:T(8,128)(2,1)S(1)} %collective-permute-done.32.refs_1_, bf16[960,256]{1,0:T(8,128)(2,1)} %collective-permute-done.33.refs_2_, ...), custom_call_target="tpu_custom_call" | custom-call | tf_op jit(solution)/shard_map/place_rows/pallas_call | solution.py:647
  565.5 6.6 %collective-permute-done.45 = bf16[256,320]{0,1:T(8,128)(2,1)S(1)} collective-permute-done((bf16[256,320]{0,1:T(8,128)(2,1)S(1)}, bf16[256,320]{0,1:T(8,128)(2,1)S(1)}, u32[]{:S(2)}, u32[]{:S(2)}) %collective-permute-start.45) | collective-permute-done | bytes 163872 | tf_op jit(solution)/shard_map/ppermute | solution.py:581
  (256 shorter events, 152.9 us)
Async XLA Ops:
  7.2 87.5 %all-gather.10.cloned.1.call-start = ((), (), s32[]{:S(2)}) async-start(), calls=%async_computation.5 | async-start | bytes 3379200 | tf_op jit(solution)/shard_map/all_gather | solution.py:724
  9.6 160.3 %all-gather.6.cloned.1.call-start = ((), (), s32[]{:S(2)}) async-start(), calls=%async_computation.2 | async-start | bytes 5898240 | tf_op jit(solution)/shard_map/all_gather | solution.py:773
  9.7 14.3 %collective-permute-start.1 = (bf16[240,120]{1,0:T(8,128)(2,1)}, bf16[240,120]{1,0:T(8,128)(2,1)S(1)}, u32[]{:S(2)}, u32[]{:S(2)}) collective-permute-start(bf16[240,120]{1,0:T(8,128)(2,1)} %param.11), channel_id=1, source_target_pairs={{4,0},{8,4},{12,8},{0,12},{5,1},{9,5},{13,9},{1,13},{6,2},{10,6},{... | collective-permute-start | bytes 172808 | tf_op jit(solution)/shard_map/ppermute | solution.py:581
  18.9 29.7 %collective-permute-start = (bf16[256,960]{1,0:T(8,128)(2,1)}, bf16[256,960]{1,0:T(8,128)(2,1)}, u32[]{:S(2)}, u32[]{:S(2)}) collective-permute-start(bf16[256,960]{1,0:T(8,128)(2,1)} %bitcast.2), channel_id=1, source_target_pairs={{0,12},{4,8},{8,4},{12,0},{1,13},{5,9},{9,5},{13,1},{2,14},{6,10},... | collective-permute-start | bytes 1474568 | tf_op jit(solution)/shard_map/ppermute | solution.py:586
  22.8 24.7 %collective-permute-start.7 = (bf16[256,960]{1,0:T(8,128)(2,1)}, bf16[256,960]{1,0:T(8,128)(2,1)}, u32[]{:S(2)}, u32[]{:S(2)}) collective-permute-start(bf16[256,960]{1,0:T(8,128)(2,1)} %bitcast.103), channel_id=1, source_target_pairs={{0,12},{4,8},{8,4},{12,0},{1,13},{5,9},{9,5},{13,1},{2,14},{6,10},... | collective-permute-start | bytes 1474568 | tf_op jit(solution)/shard_map/ppermute | solution.py:586
  114.9 130.9 %all-gather.8.cloned.1.call-start = ((), (), s32[]{:S(2)}) async-start(), calls=%async_computation.3 | async-start | bytes 4147200 | tf_op jit(solution)/shard_map/all_gather | solution.py:776
  116.3 25.6 %collective-permute-start.8 = (bf16[512,1024]{1,0:T(8,128)(2,1)}, bf16[512,1024]{1,0:T(8,128)(2,1)}, u32[]{:S(2)}, u32[]{:S(2)}) collective-permute-start(bf16[512,1024]{1,0:T(8,128)(2,1)} %pad.26.refs_1_.refs_4_), channel_id=1, source_target_pairs={{2,0},{0,2},{3,1},{1,3},{6,4},{4,6},{7,5},{5,7},{10,8},{8,10},{11,... | collective-permute-start | bytes 3145736 | tf_op jit(solution)/shard_map/ppermute | solution.py:581
  170.0 246.7 %reduce-scatter.7.cloned.1.call-start = ((), (), s32[]{:S(2)}) async-start(), calls=%async_computation.6 | async-start | bytes 4147200
  241.8 25.5 %collective-permute-start.9 = (bf16[512,1024]{1,0:T(8,128)(2,1)}, bf16[512,1024]{1,0:T(8,128)(2,1)}, u32[]{:S(2)}, u32[]{:S(2)}) collective-permute-start(bf16[512,1024]{1,0:T(8,128)(2,1)} %get-tuple-element.96.refs_0_), channel_id=1, source_target_pairs={{2,0},{0,2},{3,1},{1,3},{6,4},{4,6},{7,5},{5,7},{10,8},{8,10},{11,... | collective-permute-start | bytes 3145736 | tf_op jit(solution)/shard_map/ppermute | solution.py:581
  290.3 25.5 %collective-permute-start.16 = (bf16[512,1024]{1,0:T(8,128)(2,1)}, bf16[512,1024]{1,0:T(8,128)(2,1)}, u32[]{:S(2)}, u32[]{:S(2)}) collective-permute-start(bf16[512,1024]{1,0:T(8,128)(2,1)} %add_convert_fusion.1), channel_id=1, source_target_pairs={{2,0},{0,2},{3,1},{1,3},{6,4},{4,6},{7,5},{5,7},{10,8},{8,10},{11,... | collective-permute-start | bytes 3145736 | tf_op jit(solution)/shard_map/ppermute | solution.py:581
  315.9 170.6 %reduce-scatter.5.cloned.1.call-start = ((), (), s32[]{:S(2)}) async-start(), calls=%async_computation.4 | async-start | bytes 5898240 | tf_op jit(solution)/shard_map/reduce_scatter | solution.py:880
  316.0 56.5 %collective-permute-start.18 = (bf16[512,1024]{1,0:T(8,128)(2,1)}, bf16[512,1024]{1,0:T(8,128)(2,1)S(1)}, u32[]{:S(2)}, u32[]{:S(2)}) collective-permute-start(bf16[512,1024]{1,0:T(8,128)(2,1)} %get-tuple-element.127), channel_id=1, source_target_pairs={{1,0},{0,1},{3,2},{2,3},{5,4},{4,5},{7,6},{6,7},{9,8},{8,9},{11,10... | collective-permute-start | bytes 3145736 | tf_op jit(solution)/shard_map/ppermute | solution.py:581
  330.9 41.7 %collective-permute-start.19 = (bf16[512,1024]{1,0:T(8,128)(2,1)S(1)}, bf16[512,1024]{1,0:T(8,128)(2,1)S(1)}, u32[]{:S(2)}, u32[]{:S(2)}) collective-permute-start(bf16[512,1024]{1,0:T(8,128)(2,1)S(1)} %add_convert_fusion), channel_id=1, source_target_pairs={{2,0},{0,2},{3,1},{1,3},{6,4},{4,6},{7,5},{5,7},{10,8},{8,10},{11,... | collective-permute-start | bytes 3145736 | tf_op jit(solution)/shard_map/ppermute | solution.py:581
  379.4 34.2 %collective-permute-start.20 = (bf16[960,256]{1,0:T(8,128)(2,1)S(1)}, bf16[960,256]{1,0:T(8,128)(2,1)S(1)}, u32[]{:S(2)}, u32[]{:S(2)}) collective-permute-start(bf16[960,256]{1,0:T(8,128)(2,1)S(1)} %get-tuple-element.218), channel_id=1, source_target_pairs={{0,12},{4,8},{8,4},{12,0},{1,13},{5,9},{9,5},{13,1},{2,14},{6,10},... | collective-permute-start | bytes 1474568 | tf_op jit(solution)/shard_map/ppermute | solution.py:586
  436.7 23.4 %collective-permute-start.22 = (bf16[240,1856]{1,0:T(8,128)(2,1)S(1)}, bf16[240,1856]{1,0:T(8,128)(2,1)}, u32[]{:S(2)}, u32[]{:S(2)}) collective-permute-start(bf16[240,1856]{1,0:T(8,128)(2,1)S(1)} %dynamic-slice_bitcast_fusion.1), channel_id=1, source_target_pairs={{2,0},{0,2},{3,1},{1,3},{6,4},{4,6},{7,5},{5,7},{10,8},{8,10},{11,... | collective-permute-start | bytes 2672648 | tf_op jit(solution)/shard_map/ppermute | solution.py:581
  438.7 32.5 %collective-permute-start.26 = (bf16[960,256]{1,0:T(8,128)(2,1)S(1)}, bf16[960,256]{1,0:T(8,128)(2,1)S(1)}, u32[]{:S(2)}, u32[]{:S(2)}) collective-permute-start(bf16[960,256]{1,0:T(8,128)(2,1)S(1)} %get-tuple-element.153.refs_0_), channel_id=1, source_target_pairs={{2,0},{0,2},{3,1},{1,3},{6,4},{4,6},{7,5},{5,7},{10,8},{8,10},{11,... | collective-permute-start | bytes 1474568 | tf_op jit(solution)/shard_map/ppermute | solution.py:581
  438.8 41.8 %collective-permute-start.29 = (bf16[960,256]{1,0:T(8,128)(2,1)S(1)}, bf16[960,256]{1,0:T(8,128)(2,1)S(1)}, u32[]{:S(2)}, u32[]{:S(2)}) collective-permute-start(bf16[960,256]{1,0:T(8,128)(2,1)S(1)} %collective-permute-done.20.refs_4_), channel_id=1, source_target_pairs={{2,0},{0,2},{3,1},{1,3},{6,4},{4,6},{7,5},{5,7},{10,8},{8,10},{11,... | collective-permute-start | bytes 1474568 | tf_op jit(solution)/shard_map/ppermute | solution.py:581
  465.3 15.2 %collective-permute-start.23 = (bf16[4,240,120]{1,2,0:T(8,128)(2,1)}, bf16[4,240,120]{1,2,0:T(8,128)(2,1)}, u32[]{:S(2)}, u32[]{:S(2)}) collective-permute-start(bf16[4,240,120]{1,2,0:T(8,128)(2,1)} %dynamic-slice_bitcast_fusion.3), channel_id=1, source_target_pairs={{16,0},{0,16},{17,1},{1,17},{18,2},{2,18},{19,3},{3,19},{20,4},{4,... | collective-permute-start | bytes 691208 | tf_op jit(solution)/shard_map/ppermute | solution.py:581
  469.8 13.1 %collective-permute-start.24 = (bf16[4,240,200]{1,2,0:T(8,128)(2,1)}, bf16[4,240,200]{1,2,0:T(8,128)(2,1)}, u32[]{:S(2)}, u32[]{:S(2)}) collective-permute-start(bf16[4,240,200]{1,2,0:T(8,128)(2,1)} %bitcast.34), channel_id=1, source_target_pairs={{16,0},{17,1},{18,2},{19,3},{20,4},{21,5},{22,6},{23,7},{24,8},{25... | collective-permute-start | bytes 1152008 | tf_op jit(solution)/shard_map/ppermute | solution.py:631
  471.1 13.8 %collective-permute-start.25 = (bf16[960,256]{1,0:T(8,128)(2,1)S(1)}, bf16[960,256]{1,0:T(8,128)(2,1)S(1)}, u32[]{:S(2)}, u32[]{:S(2)}) collective-permute-start(bf16[960,256]{1,0:T(8,128)(2,1)S(1)} %get-tuple-element.153.refs_0_), channel_id=1, source_target_pairs={{1,0},{0,1},{3,2},{2,3},{5,4},{4,5},{7,6},{6,7},{9,8},{8,9},{11,10... | collective-permute-start | bytes 1474568 | tf_op jit(solution)/shard_map/ppermute | solution.py:581
  471.2 13.7 %collective-permute-start.28 = (bf16[960,256]{1,0:T(8,128)(2,1)S(1)}, bf16[960,256]{1,0:T(8,128)(2,1)S(1)}, u32[]{:S(2)}, u32[]{:S(2)}) collective-permute-start(bf16[960,256]{1,0:T(8,128)(2,1)S(1)} %collective-permute-done.20.refs_4_), channel_id=1, source_target_pairs={{1,0},{0,1},{3,2},{2,3},{5,4},{4,5},{7,6},{6,7},{9,8},{8,9},{11,10... | collective-permute-start | bytes 1474568 | tf_op jit(solution)/shard_map/ppermute | solution.py:581
  514.5 18.9 %collective-permute-start.31 = (bf16[960,256]{1,0:T(8,128)(2,1)}, bf16[960,256]{1,0:T(8,128)(2,1)S(1)}, u32[]{:S(2)}, u32[]{:S(2)}) collective-permute-start(bf16[960,256]{1,0:T(8,128)(2,1)} %get-tuple-element.152), channel_id=1, source_target_pairs={{0,12},{4,8},{8,4},{12,0},{1,13},{5,9},{9,5},{13,1},{2,14},{6,10},... | collective-permute-start | bytes 1474568 | tf_op jit(solution)/shard_map/ppermute | solution.py:586
  518.3 16.8 %collective-permute-start.42 = (bf16[240,800]{0,1:T(8,128)(2,1)}, bf16[240,800]{0,1:T(8,128)(2,1)}, u32[]{:S(2)}, u32[]{:S(2)}) collective-permute-start(bf16[240,800]{0,1:T(8,128)(2,1)} %dynamic-slice_bitcast_fusion.2), channel_id=1, source_target_pairs={{2,0},{0,2},{3,1},{1,3},{6,4},{4,6},{7,5},{5,7},{10,8},{8,10},{11,... | collective-permute-start | bytes 1152008 | tf_op jit(solution)/shard_map/ppermute | solution.py:581
  520.6 21.5 %collective-permute-start.33 = (bf16[960,256]{1,0:T(8,128)(2,1)S(1)}, bf16[960,256]{1,0:T(8,128)(2,1)}, u32[]{:S(2)}, u32[]{:S(2)}) collective-permute-start(bf16[960,256]{1,0:T(8,128)(2,1)S(1)} %get-tuple-element.162.refs_0_), channel_id=1, source_target_pairs={{2,0},{0,2},{3,1},{1,3},{6,4},{4,6},{7,5},{5,7},{10,8},{8,10},{11,... | collective-permute-start | bytes 1474568 | tf_op jit(solution)/shard_map/ppermute | solution.py:581
  533.4 18.6 %collective-permute-start.36 = (bf16[960,256]{1,0:T(8,128)(2,1)S(1)}, bf16[960,256]{1,0:T(8,128)(2,1)S(1)}, u32[]{:S(2)}, u32[]{:S(2)}) collective-permute-start(bf16[960,256]{1,0:T(8,128)(2,1)S(1)} %collective-permute-done.31.refs_4_), channel_id=1, source_target_pairs={{2,0},{0,2},{3,1},{1,3},{6,4},{4,6},{7,5},{5,7},{10,8},{8,10},{11,... | collective-permute-start | bytes 1474568 | tf_op jit(solution)/shard_map/ppermute | solution.py:581
  536.4 15.6 %collective-permute-start.43 = (bf16[4,240,200]{1,2,0:T(8,128)(2,1)S(1)}, bf16[4,240,200]{1,2,0:T(8,128)(2,1)S(1)}, u32[]{:S(2)}, u32[]{:S(2)}) collective-permute-start(bf16[4,240,200]{1,2,0:T(8,128)(2,1)S(1)} %bitcast.135), channel_id=1, source_target_pairs={{0,16},{1,17},{2,18},{3,19},{4,20},{5,21},{6,22},{7,23},{8,24},{9,... | collective-permute-start | bytes 1152008 | tf_op jit(solution)/shard_map/ppermute | solution.py:631
  539.8 15.6 %collective-permute-start.32 = (bf16[960,256]{1,0:T(8,128)(2,1)S(1)}, bf16[960,256]{1,0:T(8,128)(2,1)S(1)}, u32[]{:S(2)}, u32[]{:S(2)}) collective-permute-start(bf16[960,256]{1,0:T(8,128)(2,1)S(1)} %get-tuple-element.162.refs_0_), channel_id=1, source_target_pairs={{1,0},{0,1},{3,2},{2,3},{5,4},{4,5},{7,6},{6,7},{9,8},{8,9},{11,10... | collective-permute-start | bytes 1474568 | tf_op jit(solution)/shard_map/ppermute | solution.py:581
  539.9 19.5 %collective-permute-start.35 = (bf16[960,256]{1,0:T(8,128)(2,1)S(1)}, bf16[960,256]{1,0:T(8,128)(2,1)S(1)}, u32[]{:S(2)}, u32[]{:S(2)}) collective-permute-start(bf16[960,256]{1,0:T(8,128)(2,1)S(1)} %collective-permute-done.31.refs_4_), channel_id=1, source_target_pairs={{1,0},{0,1},{3,2},{2,3},{5,4},{4,5},{7,6},{6,7},{9,8},{8,9},{11,10... | collective-permute-start | bytes 1474568 | tf_op jit(solution)/shard_map/ppermute | solution.py:581
  542.2 16.1 %collective-permute-start.34 = (bf16[960,256]{1,0:T(8,128)(2,1)}, bf16[960,256]{1,0:T(8,128)(2,1)S(1)}, u32[]{:S(2)}, u32[]{:S(2)}) collective-permute-start(bf16[960,256]{1,0:T(8,128)(2,1)} %collective-permute-done.33.refs_2_), channel_id=1, source_target_pairs={{1,0},{0,1},{3,2},{2,3},{5,4},{4,5},{7,6},{6,7},{9,8},{8,9},{11,10... | collective-permute-start | bytes 1474568 | tf_op jit(solution)/shard_map/ppermute | solution.py:581
  552.4 13.1 %collective-permute-start.46 = (bf16[256,320]{0,1:T(8,128)(2,1)S(1)}, bf16[256,320]{0,1:T(8,128)(2,1)S(1)}, u32[]{:S(2)}, u32[]{:S(2)}) collective-permute-start(bf16[256,320]{0,1:T(8,128)(2,1)S(1)} %get-tuple-element.221), channel_id=1, source_target_pairs={{4,0},{8,4},{12,8},{0,12},{5,1},{9,5},{13,9},{1,13},{6,2},{10,6},{... | collective-permute-start | bytes 491528 | tf_op jit(solution)/shard_map/ppermute | solution.py:581
  555.4 16.7 %collective-permute-start.45 = (bf16[256,320]{0,1:T(8,128)(2,1)S(1)}, bf16[256,320]{0,1:T(8,128)(2,1)S(1)}, u32[]{:S(2)}, u32[]{:S(2)}) collective-permute-start(bf16[256,320]{0,1:T(8,128)(2,1)S(1)} %get-tuple-element.222), channel_id=1, source_target_pairs={{8,0},{12,4},{0,8},{4,12},{9,1},{13,5},{1,9},{5,13},{10,2},{14,6},... | collective-permute-start | bytes 491528 | tf_op jit(solution)/shard_map/ppermute | solution.py:581
  558.3 13.9 %collective-permute-start.44 = (bf16[256,320]{0,1:T(8,128)(2,1)S(1)}, bf16[256,320]{0,1:T(8,128)(2,1)S(1)}, u32[]{:S(2)}, u32[]{:S(2)}) collective-permute-start(bf16[256,320]{0,1:T(8,128)(2,1)S(1)} %get-tuple-element.220), channel_id=1, source_target_pairs={{12,0},{0,4},{4,8},{8,12},{13,1},{1,5},{5,9},{9,13},{14,2},{2,6},{... | collective-permute-start | bytes 491528 | tf_op jit(solution)/shard_map/ppermute | solution.py:581
  (56 other events, 391.0 us)
Sparse Core Ops, SparseCore 0:
  11.4 83.2 all-gather.9
  115.0 54.8 all-gather.5
  172.1 65.8 all-gather.7
  316.0 100.6 reduce-scatter.6
  419.4 58.8 reduce-scatter.4

commit v5 on v3

--- a/solution.py
+++ b/solution.py
@@ -714,11 +714,9 @@
         )
         return jnp.transpose(placed, (0, 2, 1))
 
-    def back_home(columns):
+    def to_send(columns):
         low, high = columns[:, :chunk], columns[:, chunk:]
-        kept = jnp.where(is_low, low, high)
-        moved = swap_ends(jnp.where(is_low, high, low))
-        return [kept, moved]
+        return jnp.where(is_low, low, high), jnp.where(is_low, high, low)
 
     tile_rows, tile_cols = qkv_weight.shape
     gain_part = gains.shape[1]
@@ -862,7 +860,8 @@
         0,
     )
     block_low, filled = lax.optimization_barrier((block_low, filled))
-    block_home = back_home(block_low)
+    block_kept, block_moved = to_send(block_low)
+    block_home = [block_kept, swap_ends(block_moved)]
     query_grad, pair_grad = attention_backward(
         place,
         query_heads,
@@ -927,30 +926,25 @@
         "finish",
         qkv_flops,
     )
-    input_grad = deliver(exchange(back_home(input_low)), jnp.float32)
+    input_kept, input_moved = to_send(input_low)
+    input_kept, input_moved, proj_grad = lax.optimization_barrier((input_kept, input_moved, proj_grad))
+    input_moved, block_out = lax.optimization_barrier((swap_ends(input_moved), block_out))
+    input_grad = deliver(exchange([input_kept, input_moved]), jnp.float32)
 
     late_cols = qkv_cols - half_cols
     qkv_grad = matmul("rd,re->de", normed, proj_grad[:, half_cols:qkv_cols]).astype(jnp.bfloat16)
     gains_grad = jnp.concatenate([gain_one_grad[:1], gain_two_grad[:1]]).astype(jnp.bfloat16)
-    folded = -(-width // late_cols)
-    gains_rows = jnp.pad(gains_grad, ((0, 0), (0, folded * late_cols - width)))
-    gains_rows = jnp.pad(
-        gains_rows.reshape(2 * folded, late_cols), ((0, extra_rows - 2 * folded), (0, 0))
-    )
-    last = jnp.concatenate(
-        [
-            qkv_grad.reshape(seq_count, sub_count, tile_rows, late_cols),
-            jnp.broadcast_to(gains_rows, (seq_count, sub_count) + gains_rows.shape),
-        ],
-        axis=2,
-    )
+    gains_rows = jnp.pad(gains_grad, ((0, extra_rows - 2), (0, wide - width)))
+    for axis in ("sub", "seq"):
+        gains_rows = total(spread(gains_rows, axis)).astype(jnp.bfloat16)
+    gains_sum = gains_rows[:2, :width]
+    last = qkv_grad.reshape(seq_count, sub_count, tile_rows, late_cols)
     last = reduce_blocks(reduce_blocks(last, "sub", 1), "seq", 0)
-    gains_sum = last[tile_rows : tile_rows + 2 * folded].reshape(2, folded * late_cols)[:, :width]
     gains_tiles = jnp.transpose(gains_sum.reshape(2, owners, gain_part), (1, 0, 2))
     gains_tiles = reduce_blocks(
         gains_tiles.reshape(owners // ctx_count, ctx_count, 2, gain_part), "shard", 0
     )
-    qkv_late = owner_sums(last[:tile_rows], tile_cols, owners // ctx_count // 2)
+    qkv_late = owner_sums(last, tile_cols, owners // ctx_count // 2)
     is_early = lax.axis_index("shard") < owners // ctx_count // 2
     qkv_sums = jnp.where(is_early, qkv_early, qkv_late)
     final = jnp.concatenate(

time: 583 us -> 586 us (level)
  waiting for transfers between devices: 173 us -> 181 us
    ppermute x39 -> x41, waiting for transfers between devices: 97.2 us -> 114 us  [pull(): lax.ppermute(values, axis, [((i + ahead) % count, i) for i in range(count)])]
    ppermute x4, waiting for transfers between devices: 8.35 us -> 0.01 us  [swap_ends(): lax.ppermute(values, 'ctx', [(i, count - 1 - i) for i in range(count)])]
    ppermute x39 -> x41, starting transfers between devices: 40.3 us -> 36.8 us  [pull(): lax.ppermute(values, axis, [((i + ahead) % count, i) for i in range(count)])]
    unnamed x82 -> x84, local copies, waits for them, and re-layouts: 20.6 us -> 22.1 us
  transfers between devices with their start and end apart: 50 -> 52, of which waited for: 22 -> 23; matrix products, arithmetic and copies ran while one was open for 12% -> 11% of each run, Pallas kernels for 31% -> 31%
where the time goes in v5:
time: 586 us; the launch traced here: 577 us
  Pallas kernels  211 us (36%)
  waiting for transfers between devices  181 us (31%)
  local copies, waits for them, and re-layouts  74.7 us (13%)
  starting transfers between devices  54.7 us (9%)
  other arithmetic  34.8 us (6%)
  between operations  14.9 us (3%)
  matrix products  6.31 us (1%)
    ppermute x41, waiting for transfers between devices, pull(): lax.ppermute(values, axis, [((i + ahead) % count, i) for i in range(count)])  114 us
    pallas_call x8, Pallas kernels, row_call(): pl.pallas_call(kernel, grid=(2,), in_specs=[whole(a.shape) if fixed else...  68.6 us
    pallas_call x2, Pallas kernels, attention_backward(): pl.pallas_call(filling if filled else kernel, out_shape=(jax.ShapeDtypeSt...  62.5 us
    pallas_call x1, Pallas kernels, attention_forward(): pl.pallas_call(functools.partial(forward_kernel, ctx_count, sub, chunk, g...  49.4 us
    ppermute x41, starting transfers between devices, pull(): lax.ppermute(values, axis, [((i + ahead) % count, i) for i in range(count)])  36.8 us
    all_gather x1, waiting for transfers between devices, shards(): first_all = lax.all_gather(first_tile, everyone, axis=0, tiled=False)  28.1 us
    all_gather x1, waiting for transfers between devices, shards(): pair_all = lax.all_gather(pair_own, ('ctx', 'sub'), axis=1, tiled=True)  28 us
    unnamed x84, local copies, waits for them, and re-layouts  22.1 us
  transfers between devices with their start and end apart: 52, of which 23 were waited for; matrix products, arithmetic and copies ran while one was open for 11% of the time, Pallas kernels for 31%

profile of v5, /device:TPU:0, one launch (start us, length us, event | category | flops | bytes accessed | tf_op | source)
XLA Modules:
  0.0 577.0 jit_solution(5530661389371744343)
XLA Ops:
  9.7 5.1 collective-permute-start.1
  34.4 9.0 %collective-permute-done.5 = bf16[2,4,240,120]{3,2,1,0:T(8,128)(2,1)S(1)} collective-permute-done((bf16[2,4,240,120]{3,2,1,0:T(8,128)(2,1)S(1)}, bf16[2,4,240,120]{3,2,1,0:T(8,128)(2,1)S(1)}, u32[]{:S(2)}, u32[]{:S(2)}) %collective-permute-start.5) | collective-permute-done | bytes 460832 | tf_op jit(solution)/shard_map/ppermute | solution.py:583
  57.4 5.0 reshape.123
  62.4 4.1 pad.25.refs_1_.refs_7_
  66.5 28.1 %all-gather.10.cloned.1.call-done = bf16[32,242,200]{1,2,0:T(8,128)(2,1)} async-done(((bf16[1,242,200]{1,2,0:T(8,128)(2,1)}), bf16[32,242,200]{1,2,0:T(8,128)(2,1)}) %all-gather.10.cloned.1.call-update) | async-done | bytes 3097616 | tf_op jit(solution)/shard_map/all_gather | solution.py:726
  96.9 6.1 %copy.73.in_ref = bf16[32,242,200]{2,1,0:T(8,128)(2,1)} copy(bf16[32,242,200]{1,2,0:T(8,128)(2,1)} %all-gather.10.cloned.1.call-done) | data formatting | bytes 6195200 | tf_op jit(solution)/shard_map/all_gather | solution.py:726
  108.1 6.8 %project.1 = (bf16[5,2,3,256,128]{4,3,2,1,0:T(8,128)(2,1)}, bf16[5,512,128]{2,1,0:T(8,128)(2,1)}, bf16[512,960]{1,0:T(8,128)(2,1)}) custom-call(bf16[512,960]{1,0:T(8,128)(2,1)} %maximum_select_fusion.1.token_ref.refs_2_, f32[1,960]{1,0:T(1,128)} %squeeze.60.gain_ref, bf16[960,1664]{1,0:T(8,128)(2,1)} %copy-done.1, f32[512,128]{1,0:T(8,128)} %pad_maximum_fusion.2.cos_ref, ...), custom_call_target="tpu_custom_call" | custom-call | flops 1635778560 | bytes 8310528 | tf_op jit(solution)/shard_map/project/pallas_call | solution.py:364
  118.5 23.4 %collective-permute-done.8.refs_1_.refs_6_ = bf16[512,1024]{1,0:T(8,128)(2,1)} collective-permute-done((bf16[512,1024]{1,0:T(8,128)(2,1)}, bf16[512,1024]{1,0:T(8,128)(2,1)}, u32[]{:S(2)}, u32[]{:S(2)}) %collective-permute-start.8) | collective-permute-done | bytes 1048608 | tf_op jit(solution)/shard_map/ppermute | solution.py:583
  141.9 28.0 %all-gather.6.cloned.1.call-done.kv_ref = bf16[5,4096,128]{2,1,0:T(8,128)(2,1)} async-done(((bf16[5,512,128]{2,1,0:T(8,128)(2,1)}), bf16[5,4096,128]{2,1,0:T(8,128)(2,1)}) %all-gather.6.cloned.1.call-update) | async-done | bytes 5242896 | tf_op jit(solution)/shard_map/all_gather | solution.py:775
  170.7 49.4 %attention_forward.1 = f32[5,1536,128]{2,1,0:T(8,128)S(1)} custom-call(s32[1]{0:T(128)} %bitcast.pair_ref, bf16[5,1536,128]{2,1,0:T(8,128)(2,1)S(1)} %bitcast.115, bf16[5,4096,128]{2,1,0:T(8,128)(2,1)} %all-gather.6.cloned.1.call-done.kv_ref), custom_call_target="tpu_custom_call" | custom-call | flops 4026531840 | bytes 11141120 | tf_op jit(solution)/shard_map/attention_forward/pallas_call | solution.py:140
  222.0 7.0 %mix.1 = (f32[512,960]{1,0:T(8,128)}, bf16[512,1024]{1,0:T(8,128)(2,1)}, bf16[512,960]{1,0:T(8,128)(2,1)}) custom-call(f32[5,2,3,256,128]{4,3,2,1,0:T(8,128)} %bitcast.113, bf16[15,128,960]{2,1,0:T(8,128)(2,1)} %pad.25.refs_1_.refs_7_, bf16[512,960]{1,0:T(8,128)(2,1)} %maximum_select_fusion.1.token_ref.refs_2_, f32[1,960]{1,0:T(1,128)} %squeeze.61.refs_3_.refs_6_), custom_call_target="tpu_custom_call" | custom-call | flops 1887436800 | bytes 12603136 | tf_op jit(solution)/shard_map/mix/pallas_call | solution.py:364
  233.5 4.3 all-gather.8.cloned.1.call-done.refs_4_
  237.8 13.6 %feed.2 = (f32[512,1024]{1,0:T(8,128)}, f32[512,1024]{1,0:T(8,128)}, bf16[512,640]{1,0:T(8,128)(2,1)}, bf16[512,1280]{1,0:T(8,128)(2,1)}, bf16[512,1024]{1,0:T(8...) custom-call(bf16[512,1024]{1,0:T(8,128)(2,1)} %get-tuple-element.96.refs_0_, ...), custom_call_target="tpu_custom_call" | custom-call | flops 10066329600 | bytes 18104320 | tf_op jit(solution)/shard_map/feed/pallas_call | solution.py:364
  259.1 13.3 %feed.3 = (f32[512,1024]{1,0:T(8,128)}, f32[512,1024]{1,0:T(8,128)}, bf16[512,640]{1,0:T(8,128)(2,1)}, bf16[512,1280]{1,0:T(8,128)(2,1)}, bf16[512,1024]{1,0:T(8...) custom-call(bf16[512,1024]{1,0:T(8,128)(2,1)} %collective-permute-done.9.refs_0_.refs_2_,, ...), custom_call_target="tpu_custom_call" | custom-call | flops 10066329600 | bytes 18104320 | tf_op jit(solution)/shard_map/feed/pallas_call | solution.py:364
  279.8 16.5 %weight_grads.1 = bf16[960,1920]{1,0:T(8,128)(2,1)} custom-call(bf16[512,1024]{1,0:T(8,128)(2,1)} %get-tuple-element.96.refs_0_, bf16[512,1024]{1,0:T(8,128)(2,1)} %collective-permute-done.10.refs_2_.refs_1_, bf16[512,1024]{1,0:T(8,128)(2,1)} %collective-permute-done.9.refs_0_.refs_2_, bf16[512,1024]{1,0:T(8,128)(2,1)} %copy-done.33, ...), custom_call_target="tpu_custom_call" | custom-call | flops 7549747200 | bytes 19415040 | tf_op jit(solution)/shard_map/weight_grads/pallas_call | solution.py:561
  296.3 7.6 %collective-permute-done.16.refs_2_ = bf16[512,1024]{1,0:T(8,128)(2,1)} collective-permute-done((bf16[512,1024]{1,0:T(8,128)(2,1)}, bf16[512,1024]{1,0:T(8,128)(2,1)}, u32[]{:S(2)}, u32[]{:S(2)}) %collective-permute-start.16) | collective-permute-done | bytes 1048608 | tf_op jit(solution)/shard_map/ppermute | solution.py:583
  308.8 10.0 %unmix.1 = (f32[512,960]{1,0:T(8,128)}, bf16[512,960]{1,0:T(8,128)(2,1)}, bf16[5,2,3,256,128]{4,3,2,1,0:T(8,128)(2,1)}, bf16[5,2,3,256,128]{4,3,2,1,0:T(8,128)(2,1)}, f32[8,960]{1,0:T(8,128)}) custom-call(f32[512,1024]{1,0:T(8,128)} %get-tuple-element.115.refs_0_, bf16[512,1024]{1,0:T(8,128)(2,1)} %collective-permute-done.12.refs_1_, ...), custom_call_target="tpu_custom_call" | custom-call | flops 1887436800 | bytes 22660864 | tf_op jit(solution)/shard_map/unmix/pallas_call | solution.py:364
  323.7 36.9 %attention_backward.2 = (f32[5,1536,128]{2,1,0:T(8,128)}, bf16[5,4096,128]{2,1,0:T(8,128)(2,1)}) custom-call(s32[1]{0:T(128)} %bitcast.pair_ref, bf16[5,1536,128]{2,1,0:T(8,128)(2,1)S(1)} %bitcast.116, bf16[5,1536,128]{2,1,0:T(8,128)(2,1)S(1)} %bitcast.118, bf16[5,1536,128]{2,1,0:T(8,128)(2,1)S(1)} %bitcast.120, ...), custom_call_target="tpu_custom_call" | custom-call | flops 6039797760 | bytes 12189696 | tf_op jit(solution)/shard_map/attention_backward/pallas_call | solution.py:244
  362.0 4.2 block.1
  367.6 7.6 %collective-permute-start.20 = (bf16[960,256]{1,0:T(8,128)(2,1)S(1)}, bf16[960,256]{1,0:T(8,128)(2,1)S(1)}, u32[]{:S(2)}, u32[]{:S(2)}) collective-permute-start(bf16[960,256]{1,0:T(8,128)(2,1)S(1)} %get-tuple-element.218), channel_id=1, source_target_pairs={{0,12},{4,8},{8,4},{12,0},{1,13},{5,9},{9,5},{13,1},{2,14},{6,10},... | collective-permute-start | bytes 1474568 | tf_op jit(solution)/shard_map/ppermute | solution.py:588
  375.2 25.6 %attention_backward.3 = (f32[5,1536,128]{2,1,0:T(8,128)}, bf16[5,4096,128]{2,1,0:T(8,128)(2,1)}) custom-call(s32[1]{0:T(128)} %bitcast.pair_ref, bf16[5,1536,128]{2,1,0:T(8,128)(2,1)S(1)} %bitcast.117, bf16[5,1536,128]{2,1,0:T(8,128)(2,1)S(1)} %bitcast.119, bf16[5,1536,128]{2,1,0:T(8,128)(2,1)S(1)} %bitcast.121, ...), custom_call_target="tpu_custom_call", output_to_operand_aliasing={{0}: (5, {}), {1}: (6, {})} | custom-call | flops 4026531840 | bytes 8126464 | tf_op jit(solution)/shard_map/attention_backward/pallas_call | solution.py:244
  400.8 6.7 %reduce-scatter.7.cloned.1.call-done = bf16[120,1920]{1,0:T(8,128)(2,1)} async-done(((bf16[960,1920]{1,0:T(8,128)(2,1)}), bf16[120,1920]{1,0:T(8,128)(2,1)}) %reduce-scatter.7.cloned.1.call-update) | async-done | bytes 460816 | tf_op jit(solution)/shard_map/optimization_barrier | solution.py:879
  407.5 4.5 early.1
  430.1 20.8 %collective-permute-done.22 = bf16[240,1856]{1,0:T(8,128)(2,1)} collective-permute-done((bf16[240,1856]{1,0:T(8,128)(2,1)S(1)}, bf16[240,1856]{1,0:T(8,128)(2,1)}, u32[]{:S(2)}, u32[]{:S(2)}) %collective-permute-start.22) | collective-permute-done | bytes 890912 | tf_op jit(solution)/shard_map/ppermute | solution.py:583
  462.4 8.7 %collective-permute-done.29.refs_6_ = bf16[960,256]{1,0:T(8,128)(2,1)S(1)} collective-permute-done((bf16[960,256]{1,0:T(8,128)(2,1)S(1)}, bf16[960,256]{1,0:T(8,128)(2,1)S(1)}, u32[]{:S(2)}, u32[]{:S(2)}) %collective-permute-start.29) | collective-permute-done | bytes 491552 | tf_op jit(solution)/shard_map/ppermute | solution.py:583
  477.0 9.2 %finish.1 = (bf16[512,1664]{1,0:T(8,128)(2,1)}, bf16[960,512]{1,0:T(8,128)(2,1)}, f32[8,960]{1,0:T(8,128)}) custom-call(f32[5,2,3,256,128]{4,3,2,1,0:T(8,128)} %bitcast.123, bf16[5,512,128]{2,1,0:T(8,128)(2,1)} %reduce-scatter.5.cloned.1.call-done.dkv_ref, f32[512,128]{1,0:T(8,128)} %pad_maximum_fusion.2.cos_ref, f32[512,128]{1,0:T(8,128)} %pad_maximum_fusion.3.sin_ref, ...), custom_call_target="tpu_custom_call" | custom-call | flops 1635778560 | bytes 13977344 | tf_op jit(solution)/shard_map/finish/pallas_call | solution.py:364
  491.0 7.8 %reshape.135 = bf16[2,2,240,800]{2,1,0,3:T(2,128)(2,1)} reshape(bf16[960,800]{0,1:T(8,128)(2,1)} %convolution_convert_fusion.2) | data formatting | bytes 3072000 | tf_op jit(solution)/shard_map/reshape | solution.py:941
  498.8 5.3 constant_dynamic-slice_fusion.1
  534.6 9.8 %collective-permute-done.36.refs_6_ = bf16[960,256]{1,0:T(8,128)(2,1)S(1)} collective-permute-done((bf16[960,256]{1,0:T(8,128)(2,1)S(1)}, bf16[960,256]{1,0:T(8,128)(2,1)S(1)}, u32[]{:S(2)}, u32[]{:S(2)}) %collective-permute-start.36) | collective-permute-done | bytes 491552 | tf_op jit(solution)/shard_map/ppermute | solution.py:583
  546.0 6.7 %collective-permute-start.45 = (bf16[256,320]{0,1:T(8,128)(2,1)S(1)}, bf16[256,320]{0,1:T(8,128)(2,1)S(1)}, u32[]{:S(2)}, u32[]{:S(2)}) collective-permute-start(bf16[256,320]{0,1:T(8,128)(2,1)S(1)} %get-tuple-element.222), channel_id=1, source_target_pairs={{8,0},{12,4},{0,8},{4,12},{9,1},{13,5},{1,9},{5,13},{10,2},{14,6},... | collective-permute-start | bytes 491528 | tf_op jit(solution)/shard_map/ppermute | solution.py:583
  553.8 6.0 %place_rows.3 = f32[2,960,1024]{2,1,0:T(8,128)} custom-call(s32[8]{0:T(128)S(1)} %stack.48.seq_ref, s32[8]{0:T(128)S(1)} %stack.103.chunk_ref, bf16[960,256]{1,0:T(8,128)(2,1)S(1)} %get-tuple-element.162.refs_0_, bf16[960,256]{1,0:T(8,128)(2,1)S(1)} %collective-permute-done.32.refs_1_, bf16[960,256]{1,0:T(8,128)(2,1)} %collective-permute-done.33.refs_2_, ...), custom_call_target="tpu_custom_call" | custom-call | tf_op jit(solution)/shard_map/place_rows/pallas_call | solution.py:649
  559.9 8.0 %collective-permute-done.45 = bf16[256,320]{0,1:T(8,128)(2,1)S(1)} collective-permute-done((bf16[256,320]{0,1:T(8,128)(2,1)S(1)}, bf16[256,320]{0,1:T(8,128)(2,1)S(1)}, u32[]{:S(2)}, u32[]{:S(2)}) %collective-permute-start.45) | collective-permute-done | bytes 163872 | tf_op jit(solution)/shard_map/ppermute | solution.py:583
  (256 shorter events, 156.7 us)
Async XLA Ops:
  7.2 87.5 %all-gather.10.cloned.1.call-start = ((), (), s32[]{:S(2)}) async-start(), calls=%async_computation.5 | async-start | bytes 3379200 | tf_op jit(solution)/shard_map/all_gather | solution.py:726
  9.6 160.3 %all-gather.6.cloned.1.call-start = ((), (), s32[]{:S(2)}) async-start(), calls=%async_computation.2 | async-start | bytes 5898240 | tf_op jit(solution)/shard_map/all_gather | solution.py:775
  9.7 14.3 %collective-permute-start.1 = (bf16[240,120]{1,0:T(8,128)(2,1)}, bf16[240,120]{1,0:T(8,128)(2,1)S(1)}, u32[]{:S(2)}, u32[]{:S(2)}) collective-permute-start(bf16[240,120]{1,0:T(8,128)(2,1)} %param.11), channel_id=1, source_target_pairs={{4,0},{8,4},{12,8},{0,12},{5,1},{9,5},{13,9},{1,13},{6,2},{10,6},{... | collective-permute-start | bytes 172808 | tf_op jit(solution)/shard_map/ppermute | solution.py:583
  18.9 29.7 %collective-permute-start = (bf16[256,960]{1,0:T(8,128)(2,1)}, bf16[256,960]{1,0:T(8,128)(2,1)}, u32[]{:S(2)}, u32[]{:S(2)}) collective-permute-start(bf16[256,960]{1,0:T(8,128)(2,1)} %bitcast.2), channel_id=1, source_target_pairs={{0,12},{4,8},{8,4},{12,0},{1,13},{5,9},{9,5},{13,1},{2,14},{6,10},... | collective-permute-start | bytes 1474568 | tf_op jit(solution)/shard_map/ppermute | solution.py:588
  22.8 24.7 %collective-permute-start.7 = (bf16[256,960]{1,0:T(8,128)(2,1)}, bf16[256,960]{1,0:T(8,128)(2,1)}, u32[]{:S(2)}, u32[]{:S(2)}) collective-permute-start(bf16[256,960]{1,0:T(8,128)(2,1)} %bitcast.103), channel_id=1, source_target_pairs={{0,12},{4,8},{8,4},{12,0},{1,13},{5,9},{9,5},{13,1},{2,14},{6,10},... | collective-permute-start | bytes 1474568 | tf_op jit(solution)/shard_map/ppermute | solution.py:588
  114.9 122.9 %all-gather.8.cloned.1.call-start = ((), (), s32[]{:S(2)}) async-start(), calls=%async_computation.3 | async-start | bytes 4147200 | tf_op jit(solution)/shard_map/all_gather | solution.py:778
  116.2 25.6 %collective-permute-start.8 = (bf16[512,1024]{1,0:T(8,128)(2,1)}, bf16[512,1024]{1,0:T(8,128)(2,1)}, u32[]{:S(2)}, u32[]{:S(2)}) collective-permute-start(bf16[512,1024]{1,0:T(8,128)(2,1)} %pad.26.refs_1_.refs_4_), channel_id=1, source_target_pairs={{2,0},{0,2},{3,1},{1,3},{6,4},{4,6},{7,5},{5,7},{10,8},{8,10},{11,... | collective-permute-start | bytes 3145736 | tf_op jit(solution)/shard_map/ppermute | solution.py:583
  169.9 237.5 %reduce-scatter.7.cloned.1.call-start = ((), (), s32[]{:S(2)}) async-start(), calls=%async_computation.6 | async-start | bytes 4147200
  229.5 25.4 %collective-permute-start.9 = (bf16[512,1024]{1,0:T(8,128)(2,1)}, bf16[512,1024]{1,0:T(8,128)(2,1)}, u32[]{:S(2)}, u32[]{:S(2)}) collective-permute-start(bf16[512,1024]{1,0:T(8,128)(2,1)} %get-tuple-element.96.refs_0_), channel_id=1, source_target_pairs={{2,0},{0,2},{3,1},{1,3},{6,4},{4,6},{7,5},{5,7},{10,8},{8,10},{11,... | collective-permute-start | bytes 3145736 | tf_op jit(solution)/shard_map/ppermute | solution.py:583
  278.3 25.5 %collective-permute-start.16 = (bf16[512,1024]{1,0:T(8,128)(2,1)}, bf16[512,1024]{1,0:T(8,128)(2,1)}, u32[]{:S(2)}, u32[]{:S(2)}) collective-permute-start(bf16[512,1024]{1,0:T(8,128)(2,1)} %add_convert_fusion.1), channel_id=1, source_target_pairs={{2,0},{0,2},{3,1},{1,3},{6,4},{4,6},{7,5},{5,7},{10,8},{8,10},{11,... | collective-permute-start | bytes 3145736 | tf_op jit(solution)/shard_map/ppermute | solution.py:583
  303.9 173.1 %reduce-scatter.5.cloned.1.call-start = ((), (), s32[]{:S(2)}) async-start(), calls=%async_computation.4 | async-start | bytes 5898240 | tf_op jit(solution)/shard_map/reduce_scatter | solution.py:882
  304.0 56.6 %collective-permute-start.18 = (bf16[512,1024]{1,0:T(8,128)(2,1)}, bf16[512,1024]{1,0:T(8,128)(2,1)S(1)}, u32[]{:S(2)}, u32[]{:S(2)}) collective-permute-start(bf16[512,1024]{1,0:T(8,128)(2,1)} %get-tuple-element.127), channel_id=1, source_target_pairs={{1,0},{0,1},{3,2},{2,3},{5,4},{4,5},{7,6},{6,7},{9,8},{8,9},{11,10... | collective-permute-start | bytes 3145736 | tf_op jit(solution)/shard_map/ppermute | solution.py:583
  318.8 41.8 %collective-permute-start.19 = (bf16[512,1024]{1,0:T(8,128)(2,1)S(1)}, bf16[512,1024]{1,0:T(8,128)(2,1)S(1)}, u32[]{:S(2)}, u32[]{:S(2)}) collective-permute-start(bf16[512,1024]{1,0:T(8,128)(2,1)S(1)} %add_convert_fusion), channel_id=1, source_target_pairs={{2,0},{0,2},{3,1},{1,3},{6,4},{4,6},{7,5},{5,7},{10,8},{8,10},{11,... | collective-permute-start | bytes 3145736 | tf_op jit(solution)/shard_map/ppermute | solution.py:583
  367.6 33.2 %collective-permute-start.20 = (bf16[960,256]{1,0:T(8,128)(2,1)S(1)}, bf16[960,256]{1,0:T(8,128)(2,1)S(1)}, u32[]{:S(2)}, u32[]{:S(2)}) collective-permute-start(bf16[960,256]{1,0:T(8,128)(2,1)S(1)} %get-tuple-element.218), channel_id=1, source_target_pairs={{0,12},{4,8},{8,4},{12,0},{1,13},{5,9},{9,5},{13,1},{2,14},{6,10},... | collective-permute-start | bytes 1474568 | tf_op jit(solution)/shard_map/ppermute | solution.py:588
  427.4 23.5 %collective-permute-start.22 = (bf16[240,1856]{1,0:T(8,128)(2,1)S(1)}, bf16[240,1856]{1,0:T(8,128)(2,1)}, u32[]{:S(2)}, u32[]{:S(2)}) collective-permute-start(bf16[240,1856]{1,0:T(8,128)(2,1)S(1)} %dynamic-slice_bitcast_fusion.1), channel_id=1, source_target_pairs={{2,0},{0,2},{3,1},{1,3},{6,4},{4,6},{7,5},{5,7},{10,8},{8,10},{11,... | collective-permute-start | bytes 2672648 | tf_op jit(solution)/shard_map/ppermute | solution.py:583
  428.0 33.8 %collective-permute-start.26 = (bf16[960,256]{1,0:T(8,128)(2,1)S(1)}, bf16[960,256]{1,0:T(8,128)(2,1)S(1)}, u32[]{:S(2)}, u32[]{:S(2)}) collective-permute-start(bf16[960,256]{1,0:T(8,128)(2,1)S(1)} %get-tuple-element.153.refs_0_), channel_id=1, source_target_pairs={{2,0},{0,2},{3,1},{1,3},{6,4},{4,6},{7,5},{5,7},{10,8},{8,10},{11,... | collective-permute-start | bytes 1474568 | tf_op jit(solution)/shard_map/ppermute | solution.py:583
  429.5 41.5 %collective-permute-start.29 = (bf16[960,256]{1,0:T(8,128)(2,1)S(1)}, bf16[960,256]{1,0:T(8,128)(2,1)S(1)}, u32[]{:S(2)}, u32[]{:S(2)}) collective-permute-start(bf16[960,256]{1,0:T(8,128)(2,1)S(1)} %collective-permute-done.20.refs_4_), channel_id=1, source_target_pairs={{2,0},{0,2},{3,1},{1,3},{6,4},{4,6},{7,5},{5,7},{10,8},{8,10},{11,... | collective-permute-start | bytes 1474568 | tf_op jit(solution)/shard_map/ppermute | solution.py:583
  456.1 14.9 %collective-permute-start.23 = (bf16[4,240,120]{1,2,0:T(8,128)(2,1)}, bf16[4,240,120]{1,2,0:T(8,128)(2,1)}, u32[]{:S(2)}, u32[]{:S(2)}) collective-permute-start(bf16[4,240,120]{1,2,0:T(8,128)(2,1)} %dynamic-slice_bitcast_fusion.3), channel_id=1, source_target_pairs={{16,0},{0,16},{17,1},{1,17},{18,2},{2,18},{19,3},{3,19},{20,4},{4,... | collective-permute-start | bytes 691208 | tf_op jit(solution)/shard_map/ppermute | solution.py:583
  460.5 12.9 %collective-permute-start.24 = (bf16[4,240,200]{1,2,0:T(8,128)(2,1)}, bf16[4,240,200]{1,2,0:T(8,128)(2,1)}, u32[]{:S(2)}, u32[]{:S(2)}) collective-permute-start(bf16[4,240,200]{1,2,0:T(8,128)(2,1)} %bitcast.34), channel_id=1, source_target_pairs={{16,0},{17,1},{18,2},{19,3},{20,4},{21,5},{22,6},{23,7},{24,8},{25... | collective-permute-start | bytes 1152008 | tf_op jit(solution)/shard_map/ppermute | solution.py:633
  461.8 13.6 %collective-permute-start.25 = (bf16[960,256]{1,0:T(8,128)(2,1)S(1)}, bf16[960,256]{1,0:T(8,128)(2,1)S(1)}, u32[]{:S(2)}, u32[]{:S(2)}) collective-permute-start(bf16[960,256]{1,0:T(8,128)(2,1)S(1)} %get-tuple-element.153.refs_0_), channel_id=1, source_target_pairs={{1,0},{0,1},{3,2},{2,3},{5,4},{4,5},{7,6},{6,7},{9,8},{8,9},{11,10... | collective-permute-start | bytes 1474568 | tf_op jit(solution)/shard_map/ppermute | solution.py:583
  461.9 13.5 %collective-permute-start.28 = (bf16[960,256]{1,0:T(8,128)(2,1)S(1)}, bf16[960,256]{1,0:T(8,128)(2,1)S(1)}, u32[]{:S(2)}, u32[]{:S(2)}) collective-permute-start(bf16[960,256]{1,0:T(8,128)(2,1)S(1)} %collective-permute-done.20.refs_4_), channel_id=1, source_target_pairs={{1,0},{0,1},{3,2},{2,3},{5,4},{4,5},{7,6},{6,7},{9,8},{8,9},{11,10... | collective-permute-start | bytes 1474568 | tf_op jit(solution)/shard_map/ppermute | solution.py:583
  505.1 20.8 %collective-permute-start.31 = (bf16[960,256]{1,0:T(8,128)(2,1)}, bf16[960,256]{1,0:T(8,128)(2,1)S(1)}, u32[]{:S(2)}, u32[]{:S(2)}) collective-permute-start(bf16[960,256]{1,0:T(8,128)(2,1)} %get-tuple-element.152), channel_id=1, source_target_pairs={{0,12},{4,8},{8,4},{12,0},{1,13},{5,9},{9,5},{13,1},{2,14},{6,10},... | collective-permute-start | bytes 1474568 | tf_op jit(solution)/shard_map/ppermute | solution.py:588
  510.8 16.0 %collective-permute-start.42 = (bf16[240,800]{0,1:T(8,128)(2,1)}, bf16[240,800]{0,1:T(8,128)(2,1)}, u32[]{:S(2)}, u32[]{:S(2)}) collective-permute-start(bf16[240,800]{0,1:T(8,128)(2,1)} %dynamic-slice_bitcast_fusion.2), channel_id=1, source_target_pairs={{2,0},{0,2},{3,1},{1,3},{6,4},{4,6},{7,5},{5,7},{10,8},{8,10},{11,... | collective-permute-start | bytes 1152008 | tf_op jit(solution)/shard_map/ppermute | solution.py:583
  513.0 21.5 %collective-permute-start.33 = (bf16[960,256]{1,0:T(8,128)(2,1)S(1)}, bf16[960,256]{1,0:T(8,128)(2,1)}, u32[]{:S(2)}, u32[]{:S(2)}) collective-permute-start(bf16[960,256]{1,0:T(8,128)(2,1)S(1)} %get-tuple-element.162.refs_0_), channel_id=1, source_target_pairs={{2,0},{0,2},{3,1},{1,3},{6,4},{4,6},{7,5},{5,7},{10,8},{8,10},{11,... | collective-permute-start | bytes 1474568 | tf_op jit(solution)/shard_map/ppermute | solution.py:583
  525.9 18.5 %collective-permute-start.36 = (bf16[960,256]{1,0:T(8,128)(2,1)S(1)}, bf16[960,256]{1,0:T(8,128)(2,1)S(1)}, u32[]{:S(2)}, u32[]{:S(2)}) collective-permute-start(bf16[960,256]{1,0:T(8,128)(2,1)S(1)} %collective-permute-done.31.refs_4_), channel_id=1, source_target_pairs={{2,0},{0,2},{3,1},{1,3},{6,4},{4,6},{7,5},{5,7},{10,8},{8,10},{11,... | collective-permute-start | bytes 1474568 | tf_op jit(solution)/shard_map/ppermute | solution.py:583
  528.0 16.4 %collective-permute-start.43 = (bf16[4,240,200]{1,2,0:T(8,128)(2,1)S(1)}, bf16[4,240,200]{1,2,0:T(8,128)(2,1)S(1)}, u32[]{:S(2)}, u32[]{:S(2)}) collective-permute-start(bf16[4,240,200]{1,2,0:T(8,128)(2,1)S(1)} %bitcast.135), channel_id=1, source_target_pairs={{0,16},{1,17},{2,18},{3,19},{4,20},{5,21},{6,22},{7,23},{8,24},{9,... | collective-permute-start | bytes 1152008 | tf_op jit(solution)/shard_map/ppermute | solution.py:633
  531.2 14.8 %collective-permute-start.32 = (bf16[960,256]{1,0:T(8,128)(2,1)S(1)}, bf16[960,256]{1,0:T(8,128)(2,1)S(1)}, u32[]{:S(2)}, u32[]{:S(2)}) collective-permute-start(bf16[960,256]{1,0:T(8,128)(2,1)S(1)} %get-tuple-element.162.refs_0_), channel_id=1, source_target_pairs={{1,0},{0,1},{3,2},{2,3},{5,4},{4,5},{7,6},{6,7},{9,8},{8,9},{11,10... | collective-permute-start | bytes 1474568 | tf_op jit(solution)/shard_map/ppermute | solution.py:583
  531.3 22.5 %collective-permute-start.35 = (bf16[960,256]{1,0:T(8,128)(2,1)S(1)}, bf16[960,256]{1,0:T(8,128)(2,1)S(1)}, u32[]{:S(2)}, u32[]{:S(2)}) collective-permute-start(bf16[960,256]{1,0:T(8,128)(2,1)S(1)} %collective-permute-done.31.refs_4_), channel_id=1, source_target_pairs={{1,0},{0,1},{3,2},{2,3},{5,4},{4,5},{7,6},{6,7},{9,8},{8,9},{11,10... | collective-permute-start | bytes 1474568 | tf_op jit(solution)/shard_map/ppermute | solution.py:583
  534.6 18.1 %collective-permute-start.34 = (bf16[960,256]{1,0:T(8,128)(2,1)}, bf16[960,256]{1,0:T(8,128)(2,1)S(1)}, u32[]{:S(2)}, u32[]{:S(2)}) collective-permute-start(bf16[960,256]{1,0:T(8,128)(2,1)} %collective-permute-done.33.refs_2_), channel_id=1, source_target_pairs={{1,0},{0,1},{3,2},{2,3},{5,4},{4,5},{7,6},{6,7},{9,8},{8,9},{11,10... | collective-permute-start | bytes 1474568 | tf_op jit(solution)/shard_map/ppermute | solution.py:583
  544.8 15.0 %collective-permute-start.46 = (bf16[256,320]{0,1:T(8,128)(2,1)S(1)}, bf16[256,320]{0,1:T(8,128)(2,1)S(1)}, u32[]{:S(2)}, u32[]{:S(2)}) collective-permute-start(bf16[256,320]{0,1:T(8,128)(2,1)S(1)} %get-tuple-element.221), channel_id=1, source_target_pairs={{4,0},{8,4},{12,8},{0,12},{5,1},{9,5},{13,9},{1,13},{6,2},{10,6},{... | collective-permute-start | bytes 491528 | tf_op jit(solution)/shard_map/ppermute | solution.py:583
  546.0 21.9 %collective-permute-start.45 = (bf16[256,320]{0,1:T(8,128)(2,1)S(1)}, bf16[256,320]{0,1:T(8,128)(2,1)S(1)}, u32[]{:S(2)}, u32[]{:S(2)}) collective-permute-start(bf16[256,320]{0,1:T(8,128)(2,1)S(1)} %get-tuple-element.222), channel_id=1, source_target_pairs={{8,0},{12,4},{0,8},{4,12},{9,1},{13,5},{1,9},{5,13},{10,2},{14,6},... | collective-permute-start | bytes 491528 | tf_op jit(solution)/shard_map/ppermute | solution.py:583
  552.7 15.1 %collective-permute-start.44 = (bf16[256,320]{0,1:T(8,128)(2,1)S(1)}, bf16[256,320]{0,1:T(8,128)(2,1)S(1)}, u32[]{:S(2)}, u32[]{:S(2)}) collective-permute-start(bf16[256,320]{0,1:T(8,128)(2,1)S(1)} %get-tuple-element.220), channel_id=1, source_target_pairs={{12,0},{0,4},{4,8},{8,12},{13,1},{1,5},{5,9},{9,13},{14,2},{2,6},{... | collective-permute-start | bytes 491528 | tf_op jit(solution)/shard_map/ppermute | solution.py:583
  (56 other events, 384.4 us)
Sparse Core Ops, SparseCore 0:
  11.4 83.1 all-gather.9
  115.0 54.8 all-gather.5
  172.0 65.7 all-gather.7
  304.0 103.3 reduce-scatter.6
  410.2 62.2 reduce-scatter.4
